TPU v7x, 32 devices: a whole 2x2x4 slice. The times are simulated.
32 devices in a mesh: section: 4 (over y, x), dp: 2 (over core), expert: 4 (over z).
Axes of the slice: x: 2, y: 2, z: 4, core: 2. Of those that a mesh axis runs over, the one named last changes fastest.
Arguments:
- tokens: bfloat16 [4, 1024, 2048], P('section', ('dp', 'expert')), may hold values from -6 to 6
- out_grad: bfloat16 [4, 1024, 2048], P('section', ('dp', 'expert')), may hold values from -6 to 6
- expert_ids: int32 [4, 1024, 2], P('section', ('dp', 'expert')), may hold values from 0 to 3, all different within a row; in each aligned block of 128 rows (0 to 127, 128 to 255, ..., all dimensions but the last counted through in order) at most 128 rows name the same one
- route_probs: float32 [4, 1024, 2], P('section', ('dp', 'expert')), may hold values from 0.1 to 1
- gate_weight: bfloat16 [4, 4, 2048, 768], P('section', 'expert', None, 'dp'), may hold values from -0.125 to 0.125
- up_weight: bfloat16 [4, 4, 2048, 768], P('section', 'expert', None, 'dp'), may hold values from -0.125 to 0.125
- down_weight: bfloat16 [4, 4, 768, 2048], P('section', 'expert', 'dp'), may hold values from -0.21875 to 0.21875
Outputs:
- grad_in: bfloat16 [4, 1024, 2048], P('section', ('dp', 'expert'))
- prob_grad: float32 [4, 1024, 2], P('section', ('dp', 'expert'))
- gate_weight_grad: bfloat16 [4, 4, 2048, 768], P('section', 'expert', None, 'dp')
- up_weight_grad: bfloat16 [4, 4, 2048, 768], P('section', 'expert', None, 'dp')
- down_weight_grad: bfloat16 [4, 4, 768, 2048], P('section', 'expert', 'dp')
Inputs may be any that keep to these rules, and one draw needn't show every extreme that they name: `expert_ids`: each token names 2 different experts; among the 128 tokens of one device (aligned blocks of 128 tokens of a section) no expert is named more than 128 times, a bound that some block reaches.
All inputs are finite; a program needn't handle non-finite values.
Results may differ from a plain program's by a relative error of at most 0.023.
Values may be sent and summed in bfloat16 or wider, within the bound.
No kernel may reach another device: no remote copies, remote signals or barrier semaphores. Data moves between devices by JAX's collectives and lax.ppermute only.
A program may use at most 128 MiB of HBM per device.

v0:
```python
import jax
import jax.numpy as jnp
from jax import lax
from jax.sharding import PartitionSpec as P


def from_behind(shard, axis, by):
    length = lax.axis_size(axis)
    return lax.ppermute(shard, axis, [(i, (i + by) % length) for i in range(length)])


def expert_grads(rows_in, grads_in, weights_in, gate_part, up_part, down_part):
    contract_last = (((1,), (1,)), ((), ()))
    contract_first = (((0,), (0,)), ((), ()))
    gate_pre = jnp.dot(rows_in, gate_part, preferred_element_type=jnp.float32)
    up_pre = jnp.dot(rows_in, up_part, preferred_element_type=jnp.float32)
    sigmoid_gate = jax.nn.sigmoid(gate_pre)
    activated = gate_pre * sigmoid_gate * up_pre
    scaled_act = (weights_in[:, None] * activated).astype(jnp.bfloat16)
    hidden_grad = lax.dot_general(
        grads_in, down_part, contract_last, preferred_element_type=jnp.float32
    )
    prob_part = jnp.sum(activated * hidden_grad, axis=1)
    hidden_scaled = weights_in[:, None] * hidden_grad
    gate_grad = (
        hidden_scaled * up_pre * sigmoid_gate * (1.0 + gate_pre * (1.0 - sigmoid_gate))
    ).astype(jnp.bfloat16)
    up_grad = (hidden_scaled * gate_pre * sigmoid_gate).astype(jnp.bfloat16)
    route_dx = lax.dot_general(
        gate_grad, gate_part, contract_last, preferred_element_type=jnp.float32
    ) + lax.dot_general(up_grad, up_part, contract_last, preferred_element_type=jnp.float32)
    grad_gate = lax.dot_general(
        rows_in, gate_grad, contract_first, preferred_element_type=jnp.float32
    )
    grad_up = lax.dot_general(rows_in, up_grad, contract_first, preferred_element_type=jnp.float32)
    grad_down = lax.dot_general(
        scaled_act, grads_in, contract_first, preferred_element_type=jnp.float32
    )
    return (route_dx, prob_part, grad_gate, grad_up, grad_down)


def per_device(tokens, out_grad, expert_ids, route_probs, gate_weight, up_weight, down_weight):
    local_tokens = tokens[0]
    local_grads = out_grad[0]
    tok_count, row_width = local_tokens.shape
    top_count = expert_ids.shape[2]
    groups = lax.axis_size("expert")
    capacity = 2 * tok_count * top_count // groups
    slots_all = groups * capacity
    route_ids = expert_ids[0].reshape(-1)
    hit_table = (route_ids[:, None] == jnp.arange(groups, dtype=jnp.int32)[None, :]).astype(
        jnp.int32
    )
    before = jnp.cumsum(hit_table, axis=0) - hit_table
    slot_rank = jnp.sum(before * hit_table, axis=1)
    slot_of = route_ids * capacity + slot_rank
    placed = slot_of[None, :] == jnp.arange(slots_all, dtype=jnp.int32)[:, None]
    per_token = jnp.any(placed.reshape(slots_all, tok_count, top_count), axis=2).astype(
        jnp.bfloat16
    )
    send_rows = jnp.dot(per_token, local_tokens, preferred_element_type=jnp.float32).astype(
        jnp.bfloat16
    )
    send_grads = jnp.dot(per_token, local_grads, preferred_element_type=jnp.float32).astype(
        jnp.bfloat16
    )
    probs_flat = route_probs[0].reshape(-1)
    send_probs = jnp.sum(jnp.where(placed, probs_flat[None, :], 0.0), axis=1)
    recv_rows, recv_grads, recv_probs = (
        lax.all_to_all(
            send_rows.reshape(groups, capacity, row_width),
            "expert",
            split_axis=0,
            concat_axis=0,
            tiled=True,
        ),
        lax.all_to_all(
            send_grads.reshape(groups, capacity, row_width),
            "expert",
            split_axis=0,
            concat_axis=0,
            tiled=True,
        ),
        lax.all_to_all(
            send_probs.reshape(groups, capacity).astype(jnp.bfloat16),
            "expert",
            split_axis=0,
            concat_axis=0,
            tiled=True,
        ).astype(jnp.float32),
    )
    recv_rows = recv_rows.reshape(slots_all, row_width)
    recv_grads = recv_grads.reshape(slots_all, row_width)
    recv_probs = recv_probs.reshape(slots_all)
    gate_part = gate_weight[0, 0]
    up_part = up_weight[0, 0]
    down_part = down_weight[0, 0]
    gate_full, up_full, down_full = (
        lax.all_gather(gate_part, "dp", axis=1, tiled=True),
        lax.all_gather(up_part, "dp", axis=1, tiled=True),
        lax.all_gather(down_part, "dp", axis=0, tiled=True),
    )
    route_dx, prob_part, grad_gate, grad_up, grad_down = expert_grads(
        recv_rows, recv_grads, recv_probs, gate_full, up_full, down_full
    )
    grad_gate, grad_up, grad_down = (
        lax.psum_scatter(
            grad_gate.astype(jnp.bfloat16), "dp", scatter_dimension=1, tiled=True
        ).astype(jnp.float32),
        lax.psum_scatter(
            grad_up.astype(jnp.bfloat16), "dp", scatter_dimension=1, tiled=True
        ).astype(jnp.float32),
        lax.psum_scatter(
            grad_down.astype(jnp.bfloat16), "dp", scatter_dimension=0, tiled=True
        ).astype(jnp.float32),
    )
    back_rows, back_probs = (
        lax.all_to_all(
            route_dx.astype(jnp.bfloat16).reshape(groups, capacity, row_width),
            "expert",
            split_axis=0,
            concat_axis=0,
            tiled=True,
        ),
        lax.all_to_all(
            prob_part.reshape(groups, capacity).astype(jnp.bfloat16),
            "expert",
            split_axis=0,
            concat_axis=0,
            tiled=True,
        ).astype(jnp.float32),
    )
    token_grad = lax.dot_general(
        per_token,
        back_rows.reshape(slots_all, row_width),
        (((0,), (0,)), ((), ())),
        preferred_element_type=jnp.float32,
    ).astype(jnp.bfloat16)
    route_grad = jnp.sum(jnp.where(placed, back_probs.reshape(slots_all)[:, None], 0.0), axis=0)
    route_grad = route_grad.reshape(tok_count, top_count)
    upstream = from_behind(token_grad, "section", -1)
    return (
        upstream[None],
        route_grad[None],
        grad_gate.astype(jnp.bfloat16)[None, None],
        grad_up.astype(jnp.bfloat16)[None, None],
        grad_down.astype(jnp.bfloat16)[None, None],
    )


def solution(mesh):
    in_specs = (
        P("section", ("dp", "expert"), None),
        P("section", ("dp", "expert"), None),
        P("section", ("dp", "expert"), None),
        P("section", ("dp", "expert"), None),
        P("section", "expert", None, "dp"),
        P("section", "expert", None, "dp"),
        P("section", "expert", "dp", None),
    )
    out_specs = (
        P("section", ("dp", "expert"), None),
        P("section", ("dp", "expert"), None),
        P("section", "expert", None, "dp"),
        P("section", "expert", None, "dp"),
        P("section", "expert", "dp", None),
    )
    return jax.shard_map(
        per_device, mesh=mesh, in_specs=in_specs, out_specs=out_specs, check_vma=False
    )
```

profile of v0, /device:TPU:0, one launch (start us, length us, event | category | flops | bytes accessed | tf_op | source)
XLA Modules:
  0.0 251.7 jit_solution(11462658683042655586)
XLA Ops:
  7.2 0.7 all-gather.11.cloned.1.call-update
  7.9 0.8 copy.31
  8.7 0.1 eq.49
  8.8 0.1 eq.45
  9.0 1.2 reduce-window.6
  10.3 0.1 copy.34
  10.4 0.1 copy.35
  10.6 0.1 reduce_sum.39
  10.9 0.1 fusion.15
  11.0 2.0 convolution_convert_fusion.3
  13.0 6.5 %all-to-all-start.2 = ((bf16[4,128,2048]{2,1,0:T(8,128)(2,1)}), bf16[4,128,2048]{2,1,0:T(8,128)(2,1)S(1)}, u32[]{:S(2)}, u32[]{:S(2)}) async-start(bf16[4,128,2048]{2,1,0:T(8,128)(2,1)} %bitcast.10), calls=%async_computation.2 | async-start | bytes 4194304 | tf_op jit(solution)/shard_map/all_to_all | solution.py:70
  19.5 0.7 all-gather.9.cloned.1.call-update
  20.2 2.0 convolution_convert_fusion.4
  22.2 45.4 %all-to-all-done.2 = bf16[4,128,2048]{2,1,0:T(8,128)(2,1)S(1)} async-done(((bf16[4,128,2048]{2,1,0:T(8,128)(2,1)}), bf16[4,128,2048]{2,1,0:T(8,128)(2,1)S(1)}, u32[]{:S(2)}, u32[]{:S(2)}) %all-to-all-start.2) | async-done | bytes 2097184 | tf_op jit(solution)/shard_map/all_to_all | solution.py:70
  67.7 4.4 %all-to-all-start.1 = ((bf16[4,128,2048]{2,1,0:T(8,128)(2,1)}), bf16[4,128,2048]{2,1,0:T(8,128)(2,1)}, u32[]{:S(2)}, u32[]{:S(2)}) async-start(bf16[4,128,2048]{2,1,0:T(8,128)(2,1)} %bitcast.6), calls=%async_computation.1 | async-start | bytes 4194304 | tf_op jit(solution)/shard_map/all_to_all | solution.py:77
  72.2 0.7 all-gather.7.cloned.1.call-update
  72.9 4.8 %fusion.2 = f32[512,768]{1,0:T(8,128)} fusion(bf16[512,2048]{1,0:T(8,128)(2,1)S(1)} %bitcast.83, bf16[1,1,2048,768]{3,2,1,0:T(8,128)(2,1)} %all-gather.11.cloned.1.call-done), kind=kOutput, calls=%fused_computation.6 | convolution fusion | flops 1610612736 | bytes 6815744 | tf_op jit(solution)/shard_map/dot_general | solution.py:15
  77.7 4.8 %fusion.6 = f32[512,768]{1,0:T(8,128)} fusion(bf16[512,2048]{1,0:T(8,128)(2,1)S(1)} %bitcast.84, bf16[1,1,2048,768]{3,2,1,0:T(8,128)(2,1)} %all-gather.9.cloned.1.call-done), kind=kOutput, calls=%fused_computation.10 | convolution fusion | flops 1610612736 | bytes 6815744 | tf_op jit(solution)/shard_map/dot_general | solution.py:16
  82.5 37.3 %all-to-all-done.1 = bf16[4,128,2048]{2,1,0:T(8,128)(2,1)} async-done(((bf16[4,128,2048]{2,1,0:T(8,128)(2,1)}), bf16[4,128,2048]{2,1,0:T(8,128)(2,1)}, u32[]{:S(2)}, u32[]{:S(2)}) %all-to-all-start.1) | async-done | bytes 2097184 | tf_op jit(solution)/shard_map/all_to_all | solution.py:77
  119.9 6.5 %multiply_reduce_fusion = (bf16[512]{0:T(512)(128)(2,1)S(1)}, f32[512,768]{1,0:T(8,128)}) fusion(f32[512,768]{1,0:T(8,128)} %fusion.6, f32[512,768]{1,0:T(8,128)} %fusion.2, bf16[512,2048]{1,0:T(8,128)(2,1)} %bitcast.7, bf16[1,1,768,2048]{3,2,1,0:T(8,128)(2,1)} %all-gather.7.cloned.1.call-done), kind=kOutput, calls=%fused_computation.18 | convolution fusion | flops 1613364736 | bytes 9962496 | tf_op jit(solution)/shard_map/dot_general | solution.py:20
  126.3 0.6 copy.39
  126.9 3.2 %all-to-all-start.4 = ((bf16[4,1,128]{2,1,0:T(2,128)(2,1)}), bf16[4,1,128]{2,1,0:T(2,128)(2,1)S(1)}, u32[]{:S(2)}, u32[]{:S(2)}) async-start(bf16[4,1,128]{2,1,0:T(2,128)(2,1)} %copy.39), calls=%async_computation.4 | async-start | bytes 4096 | tf_op jit(solution)/shard_map/all_to_all | solution.py:125
  130.2 0.1 copy.37
  130.3 0.1 broadcast_in_dim.39
  130.5 5.1 %all-to-all-done.4 = bf16[4,1,128]{2,1,0:T(2,128)(2,1)S(1)} async-done(((bf16[4,1,128]{2,1,0:T(2,128)(2,1)}), bf16[4,1,128]{2,1,0:T(2,128)(2,1)S(1)}, u32[]{:S(2)}, u32[]{:S(2)}) %all-to-all-start.4) | async-done | bytes 1056 | tf_op jit(solution)/shard_map/all_to_all | solution.py:125
  135.6 0.3 select_reduce_fusion
  135.8 7.9 %all_to_all.27 = bf16[4,1,128]{2,1,0:T(2,128)(2,1)S(1)} all-to-all(bf16[4,1,128]{2,1,0:T(2,128)(2,1)S(1)} %copy.38), channel_id=1, replica_groups=mesh['section'=4,'dp'=2,'expert'=4] {'expert'}, dimensions={0} | all-to-all | bytes 2048 | tf_op jit(solution)/shard_map/all_to_all | solution.py:84
  143.7 3.1 %multiply_convert_fusion.1 = (bf16[512,768]{1,0:T(8,128)(2,1)S(1)}, bf16[512,768]{1,0:T(8,128)(2,1)S(1)}) fusion(f32[512,768]{1,0:T(8,128)} %fusion.2, f32[512,768]{1,0:T(8,128)} %get-tuple-element.25, f32[512]{0:T(512)S(1)} %bitcast.93, f32[512,768]{1,0:T(8,128)} %fusion.6), kind=kLoop, calls=%fused_computation.20 | loop fusion | flops 5505024 | bytes 6293504 | tf_op jit(solution)/shard_map/convert_element_type | solution.py:28
  146.9 0.9 copy-done.2
  147.7 3.5 %convolution_convert_fusion.2 = bf16[2048,768]{1,0:T(8,128)(2,1)} fusion(bf16[512,2048]{1,0:T(8,128)(2,1)S(1)} %bitcast.85, bf16[512,768]{1,0:T(8,128)(2,1)S(1)} %get-tuple-element.23), kind=kOutput, calls=%fused_computation.3 | convolution fusion | flops 1612185600 | bytes 6029312 | tf_op jit(solution)/shard_map/dot_general | solution.py:32
  151.2 4.7 %copy.41 = bf16[2048,768]{0,1:T(8,128)(2,1)} copy(bf16[2048,768]{1,0:T(8,128)(2,1)} %convolution_convert_fusion.2) | data formatting | bytes 6291456
  156.0 0.2 reduce-scatter.12.cloned.1.call-start
  156.2 3.5 %convolution_convert_fusion.1 = bf16[2048,768]{1,0:T(8,128)(2,1)} fusion(bf16[512,2048]{1,0:T(8,128)(2,1)S(1)} %bitcast.86, bf16[512,768]{1,0:T(8,128)(2,1)S(1)} %get-tuple-element.22), kind=kOutput, calls=%fused_computation.2 | convolution fusion | flops 1612185600 | bytes 6029312 | tf_op jit(solution)/shard_map/dot_general | solution.py:35
  159.7 5.0 %copy.43 = bf16[2048,768]{0,1:T(8,128)(2,1)} copy(bf16[2048,768]{1,0:T(8,128)(2,1)} %convolution_convert_fusion.1) | data formatting | bytes 6291456
  164.7 1.4 copy-done.1
  166.1 5.7 %convolution_convert_fusion = bf16[768,2048]{1,0:T(8,128)(2,1)} fusion(bf16[512,2048]{1,0:T(8,128)(2,1)} %bitcast.7, f32[512]{0:T(512)S(1)} %bitcast.94, f32[512,768]{1,0:T(8,128)} %fusion.6, f32[512,768]{1,0:T(8,128)S(1)} %copy-done.1), kind=kOutput, calls=%fused_computation.1 | convolution fusion | flops 1614938112 | bytes 8390656 | tf_op jit(solution)/shard_map/dot_general | solution.py:36
  171.8 1.1 copy-done.3
  172.9 4.3 %fusion = f32[512,2048]{1,0:T(8,128)S(1)} fusion(bf16[512,768]{1,0:T(8,128)(2,1)S(1)} %copy-done.3, bf16[1,1,2048,768]{3,2,1,0:T(8,128)(2,1)} %all-gather.11.cloned.1.call-done), kind=kOutput, calls=%fused_computation.4 | convolution fusion | flops 1610612736 | bytes 8126464 | tf_op jit(solution)/shard_map/dot_general | solution.py:29
  177.3 1.9 add_convert_fusion
  179.1 47.4 %all_to_all.28 = bf16[4,128,2048]{2,1,0:T(8,128)(2,1)S(1)} all-to-all(bf16[4,128,2048]{2,1,0:T(8,128)(2,1)S(1)} %bitcast.87), channel_id=1, replica_groups=mesh['section'=4,'dp'=2,'expert'=4] {'expert'}, dimensions={0} | all-to-all | bytes 4194304 | tf_op jit(solution)/shard_map/all_to_all | solution.py:118
  226.5 0.5 convolution_convert_fusion.5
  227.0 2.6 %collective-permute-start = (bf16[128,2048]{1,0:T(8,128)(2,1)S(1)}, bf16[128,2048]{1,0:T(8,128)(2,1)S(1)}, u32[]{:S(2)}, u32[]{:S(2)}) collective-permute-start(bf16[128,2048]{1,0:T(8,128)(2,1)S(1)} %convolution_convert_fusion.5), channel_id=1, source_target_pairs={{0,24},{8,0},{16,8},{24,16},{1,25},{9,1},{17,9},{25,17},{2,26},{10... | collective-permute-start | bytes 1572872 | tf_op jit(solution)/shard_map/ppermute | solution.py:9
  229.6 0.1 broadcast_in_dim_reshape.2
  229.7 0.6 copy.40
  230.4 8.5 %collective-permute-done = bf16[128,2048]{1,0:T(8,128)(2,1)S(1)} collective-permute-done((bf16[128,2048]{1,0:T(8,128)(2,1)S(1)}, bf16[128,2048]{1,0:T(8,128)(2,1)S(1)}, u32[]{:S(2)}, u32[]{:S(2)}) %collective-permute-start) | collective-permute-done | bytes 524320 | tf_op jit(solution)/shard_map/ppermute | solution.py:9
  238.9 2.6 %copy.42 = bf16[2048,384]{1,0:T(8,128)(2,1)} copy(bf16[2048,384]{0,1:T(8,128)(2,1)} %bitcast.88) | data formatting | bytes 3145728
  241.4 2.6 %copy.44 = bf16[2048,384]{1,0:T(8,128)(2,1)} copy(bf16[2048,384]{0,1:T(8,128)(2,1)} %bitcast.89) | data formatting | bytes 3145728
  244.0 0.8 copy.48
  (37 shorter events, 0.6 us)
Async XLA Ops:
  7.2 3.8 %copy-start = (bf16[1,128,2048]{2,1,0:T(8,128)(2,1)S(1)}, bf16[1,128,2048]{2,1,0:T(8,128)(2,1)}, u32[]{:S(2)}) copy-start(bf16[1,128,2048]{2,1,0:T(8,128)(2,1)} %param.7) | copy-start | bytes 1572868
  7.2 65.7 %all-gather.11.cloned.1.call-start = ((), (), s32[]{:S(2)}) async-start(), calls=%async_computation.11 | async-start | bytes 4718592 | tf_op jit(solution)/shard_map/all_gather | solution.py:99
  13.0 7.2 %copy-start.4 = (bf16[1,128,2048]{2,1,0:T(8,128)(2,1)S(1)}, bf16[1,128,2048]{2,1,0:T(8,128)(2,1)}, u32[]{:S(2)}) copy-start(bf16[1,128,2048]{2,1,0:T(8,128)(2,1)} %param.8) | copy-start | bytes 1572868
  13.0 54.6 %all-to-all-start.2 = ((bf16[4,128,2048]{2,1,0:T(8,128)(2,1)}), bf16[4,128,2048]{2,1,0:T(8,128)(2,1)S(1)}, u32[]{:S(2)}, u32[]{:S(2)}) async-start(bf16[4,128,2048]{2,1,0:T(8,128)(2,1)} %bitcast.10), calls=%async_computation.2 | async-start | bytes 4194304 | tf_op jit(solution)/shard_map/all_to_all | solution.py:70
  19.5 58.2 %all-gather.9.cloned.1.call-start = ((), (), s32[]{:S(2)}) async-start(), calls=%async_computation.10 | async-start | bytes 4718592 | tf_op jit(solution)/shard_map/all_gather | solution.py:100
  67.7 52.2 %all-to-all-start.1 = ((bf16[4,128,2048]{2,1,0:T(8,128)(2,1)}), bf16[4,128,2048]{2,1,0:T(8,128)(2,1)}, u32[]{:S(2)}, u32[]{:S(2)}) async-start(bf16[4,128,2048]{2,1,0:T(8,128)(2,1)} %bitcast.6), calls=%async_computation.1 | async-start | bytes 4194304 | tf_op jit(solution)/shard_map/all_to_all | solution.py:77
  72.1 47.8 %all-gather.7.cloned.1.call-start = ((), (), s32[]{:S(2)}) async-start(), calls=%async_computation.9 | async-start | bytes 4718592 | tf_op jit(solution)/shard_map/all_gather | solution.py:101
  119.9 10.3 %copy-start.5 = (f32[1,128,2]{1,2,0:T(2,128)S(1)}, f32[1,128,2]{1,2,0:T(2,128)}, u32[]{:S(2)}) copy-start(f32[1,128,2]{1,2,0:T(2,128)} %param.10) | copy-start | bytes 3076
  126.9 8.7 %all-to-all-start.4 = ((bf16[4,1,128]{2,1,0:T(2,128)(2,1)}), bf16[4,1,128]{2,1,0:T(2,128)(2,1)S(1)}, u32[]{:S(2)}, u32[]{:S(2)}) async-start(bf16[4,1,128]{2,1,0:T(2,128)(2,1)} %copy.39), calls=%async_computation.4 | async-start | bytes 4096 | tf_op jit(solution)/shard_map/all_to_all | solution.py:125
  130.1 108.7 %reduce-scatter.10.cloned.1.call-start = ((), (), s32[]{:S(2)}) async-start(), calls=%async_computation.12 | async-start | bytes 4718592
  146.8 0.9 copy-start.2
  156.0 85.5 %reduce-scatter.12.cloned.1.call-start = ((), (), s32[]{:S(2)}) async-start(), calls=%async_computation.13 | async-start | bytes 4718592
  164.6 1.5 copy-start.1
  164.7 79.4 %reduce-scatter.8.cloned.1.call-start = ((), (), s32[]{:S(2)}) async-start(), calls=%async_computation.8 | async-start | bytes 4718592 | tf_op jit(solution)/shard_map/reduce_scatter | solution.py:113
  171.8 1.1 copy-start.3
  172.9 4.3 %copy-start.6 = (bf16[1,1,2048,768]{3,2,1,0:T(8,128)(2,1)S(1)}, bf16[1,1,2048,768]{3,2,1,0:T(8,128)(2,1)}, u32[]{:S(2)}) copy-start(bf16[1,1,2048,768]{3,2,1,0:T(8,128)(2,1)} %all-gather.9.cloned.1.call-done) | copy-start | bytes 9437188
  227.0 11.9 %collective-permute-start = (bf16[128,2048]{1,0:T(8,128)(2,1)S(1)}, bf16[128,2048]{1,0:T(8,128)(2,1)S(1)}, u32[]{:S(2)}, u32[]{:S(2)}) collective-permute-start(bf16[128,2048]{1,0:T(8,128)(2,1)S(1)} %convolution_convert_fusion.5), channel_id=1, source_target_pairs={{0,24},{8,0},{16,8},{24,16},{1,25},{9,1},{17,9},{25,17},{2,26},{10... | collective-permute-start | bytes 1572872 | tf_op jit(solution)/shard_map/ppermute | solution.py:9
Sparse Core Ops, SparseCore 0:
  9.6 14.7 all-gather.10
  25.9 13.1 all-gather.8
  74.5 13.5 all-gather.6
  156.1 9.1 reduce-scatter.9
  167.4 12.0 reduce-scatter.11
  182.2 12.0 reduce-scatter.7
where the time goes:
time: 252 us
  waiting for transfers between devices  98.6 us (39%)
  blocking collectives  55.3 us (22%)
  matrix products  39.5 us (16%)
  local copies, waits for them, and re-layouts  22.2 us (9%)
  starting transfers between devices  17.1 us (7%)
  between operations  14.3 us (6%)
  other arithmetic  4.82 us (2%)
    all_to_all x1, blocking collectives, per_device(): lax.all_to_all(route_dx.astype(jnp.bfloat16).reshape(groups, capacity, ro...  47.4 us
    all_to_all x1, waiting for transfers between devices, per_device(): lax.all_to_all(send_rows.reshape(groups, capacity, row_width), 'expert',...  45.4 us
    all_to_all x1, waiting for transfers between devices, per_device(): lax.all_to_all(send_grads.reshape(groups, capacity, row_width), 'expert',...  37.3 us
    unnamed x22, local copies, waits for them, and re-layouts  20.6 us
    ppermute x1, waiting for transfers between devices, from_behind(): lax.ppermute(shard, axis, [(i, (i + by) % length) for i in range(length)])  8.49 us
    all_to_all x1, blocking collectives, per_device(): lax.all_to_all(send_probs.reshape(groups, capacity).astype(jnp.bfloat16),...  7.89 us
    dot_general x1, matrix products, expert_grads(): lax.dot_general(grads_in, down_part, contract_last, preferred_element_typ...  6.46 us
    all_to_all x1, starting transfers between devices, per_device(): lax.all_to_all(send_rows.reshape(groups, capacity, row_width), 'expert',...  6.45 us
  transfers between devices with their start and end apart: 10, of which 4 were waited for; matrix products, arithmetic and copies ran while one was open for 17% of the time, Pallas kernels for 0%

commit v1 on v0

--- a/solution.py
+++ b/solution.py
@@ -39,7 +39,7 @@
     return (route_dx, prob_part, grad_gate, grad_up, grad_down)
 
 
-def per_device(tokens, out_grad, expert_ids, route_probs, gate_weight, up_weight, down_weight):
+def exchange_plan(tokens, out_grad, expert_ids, route_probs, gate_weight, up_weight, down_weight):
     local_tokens = tokens[0]
     local_grads = out_grad[0]
     tok_count, row_width = local_tokens.shape
@@ -148,6 +148,140 @@
     )
 
 
+INWARD = [(0, 1), (3, 2)]
+OUTWARD = [(1, 0), (2, 3)]
+MIDDLE = [(1, 2), (2, 1)]
+PAIRS = INWARD + OUTWARD
+SWAP = [(0, 1), (1, 0)]
+
+
+def line_plan(tokens, out_grad, expert_ids, route_probs, gate_weight, up_weight, down_weight):
+    f32, bf16 = jnp.float32, jnp.bfloat16
+    place = lax.axis_index("expert")
+    inner = (place == 1) | (place == 2)
+    tok, grd = tokens[0], out_grad[0]
+    ids, probs = expert_ids[0], route_probs[0]
+    half = gate_weight.shape[3]
+
+    def over(x, pairs):
+        return lax.ppermute(x, "expert", pairs)
+
+    def pick(a, b):
+        return jnp.where(inner, a, b)
+
+    def mm(a, b, dims):
+        return lax.dot_general(a, b, (dims, ((), ())), preferred_element_type=f32)
+
+    def column(k):
+        return jnp.sum(jnp.where(ids == (place ^ k), probs, 0.0), axis=1)
+
+    def flip(x, k):
+        return over(x, [(i, i ^ k) for i in range(4)])
+
+    own_w = jnp.concatenate([gate_weight[0, 0], up_weight[0, 0]], axis=1)
+    own_d = down_weight[0, 0]
+    t_near = over(tok, PAIRS)
+    t_mid_in = over(tok, MIDDLE)
+    g_in = over(grd, INWARD)
+    sib_w = lax.ppermute(own_w, "dp", SWAP)
+    sib_d = lax.ppermute(own_d, "dp", SWAP)
+    p_own = column(0)
+    p1, p2, p3 = (flip(column(k).reshape(1, -1), k).reshape(-1) for k in (1, 2, 3))
+    p_mid, p_far = pick(p3, p2), pick(p2, p3)
+
+    t_mid_out = over(t_mid_in, OUTWARD)
+    t_far_in = over(t_near, MIDDLE)
+    t_far_out = over(t_far_in, OUTWARD)
+    g_far_in = over(g_in, MIDDLE)
+    g_far_out = over(g_far_in, OUTWARD)
+    g_mid_in = over(grd, MIDDLE)
+    g_mid_out = over(g_mid_in, OUTWARD)
+    g_out = over(grd, OUTWARD)
+    t_mid, t_far = pick(t_mid_in, t_mid_out), pick(t_far_in, t_far_out)
+    g_far, g_mid, g_near = pick(g_far_in, g_far_out), pick(g_mid_in, g_mid_out), g_in + g_out
+
+    def ahead(rows, p):
+        out = []
+        for w in (own_w, sib_w):
+            both = mm(rows, w, ((1,), (0,)))
+            gate, up = both[:, :half], both[:, half:]
+            sig = jax.nn.sigmoid(gate)
+            silu = gate * sig
+            act = silu * up
+            scaled = (p[:, None] * act).astype(bf16)
+            by_gate = p[:, None] * up * sig * (1.0 + gate * (1.0 - sig))
+            by_up = p[:, None] * silu
+            out.append((act, scaled, by_gate, by_up))
+        return out
+
+    def behind(grads, parts):
+        dots, halves, dx = 0.0, [], 0.0
+        for (act, scaled, by_gate, by_up), d, w in zip(parts, (own_d, sib_d), (own_w, sib_w)):
+            hidden = mm(grads, d, ((1,), (1,)))
+            dots = dots + jnp.sum(act * hidden, axis=1)
+            both = jnp.concatenate([hidden * by_gate, hidden * by_up], axis=1).astype(bf16)
+            dx = dx + mm(both, w, ((1,), (1,)))
+            halves.append(both)
+        return dx.astype(bf16), dots, halves
+
+    a_own, a_near = ahead(tok, p_own), ahead(t_near, p1)
+    a_mid, a_far = ahead(t_mid, p_mid), ahead(t_far, p_far)
+    dx_own, dot_own, h_own = behind(grd, a_own)
+    dx_far, dot_far, h_far = behind(g_far, a_far)
+    r5 = over(dx_far, INWARD)
+    dx_mid, dot_mid, h_mid = behind(g_mid, a_mid)
+    r4 = over(dx_mid, INWARD)
+    r3 = over(dx_far + r5, MIDDLE)
+    r2 = over(dx_mid + r4, MIDDLE)
+    dx_near, dot_near, h_near = behind(g_near, a_near)
+    r1 = over(dx_near + r3, PAIRS)
+
+    def section_hop(x):
+        n = lax.axis_size("section")
+        return lax.ppermute(x, "section", [(i, (i - 1) % n) for i in range(n)])
+
+    token_grad = (dx_own.astype(f32) + r1.astype(f32) + r2.astype(f32)).astype(bf16)
+    upstream = section_hop(token_grad)
+
+    d1 = flip(dot_near.reshape(1, -1), 1).reshape(-1)
+    d2 = flip(pick(dot_far, dot_mid).reshape(1, -1), 2).reshape(-1)
+    d3 = flip(pick(dot_mid, dot_far).reshape(1, -1), 3).reshape(-1)
+    prob_grad = sum(
+        jnp.where(ids == (place ^ k), d[:, None], 0.0) for k, d in enumerate((dot_own, d1, d2, d3))
+    )
+
+    rows = jnp.concatenate([tok, t_far, t_mid, t_near], axis=0)
+    grads = jnp.concatenate([grd, g_far, g_mid, g_near], axis=0)
+    slots = ((a_own, h_own), (a_far, h_far), (a_mid, h_mid), (a_near, h_near))
+
+    def weight_grads(side):
+        hs = jnp.concatenate([h[side] for _, h in slots], axis=0)
+        sc = jnp.concatenate([a[side][1] for a, _ in slots], axis=0)
+        return mm(rows, hs, ((0,), (0,))), mm(sc, grads, ((0,), (0,)))
+
+    sib_gu, sib_dn = weight_grads(1)
+    got_gu = lax.ppermute(sib_gu.astype(bf16), "dp", SWAP)
+    got_dn = lax.ppermute(sib_dn.astype(bf16), "dp", SWAP)
+    own_gu, own_dn = weight_grads(0)
+    sum_gu = (own_gu + got_gu.astype(f32)).astype(bf16)
+    sum_dn = (own_dn + got_dn.astype(f32)).astype(bf16)
+    return (
+        upstream[None],
+        prob_grad[None],
+        sum_gu[:, :half][None, None],
+        sum_gu[:, half:][None, None],
+        sum_dn[None, None],
+    )
+
+
+def per_device(tokens, out_grad, expert_ids, route_probs, gate_weight, up_weight, down_weight):
+    count, top = expert_ids.shape[1:]
+    groups = lax.axis_size("expert")
+    whole_blocks = 2 * count * top // groups >= count
+    plan = line_plan if groups == 4 and lax.axis_size("dp") == 2 and whole_blocks else exchange_plan
+    return plan(tokens, out_grad, expert_ids, route_probs, gate_weight, up_weight, down_weight)
+
+
 def solution(mesh):
     in_specs = (
         P("section", ("dp", "expert"), None),

time: 252 us -> 157 us (0.62)
  blocking collectives: 55.3 us -> 0 us
  waiting for transfers between devices: 98.6 us -> 71.5 us
  starting transfers between devices: 17.1 us -> 42.9 us
  local copies, waits for them, and re-layouts: 22.2 us -> 4.4 us
  between operations: 14.3 us -> 1.2 us
  matrix products: 39.5 us -> 31.4 us
    all_to_all x3 -> x0, waiting for transfers between devices: 87.9 us -> none  [the longest x1 45.4 us: per_device(): lax.all_to_all(send_rows.reshape(groups, capacity, row_width), 'expert',...]
    ppermute x1 -> x27, waiting for transfers between devices: 8.49 us -> 71.5 us  [the longest x22 64.4 us: over(): return lax.ppermute(x, 'expert', pairs)]
    all_to_all x2 -> x0, blocking collectives: 55.3 us -> none  [the longest x1 47.4 us: per_device(): lax.all_to_all(route_dx.astype(jnp.bfloat16).reshape(groups, capacity, ro...]
    ppermute x1 -> x27, starting transfers between devices: 2.59 us -> 42.9 us  [the longest x22 39.5 us: over(): return lax.ppermute(x, 'expert', pairs)]
    unnamed x22 -> x17, local copies, waits for them, and re-layouts: 20.6 us -> 2.42 us
    all_to_all x3 -> x0, starting transfers between devices: 14.1 us -> none  [the longest x1 6.45 us: per_device(): lax.all_to_all(send_rows.reshape(groups, capacity, row_width), 'expert',...]
    dot_general x11 -> x28, matrix products: 39.5 us -> 31.4 us  [mm(): return lax.dot_general(a, b, (dims, ((), ())), preferred_element_type=f32)]
    convert_element_type x4 -> x0, other arithmetic: 3.11 us -> none  [the longest x1 3.1 us: expert_grads(): up_grad = (hidden_scaled * gate_pre * sigmoid_gate).astype(jnp.bfloat16)]
  transfers between devices with their start and end apart: 10 -> 27, of which waited for: 4 -> 9; matrix products, arithmetic and copies ran while one was open for 17% -> 21% of each run, Pallas kernels for 0% -> 0%
where the time goes in v1:
time: 157 us; the launch traced here: 156 us
  waiting for transfers between devices  71.5 us (46%)
  starting transfers between devices  42.9 us (27%)
  matrix products  31.4 us (20%)
  other arithmetic  4.66 us (3%)
  local copies, waits for them, and re-layouts  4.4 us (3%)
    ppermute x22, waiting for transfers between devices, over(): return lax.ppermute(x, 'expert', pairs)  64.4 us
    ppermute x22, starting transfers between devices, over(): return lax.ppermute(x, 'expert', pairs)  39.5 us
    dot_general x28, matrix products, mm(): return lax.dot_general(a, b, (dims, ((), ())), preferred_element_type=f32)  31.4 us
    ppermute x1, waiting for transfers between devices, section_hop(): return lax.ppermute(x, 'section', [(i, (i - 1) % n) for i in range(n)])  7.09 us
  transfers between devices with their start and end apart: 27, of which 9 were waited for; matrix products, arithmetic and copies ran while one was open for 21% of the time, Pallas kernels for 0%

profile of v1, /device:TPU:0, one launch (start us, length us, event | category | flops | bytes accessed | tf_op | source)
XLA Modules:
  0.0 156.1 jit_solution(12842615243219571)
XLA Ops:
  0.6 1.5 collective-permute-start.17
  2.1 5.1 %collective-permute-start.5 = (bf16[128,2048]{1,0:T(8,128)(2,1)}, bf16[128,2048]{1,0:T(8,128)(2,1)}, u32[]{:S(2)}, u32[]{:S(2)}) collective-permute-start(bf16[128,2048]{1,0:T(8,128)(2,1)} %bitcast.94), channel_id=1, source_target_pairs={{0,1},{3,2},{1,0},{2,3},{4,5},{7,6},{5,4},{6,7},{8,9},{11,10},{9,8... | collective-permute-start | bytes 1572872 | tf_op jit(solution)/shard_map/ppermute | solution.py:167
  7.2 1.2 select_reduce_fusion.2
  8.4 1.3 collective-permute-start.9
  9.9 1.5 collective-permute-start.15
  11.4 2.2 %pad_maximum_fusion = bf16[2048,768]{1,0:T(8,128)(2,1)S(1)} fusion(bf16[2048,384]{1,0:T(8,128)(2,1)} %bitcast.98, bf16[2048,384]{1,0:T(8,128)(2,1)} %bitcast.99), kind=kLoop, calls=%fused_computation.2 | loop fusion | flops 6291456 | bytes 6291456 | tf_op jit(solution)/shard_map/concatenate | solution.py:181
  15.1 1.3 fusion.114
  16.4 3.7 %collective-permute-done.9 = f32[1,128]{1,0:T(1,128)S(1)} collective-permute-done((f32[1,128]{1,0:T(1,128)}, f32[1,128]{1,0:T(1,128)S(1)}, u32[]{:S(2)}, u32[]{:S(2)}) %collective-permute-start.9) | collective-permute-done | bytes 544 | tf_op jit(solution)/shard_map/ppermute | solution.py:167
  20.1 1.3 collective-permute-start.3
  21.4 4.6 %collective-permute-start.2 = (bf16[128,2048]{1,0:T(8,128)(2,1)}, bf16[128,2048]{1,0:T(8,128)(2,1)S(1)}, u32[]{:S(2)}, u32[]{:S(2)}) collective-permute-start(bf16[128,2048]{1,0:T(8,128)(2,1)} %bitcast.103), channel_id=1, source_target_pairs={{0,1},{3,2},{4,5},{7,6},{8,9},{11,10},{12,13},{15,14},{16,17},{19,... | collective-permute-start | bytes 1572872 | tf_op jit(solution)/shard_map/ppermute | solution.py:167
  26.1 1.3 collective-permute-start.18
  27.4 0.8 collective-permute-start.10
  28.2 1.3 collective-permute-start.16
  29.5 1.6 %convolution_bitcast_fusion.1 = f32[128,768]{1,0:T(8,128)S(1)} fusion(bf16[128,2048]{1,0:T(8,128)(2,1)} %collective-permute-done.5, bf16[2048,768]{1,0:T(8,128)(2,1)S(1)} %pad_maximum_fusion), kind=kOutput, calls=%fused_computation.24 | convolution fusion | flops 402653184 | bytes 4063232 | tf_op jit(solution)/shard_map/dot_general | solution.py:173
  31.2 5.9 %collective-permute-done.3 = bf16[128,2048]{1,0:T(8,128)(2,1)S(1)} collective-permute-done((bf16[128,2048]{1,0:T(8,128)(2,1)}, bf16[128,2048]{1,0:T(8,128)(2,1)S(1)}, u32[]{:S(2)}, u32[]{:S(2)}) %collective-permute-start.3) | collective-permute-done | bytes 524320 | tf_op jit(solution)/shard_map/ppermute | solution.py:167
  37.1 1.0 collective-permute-start.4
  38.2 10.1 %collective-permute-done.18 = bf16[128,2048]{1,0:T(8,128)(2,1)S(1)} collective-permute-done((bf16[128,2048]{1,0:T(8,128)(2,1)}, bf16[128,2048]{1,0:T(8,128)(2,1)S(1)}, u32[]{:S(2)}, u32[]{:S(2)}) %collective-permute-start.18) | collective-permute-done | bytes 524320 | tf_op jit(solution)/shard_map/ppermute | solution.py:167
  49.2 7.7 %collective-permute-done.16 = bf16[128,2048]{1,0:T(8,128)(2,1)S(1)} collective-permute-done((bf16[128,2048]{1,0:T(8,128)(2,1)}, bf16[128,2048]{1,0:T(8,128)(2,1)S(1)}, u32[]{:S(2)}, u32[]{:S(2)}) %collective-permute-start.16) | collective-permute-done | bytes 524320 | tf_op jit(solution)/shard_map/ppermute | solution.py:167
  56.9 1.3 collective-permute-start.11
  58.2 1.3 collective-permute-start.7
  60.1 13.5 %collective-permute-done.11 = bf16[128,2048]{1,0:T(8,128)(2,1)S(1)} collective-permute-done((bf16[128,2048]{1,0:T(8,128)(2,1)S(1)}, bf16[128,2048]{1,0:T(8,128)(2,1)S(1)}, u32[]{:S(2)}, u32[]{:S(2)}) %collective-permute-start.11) | collective-permute-done | bytes 524320 | tf_op jit(solution)/shard_map/ppermute | solution.py:167
  74.3 7.0 %collective-permute-done.7 = bf16[128,2048]{1,0:T(8,128)(2,1)S(1)} collective-permute-done((bf16[128,2048]{1,0:T(8,128)(2,1)S(1)}, bf16[128,2048]{1,0:T(8,128)(2,1)S(1)}, u32[]{:S(2)}, u32[]{:S(2)}) %collective-permute-start.7) | collective-permute-done | bytes 524320 | tf_op jit(solution)/shard_map/ppermute | solution.py:167
  85.2 0.8 multiply_convert_fusion.15
  86.6 1.1 fusion.68
  87.7 1.1 fusion.7
  88.9 4.6 %collective-permute-start.12 = (bf16[128,2048]{1,0:T(8,128)(2,1)S(1)}, bf16[128,2048]{1,0:T(8,128)(2,1)S(1)}, u32[]{:S(2)}, u32[]{:S(2)}) collective-permute-start(bf16[128,2048]{1,0:T(8,128)(2,1)S(1)} %fusion.7), channel_id=1, source_target_pairs={{0,1},{3,2},{4,5},{7,6},{8,9},{11,10},{12,13},{15,14},{16,17},{19,... | collective-permute-start | bytes 1572872 | tf_op jit(solution)/shard_map/ppermute | solution.py:167
  93.5 1.6 %convolution_bitcast_fusion = f32[128,768]{1,0:T(8,128)S(1)} fusion(bf16[128,2048]{1,0:T(8,128)(2,1)} %collective-permute-done.5, bf16[2048,768]{1,0:T(8,128)(2,1)S(1)} %collective-permute-done.1), kind=kOutput, calls=%fused_computation.23 | convolution fusion | flops 402653184 | bytes 4063232 | tf_op jit(solution)/shard_map/dot_general | solution.py:173
  95.2 0.8 multiply_convert_fusion.19
  97.3 0.8 multiply_convert_fusion.23
  98.1 2.9 %convolution_convert_fusion = bf16[2048,768]{1,0:T(8,128)(2,1)S(1)} fusion(bf16[128,384]{1,0:T(8,128)(2,1)S(1)} %get-tuple-element.57, bf16[128,384]{1,0:T(8,128)(2,1)S(1)} %get-tuple-element.58, bf16[128,384]{1,0:T(8,128)(2,1)S(1)} %get-tuple-element.49, bf16[128,384]{1,0:T(8,128)(2,1)S(1)} %get-tuple-element.50, ...), kind=kOutput, calls=%fused_computation.1 | convolution fusion | flops 1626865664 | bytes 6029312 | tf_op jit(solution)/shard_map/dot_general | solution.py:173
  101.1 1.1 fusion.75
  102.2 1.2 fusion.8
  103.4 1.3 collective-permute-start.19
  105.6 1.0 convolution_convert_fusion.1
  107.2 1.1 fusion.61
  108.4 8.5 %collective-permute-done.19 = bf16[128,2048]{1,0:T(8,128)(2,1)S(1)} collective-permute-done((bf16[128,2048]{1,0:T(8,128)(2,1)S(1)}, bf16[128,2048]{1,0:T(8,128)(2,1)S(1)}, u32[]{:S(2)}, u32[]{:S(2)}) %collective-permute-start.19) | collective-permute-done | bytes 524320 | tf_op jit(solution)/shard_map/ppermute | solution.py:167
  117.7 1.2 fusion.9
  118.8 4.2 %collective-permute-start.14 = (bf16[128,2048]{1,0:T(8,128)(2,1)S(1)}, bf16[128,2048]{1,0:T(8,128)(2,1)S(1)}, u32[]{:S(2)}, u32[]{:S(2)}) collective-permute-start(bf16[128,2048]{1,0:T(8,128)(2,1)S(1)} %fusion.9), channel_id=1, source_target_pairs={{0,1},{3,2},{1,0},{2,3},{4,5},{7,6},{5,4},{6,7},{8,9},{11,10},{9,8... | collective-permute-start | bytes 1572872 | tf_op jit(solution)/shard_map/ppermute | solution.py:167
  123.0 1.1 fusion.54
  124.2 2.5 %collective-permute-start.24 = (f32[1,128]{1,0:T(1,128)S(1)}, f32[1,128]{1,0:T(1,128)S(1)}, u32[]{:S(2)}, u32[]{:S(2)}) collective-permute-start(f32[1,128]{1,0:T(1,128)S(1)} %get-tuple-element.44), channel_id=1, source_target_pairs={{0,3},{1,2},{2,1},{3,0},{4,7},{5,6},{6,5},{7,4},{8,11},{9,10},{10,... | collective-permute-start | bytes 1544 | tf_op jit(solution)/shard_map/ppermute | solution.py:167
  126.7 8.0 %collective-permute-done.14 = bf16[128,2048]{1,0:T(8,128)(2,1)S(1)} collective-permute-done((bf16[128,2048]{1,0:T(8,128)(2,1)S(1)}, bf16[128,2048]{1,0:T(8,128)(2,1)S(1)}, u32[]{:S(2)}, u32[]{:S(2)}) %collective-permute-start.14) | collective-permute-done | bytes 524320 | tf_op jit(solution)/shard_map/ppermute | solution.py:167
  134.8 1.7 %collective-permute-start.22 = (f32[1,128]{1,0:T(1,128)S(1)}, f32[1,128]{1,0:T(1,128)S(1)}, u32[]{:S(2)}, u32[]{:S(2)}) collective-permute-start(f32[1,128]{1,0:T(1,128)S(1)} %add_bitcast_fusion), channel_id=1, source_target_pairs={{0,1},{1,0},{2,3},{3,2},{4,5},{5,4},{6,7},{7,6},{8,9},{9,8},{10,11... | collective-permute-start | bytes 1544 | tf_op jit(solution)/shard_map/ppermute | solution.py:167
  136.5 1.2 fusion.5
  137.7 2.7 %collective-permute-start.21 = (bf16[128,2048]{1,0:T(8,128)(2,1)S(1)}, bf16[128,2048]{1,0:T(8,128)(2,1)S(1)}, u32[]{:S(2)}, u32[]{:S(2)}) collective-permute-start(bf16[128,2048]{1,0:T(8,128)(2,1)S(1)} %fusion.5), channel_id=1, source_target_pairs={{0,24},{8,0},{16,8},{24,16},{1,25},{9,1},{17,9},{25,17},{2,26},{10... | collective-permute-start | bytes 1572872 | tf_op jit(solution)/shard_map/ppermute | solution.py:241
  141.0 2.2 %fusion = bf16[1,1,384,2048]{3,2,1,0:T(8,128)(2,1)} fusion(bf16[384,2048]{1,0:T(8,128)(2,1)S(1)} %collective-permute-done.26, bf16[128,384]{1,0:T(8,128)(2,1)S(1)} %get-tuple-element.39, bf16[128,384]{1,0:T(8,128)(2,1)S(1)} %get-tuple-element.35, bf16[128,384]{1,0:T(8,128)(2,1)S(1)} %get-tuple-element.37, bf16[128,384]{1,0:T(8,128)(2,1)S(1)} %get-tuple-element.41, ...), kind=kOutput, calls=%fused_computation.5 | convolution fusion | flops 817627136 | bytes 5636096 | tf_op jit(solution)/shard_map/dot_general | solution.py:173
  143.2 7.1 %collective-permute-done.21 = bf16[128,2048]{1,0:T(8,128)(2,1)S(1)} collective-permute-done((bf16[128,2048]{1,0:T(8,128)(2,1)S(1)}, bf16[128,2048]{1,0:T(8,128)(2,1)S(1)}, u32[]{:S(2)}, u32[]{:S(2)}) %collective-permute-start.21) | collective-permute-done | bytes 524320 | tf_op jit(solution)/shard_map/ppermute | solution.py:241
  150.3 3.0 %add_convert_fusion = bf16[2048,768]{1,0:T(8,128)(2,1)S(1)} fusion(bf16[2048,768]{1,0:T(8,128)(2,1)S(1)} %collective-permute-done.25, bf16[128,384]{1,0:T(8,128)(2,1)S(1)} %get-tuple-element.16, bf16[128,384]{1,0:T(8,128)(2,1)S(1)} %get-tuple-element.15, bf16[128,384]{1,0:T(8,128)(2,1)S(1)} %get-tuple-element.24, bf16[128,384]{1,0:T(8,128)(2,1)S(1)} %get-tuple-element.23, ...), kind=kOutput, calls=%fused_computation | convolution fusion | flops 1630011392 | bytes 9175040 | tf_op jit(solution)/shard_map/dot_general | solution.py:173
  153.4 2.0 %slice_bitcast_fusion = (bf16[1,1,2048,384]{3,2,1,0:T(8,128)(2,1)}, bf16[1,1,2048,384]{3,2,1,0:T(8,128)(2,1)}) fusion(bf16[2048,768]{1,0:T(8,128)(2,1)S(1)} %add_convert_fusion), kind=kLoop, calls=%fused_computation.21 | loop fusion | bytes 6291456 | tf_op jit(solution)/shard_map/broadcast_in_dim | solution.py:272
  (66 shorter events, 13.4 us)
Async XLA Ops:
  0.6 25.4 %collective-permute-start.17 = (bf16[128,2048]{1,0:T(8,128)(2,1)}, bf16[128,2048]{1,0:T(8,128)(2,1)}, u32[]{:S(2)}, u32[]{:S(2)}) collective-permute-start(bf16[128,2048]{1,0:T(8,128)(2,1)} %bitcast.93), channel_id=1, source_target_pairs={{1,2},{2,1},{5,6},{6,5},{9,10},{10,9},{13,14},{14,13},{17,18},{18,... | collective-permute-start | bytes 1572872 | tf_op jit(solution)/shard_map/ppermute | solution.py:167
  2.1 25.3 %collective-permute-start.5 = (bf16[128,2048]{1,0:T(8,128)(2,1)}, bf16[128,2048]{1,0:T(8,128)(2,1)}, u32[]{:S(2)}, u32[]{:S(2)}) collective-permute-start(bf16[128,2048]{1,0:T(8,128)(2,1)} %bitcast.94), channel_id=1, source_target_pairs={{0,1},{3,2},{1,0},{2,3},{4,5},{7,6},{5,4},{6,7},{8,9},{11,10},{9,8... | collective-permute-start | bytes 1572872 | tf_op jit(solution)/shard_map/ppermute | solution.py:167
  8.4 11.7 %collective-permute-start.9 = (f32[1,128]{1,0:T(1,128)}, f32[1,128]{1,0:T(1,128)S(1)}, u32[]{:S(2)}, u32[]{:S(2)}) collective-permute-start(f32[1,128]{1,0:T(1,128)} %bitcast.12), channel_id=1, source_target_pairs={{0,3},{1,2},{2,1},{3,0},{4,7},{5,6},{6,5},{7,4},{8,11},{9,10},{10,... | collective-permute-start | bytes 1544 | tf_op jit(solution)/shard_map/ppermute | solution.py:167
  9.8 11.6 %collective-permute-start.8 = (f32[1,128]{1,0:T(1,128)}, f32[1,128]{1,0:T(1,128)S(1)}, u32[]{:S(2)}, u32[]{:S(2)}) collective-permute-start(f32[1,128]{1,0:T(1,128)} %bitcast.11), channel_id=1, source_target_pairs={{0,2},{1,3},{2,0},{3,1},{4,6},{5,7},{6,4},{7,5},{8,10},{9,11},{10,... | collective-permute-start | bytes 1544 | tf_op jit(solution)/shard_map/ppermute | solution.py:167
  9.9 18.3 %collective-permute-start.15 = (bf16[128,2048]{1,0:T(8,128)(2,1)}, bf16[128,2048]{1,0:T(8,128)(2,1)}, u32[]{:S(2)}, u32[]{:S(2)}) collective-permute-start(bf16[128,2048]{1,0:T(8,128)(2,1)} %bitcast.101), channel_id=1, source_target_pairs={{1,2},{2,1},{5,6},{6,5},{9,10},{10,9},{13,14},{14,13},{17,18},{18,... | collective-permute-start | bytes 1572872 | tf_op jit(solution)/shard_map/ppermute | solution.py:167
  11.4 2.2 %copy-start = (bf16[1,128,2048]{2,1,0:T(8,128)(2,1)S(1)}, bf16[1,128,2048]{2,1,0:T(8,128)(2,1)}, u32[]{:S(2)}) copy-start(bf16[1,128,2048]{2,1,0:T(8,128)(2,1)} %param.7) | copy-start | bytes 1572868
  13.6 1.4 copy-start.2
  13.6 1.5 copy-start.4
  20.1 17.0 %collective-permute-start.3 = (bf16[128,2048]{1,0:T(8,128)(2,1)}, bf16[128,2048]{1,0:T(8,128)(2,1)S(1)}, u32[]{:S(2)}, u32[]{:S(2)}) collective-permute-start(bf16[128,2048]{1,0:T(8,128)(2,1)} %bitcast.102), channel_id=1, source_target_pairs={{1,0},{2,3},{5,4},{6,7},{9,8},{10,11},{13,12},{14,15},{17,16},{18,... | collective-permute-start | bytes 1572872 | tf_op jit(solution)/shard_map/ppermute | solution.py:167
  21.4 15.7 %collective-permute-start.2 = (bf16[128,2048]{1,0:T(8,128)(2,1)}, bf16[128,2048]{1,0:T(8,128)(2,1)S(1)}, u32[]{:S(2)}, u32[]{:S(2)}) collective-permute-start(bf16[128,2048]{1,0:T(8,128)(2,1)} %bitcast.103), channel_id=1, source_target_pairs={{0,1},{3,2},{4,5},{7,6},{8,9},{11,10},{12,13},{15,14},{16,17},{19,... | collective-permute-start | bytes 1572872 | tf_op jit(solution)/shard_map/ppermute | solution.py:167
  26.1 22.3 %collective-permute-start.18 = (bf16[128,2048]{1,0:T(8,128)(2,1)}, bf16[128,2048]{1,0:T(8,128)(2,1)S(1)}, u32[]{:S(2)}, u32[]{:S(2)}) collective-permute-start(bf16[128,2048]{1,0:T(8,128)(2,1)} %collective-permute-done.17), channel_id=1, source_target_pairs={{1,0},{2,3},{5,4},{6,7},{9,8},{10,11},{13,12},{14,15},{17,16},{18,... | collective-permute-start | bytes 1572872 | tf_op jit(solution)/shard_map/ppermute | solution.py:167
  27.4 21.7 %copy-start.3 = (bf16[1,1,384,2048]{3,2,1,0:T(8,128)(2,1)S(1)}, bf16[1,1,384,2048]{3,2,1,0:T(8,128)(2,1)}, u32[]{:S(2)}) copy-start(bf16[1,1,384,2048]{3,2,1,0:T(8,128)(2,1)} %param.13) | copy-start | bytes 4718596
  27.4 21.7 %collective-permute-start.10 = (bf16[128,2048]{1,0:T(8,128)(2,1)}, bf16[128,2048]{1,0:T(8,128)(2,1)S(1)}, u32[]{:S(2)}, u32[]{:S(2)}) collective-permute-start(bf16[128,2048]{1,0:T(8,128)(2,1)} %collective-permute-done.5), channel_id=1, source_target_pairs={{1,2},{2,1},{5,6},{6,5},{9,10},{10,9},{13,14},{14,13},{17,18},{18,... | collective-permute-start | bytes 1572872 | tf_op jit(solution)/shard_map/ppermute | solution.py:167
  28.2 28.6 %collective-permute-start.16 = (bf16[128,2048]{1,0:T(8,128)(2,1)}, bf16[128,2048]{1,0:T(8,128)(2,1)S(1)}, u32[]{:S(2)}, u32[]{:S(2)}) collective-permute-start(bf16[128,2048]{1,0:T(8,128)(2,1)} %collective-permute-done.15), channel_id=1, source_target_pairs={{1,0},{2,3},{5,4},{6,7},{9,8},{10,11},{13,12},{14,15},{17,16},{18,... | collective-permute-start | bytes 1572872 | tf_op jit(solution)/shard_map/ppermute | solution.py:167
  37.1 46.1 %collective-permute-start.1 = (bf16[2048,768]{1,0:T(8,128)(2,1)S(1)}, bf16[2048,768]{1,0:T(8,128)(2,1)S(1)}, u32[]{:S(2)}, u32[]{:S(2)}) collective-permute-start(bf16[2048,768]{1,0:T(8,128)(2,1)S(1)} %pad_maximum_fusion), channel_id=1, source_target_pairs={{0,4},{4,0},{1,5},{5,1},{2,6},{6,2},{3,7},{7,3},{8,12},{12,8},{9,1... | collective-permute-start | bytes 9437192 | tf_op jit(solution)/shard_map/ppermute | solution.py:186
  37.1 58.1 %collective-permute-start.4 = (f32[1,128]{1,0:T(1,128)S(1)}, f32[1,128]{1,0:T(1,128)S(1)}, u32[]{:S(2)}, u32[]{:S(2)}) collective-permute-start(f32[1,128]{1,0:T(1,128)S(1)} %bitcast.106), channel_id=1, source_target_pairs={{0,1},{1,0},{2,3},{3,2},{4,5},{5,4},{6,7},{7,6},{8,9},{9,8},{10,11... | collective-permute-start | bytes 1544 | tf_op jit(solution)/shard_map/ppermute | solution.py:167
  48.3 9.9 %collective-permute-start.6 = (bf16[128,2048]{1,0:T(8,128)(2,1)S(1)}, bf16[128,2048]{1,0:T(8,128)(2,1)S(1)}, u32[]{:S(2)}, u32[]{:S(2)}) collective-permute-start(bf16[128,2048]{1,0:T(8,128)(2,1)S(1)} %collective-permute-done.2), channel_id=1, source_target_pairs={{1,2},{2,1},{5,6},{6,5},{9,10},{10,9},{13,14},{14,13},{17,18},{18,... | collective-permute-start | bytes 1572872 | tf_op jit(solution)/shard_map/ppermute | solution.py:167
  49.1 32.2 %collective-permute-start = (bf16[384,2048]{1,0:T(8,128)(2,1)S(1)}, bf16[384,2048]{1,0:T(8,128)(2,1)S(1)}, u32[]{:S(2)}, u32[]{:S(2)}) collective-permute-start(bf16[384,2048]{1,0:T(8,128)(2,1)S(1)} %bitcast.97), channel_id=1, source_target_pairs={{0,4},{4,0},{1,5},{5,1},{2,6},{6,2},{3,7},{7,3},{8,12},{12,8},{9,1... | collective-permute-start | bytes 4718600 | tf_op jit(solution)/shard_map/ppermute | solution.py:187
  56.9 16.7 %collective-permute-start.11 = (bf16[128,2048]{1,0:T(8,128)(2,1)S(1)}, bf16[128,2048]{1,0:T(8,128)(2,1)S(1)}, u32[]{:S(2)}, u32[]{:S(2)}) collective-permute-start(bf16[128,2048]{1,0:T(8,128)(2,1)S(1)} %collective-permute-done.10), channel_id=1, source_target_pairs={{1,0},{2,3},{5,4},{6,7},{9,8},{10,11},{13,12},{14,15},{17,16},{18,... | collective-permute-start | bytes 1572872 | tf_op jit(solution)/shard_map/ppermute | solution.py:167
  58.2 23.0 %collective-permute-start.7 = (bf16[128,2048]{1,0:T(8,128)(2,1)S(1)}, bf16[128,2048]{1,0:T(8,128)(2,1)S(1)}, u32[]{:S(2)}, u32[]{:S(2)}) collective-permute-start(bf16[128,2048]{1,0:T(8,128)(2,1)S(1)} %collective-permute-done.6), channel_id=1, source_target_pairs={{1,0},{2,3},{5,4},{6,7},{9,8},{10,11},{13,12},{14,15},{17,16},{18,... | collective-permute-start | bytes 1572872 | tf_op jit(solution)/shard_map/ppermute | solution.py:167
  86.0 51.7 %collective-permute-start.23 = (f32[1,128]{1,0:T(1,128)S(1)}, f32[1,128]{1,0:T(1,128)S(1)}, u32[]{:S(2)}, u32[]{:S(2)}) collective-permute-start(f32[1,128]{1,0:T(1,128)S(1)} %get-tuple-element.43), channel_id=1, source_target_pairs={{0,2},{1,3},{2,0},{3,1},{4,6},{5,7},{6,4},{7,5},{8,10},{9,11},{10,... | collective-permute-start | bytes 1544 | tf_op jit(solution)/shard_map/ppermute | solution.py:167
  88.9 15.8 %collective-permute-start.12 = (bf16[128,2048]{1,0:T(8,128)(2,1)S(1)}, bf16[128,2048]{1,0:T(8,128)(2,1)S(1)}, u32[]{:S(2)}, u32[]{:S(2)}) collective-permute-start(bf16[128,2048]{1,0:T(8,128)(2,1)S(1)} %fusion.7), channel_id=1, source_target_pairs={{0,1},{3,2},{4,5},{7,6},{8,9},{11,10},{12,13},{15,14},{16,17},{19,... | collective-permute-start | bytes 1572872 | tf_op jit(solution)/shard_map/ppermute | solution.py:167
  95.2 1.0 copy-start.1
  96.2 1.0 copy-start.5
  96.2 1.1 copy-start.6
  101.0 49.3 %collective-permute-start.25 = (bf16[2048,768]{1,0:T(8,128)(2,1)S(1)}, bf16[2048,768]{1,0:T(8,128)(2,1)S(1)}, u32[]{:S(2)}, u32[]{:S(2)}) collective-permute-start(bf16[2048,768]{1,0:T(8,128)(2,1)S(1)} %convolution_convert_fusion), channel_id=1, source_target_pairs={{0,4},{4,0},{1,5},{5,1},{2,6},{6,2},{3,7},{7,3},{8,12},{12,8},{9,1... | collective-permute-start | bytes 9437192 | tf_op jit(solution)/shard_map/ppermute | solution.py:263
  103.4 13.4 %collective-permute-start.19 = (bf16[128,2048]{1,0:T(8,128)(2,1)S(1)}, bf16[128,2048]{1,0:T(8,128)(2,1)S(1)}, u32[]{:S(2)}, u32[]{:S(2)}) collective-permute-start(bf16[128,2048]{1,0:T(8,128)(2,1)S(1)} %fusion.8), channel_id=1, source_target_pairs={{0,1},{3,2},{4,5},{7,6},{8,9},{11,10},{12,13},{15,14},{16,17},{19,... | collective-permute-start | bytes 1572872 | tf_op jit(solution)/shard_map/ppermute | solution.py:167
  104.9 12.7 %collective-permute-start.13 = (bf16[128,2048]{1,0:T(8,128)(2,1)S(1)}, bf16[128,2048]{1,0:T(8,128)(2,1)S(1)}, u32[]{:S(2)}, u32[]{:S(2)}) collective-permute-start(bf16[128,2048]{1,0:T(8,128)(2,1)S(1)} %add.162), channel_id=1, source_target_pairs={{1,2},{2,1},{5,6},{6,5},{9,10},{10,9},{13,14},{14,13},{17,18},{18,... | collective-permute-start | bytes 1572872 | tf_op jit(solution)/shard_map/ppermute | solution.py:167
  106.6 34.4 %collective-permute-start.26 = (bf16[384,2048]{1,0:T(8,128)(2,1)S(1)}, bf16[384,2048]{1,0:T(8,128)(2,1)S(1)}, u32[]{:S(2)}, u32[]{:S(2)}) collective-permute-start(bf16[384,2048]{1,0:T(8,128)(2,1)S(1)} %convolution_convert_fusion.1), channel_id=1, source_target_pairs={{0,4},{4,0},{1,5},{5,1},{2,6},{6,2},{3,7},{7,3},{8,12},{12,8},{9,1... | collective-permute-start | bytes 4718600 | tf_op jit(solution)/shard_map/ppermute | solution.py:264
  116.9 7.3 %collective-permute-start.20 = (bf16[128,2048]{1,0:T(8,128)(2,1)S(1)}, bf16[128,2048]{1,0:T(8,128)(2,1)S(1)}, u32[]{:S(2)}, u32[]{:S(2)}) collective-permute-start(bf16[128,2048]{1,0:T(8,128)(2,1)S(1)} %add.170), channel_id=1, source_target_pairs={{1,2},{2,1},{5,6},{6,5},{9,10},{10,9},{13,14},{14,13},{17,18},{18,... | collective-permute-start | bytes 1572872 | tf_op jit(solution)/shard_map/ppermute | solution.py:167
  118.8 16.0 %collective-permute-start.14 = (bf16[128,2048]{1,0:T(8,128)(2,1)S(1)}, bf16[128,2048]{1,0:T(8,128)(2,1)S(1)}, u32[]{:S(2)}, u32[]{:S(2)}) collective-permute-start(bf16[128,2048]{1,0:T(8,128)(2,1)S(1)} %fusion.9), channel_id=1, source_target_pairs={{0,1},{3,2},{1,0},{2,3},{4,5},{7,6},{5,4},{6,7},{8,9},{11,10},{9,8... | collective-permute-start | bytes 1572872 | tf_op jit(solution)/shard_map/ppermute | solution.py:167
  124.2 16.3 %copy-start.7 = (s32[1,128,2]{1,2,0:T(2,128)S(1)}, s32[1,128,2]{1,2,0:T(2,128)}, u32[]{:S(2)}) copy-start(s32[1,128,2]{1,2,0:T(2,128)} %param.9) | copy-start | bytes 3076
  124.2 16.2 %collective-permute-start.24 = (f32[1,128]{1,0:T(1,128)S(1)}, f32[1,128]{1,0:T(1,128)S(1)}, u32[]{:S(2)}, u32[]{:S(2)}) collective-permute-start(f32[1,128]{1,0:T(1,128)S(1)} %get-tuple-element.44), channel_id=1, source_target_pairs={{0,3},{1,2},{2,1},{3,0},{4,7},{5,6},{6,5},{7,4},{8,11},{9,10},{10,... | collective-permute-start | bytes 1544 | tf_op jit(solution)/shard_map/ppermute | solution.py:167
  134.8 5.7 %collective-permute-start.22 = (f32[1,128]{1,0:T(1,128)S(1)}, f32[1,128]{1,0:T(1,128)S(1)}, u32[]{:S(2)}, u32[]{:S(2)}) collective-permute-start(f32[1,128]{1,0:T(1,128)S(1)} %add_bitcast_fusion), channel_id=1, source_target_pairs={{0,1},{1,0},{2,3},{3,2},{4,5},{5,4},{6,7},{7,6},{8,9},{9,8},{10,11... | collective-permute-start | bytes 1544 | tf_op jit(solution)/shard_map/ppermute | solution.py:167
  137.7 12.6 %collective-permute-start.21 = (bf16[128,2048]{1,0:T(8,128)(2,1)S(1)}, bf16[128,2048]{1,0:T(8,128)(2,1)S(1)}, u32[]{:S(2)}, u32[]{:S(2)}) collective-permute-start(bf16[128,2048]{1,0:T(8,128)(2,1)S(1)} %fusion.5), channel_id=1, source_target_pairs={{0,24},{8,0},{16,8},{24,16},{1,25},{9,1},{17,9},{25,17},{2,26},{10... | collective-permute-start | bytes 1572872 | tf_op jit(solution)/shard_map/ppermute | solution.py:241

commit v2 on v0

--- a/solution.py
+++ b/solution.py
@@ -39,7 +39,7 @@
     return (route_dx, prob_part, grad_gate, grad_up, grad_down)
 
 
-def per_device(tokens, out_grad, expert_ids, route_probs, gate_weight, up_weight, down_weight):
+def exchange_plan(tokens, out_grad, expert_ids, route_probs, gate_weight, up_weight, down_weight):
     local_tokens = tokens[0]
     local_grads = out_grad[0]
     tok_count, row_width = local_tokens.shape
@@ -148,6 +148,194 @@
     )
 
 
+INWARD = [(0, 1), (3, 2)]
+OUTWARD = [(1, 0), (2, 3)]
+MIDDLE = [(1, 2), (2, 1)]
+PAIRS = INWARD + OUTWARD
+SWAP = [(0, 1), (1, 0)]
+F32, BF16 = jnp.float32, jnp.bfloat16
+
+
+def line_plan(tokens, out_grad, expert_ids, route_probs, gate_weight, up_weight, down_weight):
+    place = lax.axis_index("expert")
+    inner = (place == 1) | (place == 2)
+    tok, grd = tokens[0], out_grad[0]
+    ids, probs = expert_ids[0], route_probs[0]
+    half = gate_weight.shape[3]
+
+    def over(x, pairs, name, axis="expert"):
+        with jax.named_scope(name):
+            return lax.ppermute(x, axis, pairs)
+
+    def mm(a, b, dims):
+        return lax.dot_general(a, b, (dims, ((), ())), preferred_element_type=F32)
+
+    def pick(a, b):
+        return jnp.where(inner, a, b)
+
+    def small(x, k, name):
+        return over(x, [(i, i ^ k) for i in range(4)], name)
+
+    v = dict(tok=tok, grd=grd, gate=gate_weight[0, 0], up=up_weight[0, 0], own_d=down_weight[0, 0])
+
+    def sync(**ready):
+        v.update(ready)
+        v.update(lax.optimization_barrier(v))
+
+    def ahead(rows, w):
+        with jax.named_scope("ahead"):
+            return mm(w, rows, ((0,), (1,)))
+
+    def ahead_both(rows):
+        return [ahead(rows, v["own_w"]), ahead(rows, v["sib_w"])]
+
+    def behind(grads, parts, p):
+        with jax.named_scope("behind"):
+            dots, halves, dx = 0.0, [], 0.0
+            for pre, d, w in zip(parts, (v["own_d"], v["sib_d"]), (v["own_w"], v["sib_w"])):
+                gate, up = pre[:half], pre[half:]
+                sig = jax.nn.sigmoid(gate)
+                silu = gate * sig
+                act = silu * up
+                by_gate = up * sig * (1.0 + gate * (1.0 - sig))
+                hidden = mm(d, grads, ((1,), (1,)))
+                dots = dots + jnp.sum(act * hidden, axis=0, keepdims=True)
+                scaled = p * hidden
+                both = jnp.concatenate([scaled * by_gate, scaled * silu], axis=0).astype(BF16)
+                dx = dx + mm(both, w, ((0,), (1,)))
+                halves.append((both, (p * act).astype(BF16)))
+            return dx.astype(BF16), (dots, halves)
+
+    columns = [
+        jnp.sum(jnp.where(ids == (place ^ k), probs, 0.0), axis=1).reshape(1, -1) for k in range(4)
+    ]
+    def tick():
+        return over(v["columns"][0], SWAP, "tick", "dp")
+
+    sync(columns=columns)
+    t_near = over(v["tok"], PAIRS, "t_near")
+    t_mid_in = over(v["tok"], MIDDLE, "t_mid_in")
+    p_near, p_cross, p_flip = (small(v["columns"][k], k, "p") for k in (1, 2, 3))
+    own_w = jnp.concatenate([v["gate"], v["up"]], axis=1)
+    a_own = ahead(v["tok"], own_w)
+    sync(own_w=own_w, a_own=a_own)
+
+    sync(t_near=t_near, t_mid_in=t_mid_in, p_near=p_near, p_cross=p_cross, p_flip=p_flip, tick=tick())
+    g_near = over(v["grd"], PAIRS, "g_near")
+    t_mid_out = over(v["t_mid_in"], OUTWARD, "t_mid_out")
+    t_far_in = over(v["t_near"], MIDDLE, "t_far_in")
+    sib_g = over(v["gate"], SWAP, "sib_g", "dp")
+    sib_u = over(v["up"], SWAP, "sib_u", "dp")
+
+    sync(g_near=g_near, t_far_in=t_far_in, sib_g=sib_g, sib_u=sib_u)
+    g_far_in = over(v["g_near"], MIDDLE, "g_far_in")
+    t_far_out = over(v["t_far_in"], OUTWARD, "t_far_out")
+    g_mid_in = over(v["grd"], MIDDLE, "g_mid_in")
+    sib_d = over(v["own_d"], SWAP, "sib_d", "dp")
+    sib_w = jnp.concatenate([v["sib_g"], v["sib_u"]], axis=1)
+    for name in ("gate", "up", "sib_g", "sib_u"):
+        del v[name]
+    a_own = [v["a_own"], ahead(v["tok"], sib_w)]
+    sync(a_own=a_own, sib_w=sib_w)
+
+    sync(t_mid_out=t_mid_out, g_far_in=g_far_in, tick=tick())
+    g_far_out = over(v["g_far_in"], OUTWARD, "g_far_out")
+    t_cross = pick(v["t_far_in"], v["t_mid_out"])
+    a_near, a_cross = ahead_both(v["t_near"]), ahead_both(t_cross)
+    sync(t_cross=t_cross, a_cross=a_cross, a_near=a_near)
+
+    sync(t_far_out=t_far_out, g_mid_in=g_mid_in, sib_d=sib_d, tick=tick())
+    g_mid_out = over(v["g_mid_in"], OUTWARD, "g_mid_out")
+    t_flip = pick(v["t_mid_in"], v["t_far_out"])
+    a_flip = ahead_both(t_flip)
+    dx_own, k_own = behind(v["grd"], v["a_own"], v["columns"][0])
+    sync(t_flip=t_flip, a_flip=a_flip, dx_own=dx_own, k_own=k_own)
+    sync(tick=tick())
+
+    sync(g_far_out=g_far_out)
+    g_flip = pick(v["g_mid_in"], v["g_far_out"])
+    dx_flip, k_flip = behind(g_flip, v["a_flip"], v["p_flip"])
+    sync(g_flip=g_flip, dx_flip=dx_flip, k_flip=k_flip)
+    r5 = over(v["dx_flip"], INWARD, "r5")
+
+    sync(g_mid_out=g_mid_out)
+    g_cross = pick(v["g_far_in"], v["g_mid_out"])
+    dx_cross, k_cross = behind(g_cross, v["a_cross"], v["p_cross"])
+    sync(g_cross=g_cross, dx_cross=dx_cross, k_cross=k_cross)
+    r4 = over(v["dx_cross"], INWARD, "r4")
+    dx_near, k_near = behind(v["g_near"], v["a_near"], v["p_near"])
+    sync(dx_near=dx_near, k_near=k_near)
+
+    sync(r5=r5, tick=tick())
+    back = v["dx_cross"] + v["r5"]
+    sync(back=back)
+    r3 = over(v["back"], MIDDLE, "r3")
+
+    def kept(which, side):
+        slots = [v["k_" + name][1][side][which] for name in ("own", "near", "cross", "flip")]
+        return jnp.concatenate(slots, axis=1)
+
+    def all_rows():
+        return jnp.concatenate([v["tok"], v["t_near"], v["t_cross"], v["t_flip"]], axis=0)
+
+    def all_grads():
+        return jnp.concatenate([v["grd"], v["g_near"], v["g_cross"], v["g_flip"]], axis=0)
+
+    with jax.named_scope("weight_grads"):
+        sib_gu = mm(all_rows(), kept(0, 1), ((0,), (1,))).astype(BF16)
+        sib_dn = mm(kept(1, 1), all_grads(), ((1,), (0,))).astype(BF16)
+    sync(sib_gu=sib_gu, sib_dn=sib_dn)
+
+    sync(r4=r4, tick=tick())
+    back = v["dx_flip"] + v["r4"]
+    sync(back=back)
+    r2 = over(v["back"], MIDDLE, "r2")
+
+    sync(r3=r3)
+    back = v["dx_near"] + v["r3"]
+    sync(back=back)
+    r1 = over(v["back"], PAIRS, "r1")
+    got_gu = over(v["sib_gu"], SWAP, "got_gu", "dp")
+    got_dn = over(v["sib_dn"], SWAP, "got_dn", "dp")
+
+    sync(got_dn=got_dn, got_gu=got_gu)
+    with jax.named_scope("weight_grads"):
+        own_n = mm(kept(1, 0), all_grads(), ((1,), (0,))) + v["got_dn"].astype(F32)
+    sync(own_n=own_n.astype(BF16))
+
+    sync(r2=r2, r1=r1, tick=tick())
+    n = lax.axis_size("section")
+    total = v["dx_own"].astype(F32) + v["r1"].astype(F32) + v["r2"].astype(F32)
+    sync(total=total.astype(BF16))
+    upstream = over(v["total"], [(i, (i - 1) % n) for i in range(n)], "up", "section")
+    with jax.named_scope("weight_grads"):
+        hs = kept(0, 0)
+        own_g = mm(all_rows(), hs[:half], ((0,), (1,))) + v["got_gu"][:, :half].astype(F32)
+        own_u = mm(all_rows(), hs[half:], ((0,), (1,))) + v["got_gu"][:, half:].astype(F32)
+    sync(own_g=own_g.astype(BF16), own_u=own_u.astype(BF16))
+    dots = [v["k_own"][0]] + [
+        small(v["k_" + name][0], k, "dot") for k, name in ((1, "near"), (2, "cross"), (3, "flip"))
+    ]
+    prob_grad = sum(
+        jnp.where(ids == (place ^ k), d.reshape(-1, 1), 0.0) for k, d in enumerate(dots)
+    )
+    return (
+        upstream[None],
+        prob_grad[None],
+        v["own_g"][None, None],
+        v["own_u"][None, None],
+        v["own_n"][None, None],
+    )
+
+
+def per_device(tokens, out_grad, expert_ids, route_probs, gate_weight, up_weight, down_weight):
+    count, top = expert_ids.shape[1:]
+    groups = lax.axis_size("expert")
+    whole_blocks = 2 * count * top // groups >= count
+    plan = line_plan if groups == 4 and lax.axis_size("dp") == 2 and whole_blocks else exchange_plan
+    return plan(tokens, out_grad, expert_ids, route_probs, gate_weight, up_weight, down_weight)
+
+
 def solution(mesh):
     in_specs = (
         P("section", ("dp", "expert"), None),

time: 252 us -> 142 us (0.56)
  waiting for transfers between devices: 98.6 us -> 43.2 us
  blocking collectives: 55.3 us -> 0 us
  starting transfers between devices: 17.1 us -> 43.2 us
  local copies, waits for them, and re-layouts: 22.2 us -> 8.77 us
  between operations: 14.3 us -> 1.17 us
  matrix products: 39.5 us -> 42.5 us
  other arithmetic: 4.82 us -> 2.28 us
    all_to_all x3 -> x0, waiting for transfers between devices: 87.9 us -> none  [the longest x1 45.4 us: per_device(): lax.all_to_all(send_rows.reshape(groups, capacity, row_width), 'expert',...]
    all_to_all x2 -> x0, blocking collectives: 55.3 us -> none  [the longest x1 47.4 us: per_device(): lax.all_to_all(route_dx.astype(jnp.bfloat16).reshape(groups, capacity, ro...]
    ppermute x1 -> x27, starting transfers between devices: 2.59 us -> 43.2 us  [over(): return lax.ppermute(x, axis, pairs)]
    ppermute x1 -> x27, waiting for transfers between devices: 8.49 us -> 43.2 us  [over(): return lax.ppermute(x, axis, pairs)]
    unnamed x22 -> x17, local copies, waits for them, and re-layouts: 20.6 us -> 5.23 us
    all_to_all x3 -> x0, starting transfers between devices: 14.1 us -> none  [the longest x1 6.45 us: per_device(): lax.all_to_all(send_rows.reshape(groups, capacity, row_width), 'expert',...]
    concatenate x0 -> x4, local copies, waits for them, and re-layouts: none -> 3.54 us  [the longest x1 1.73 us: line_plan(): own_w = jnp.concatenate([v['gate'], v['up']], axis=1)]
    dot_general x11 -> x29, matrix products: 39.5 us -> 42.5 us  [mm(): return lax.dot_general(a, b, (dims, ((), ())), preferred_element_type=F32)]
  transfers between devices with their start and end apart: 10 -> 27, of which waited for: 4 -> 13; matrix products, arithmetic and copies ran while one was open for 17% -> 37% of each run, Pallas kernels for 0% -> 0%
where the time goes in v2:
time: 142 us; the launch traced here: 141 us
  starting transfers between devices  43.2 us (30%)
  waiting for transfers between devices  43.2 us (30%)
  matrix products  42.5 us (30%)
  local copies, waits for them, and re-layouts  8.77 us (6%)
  other arithmetic  2.28 us (2%)
    ppermute x27, waiting for transfers between devices, over(): return lax.ppermute(x, axis, pairs)  43.2 us
    ppermute x27, starting transfers between devices, over(): return lax.ppermute(x, axis, pairs)  43.2 us
    dot_general x29, matrix products, mm(): return lax.dot_general(a, b, (dims, ((), ())), preferred_element_type=F32)  42.5 us
    unnamed x17, local copies, waits for them, and re-layouts  5.23 us
  transfers between devices with their start and end apart: 27, of which 13 were waited for; matrix products, arithmetic and copies ran while one was open for 37% of the time, Pallas kernels for 0%

profile of v2, /device:TPU:0, one launch (start us, length us, event | category | flops | bytes accessed | tf_op | source)
XLA Modules:
  0.0 141.1 jit_solution(1456560915252995048)
XLA Ops:
  1.4 1.6 %collective-permute-start.3 = (bf16[128,2048]{1,0:T(8,128)(2,1)}, bf16[128,2048]{1,0:T(8,128)(2,1)}, u32[]{:S(2)}, u32[]{:S(2)}) collective-permute-start(bf16[128,2048]{1,0:T(8,128)(2,1)} %bitcast.71), channel_id=1, source_target_pairs={{1,2},{2,1},{5,6},{6,5},{9,10},{10,9},{13,14},{14,13},{17,18},{18,... | collective-permute-start | bytes 1572872 | tf_op jit(solution)/shard_map/t_mid_in/ppermute | solution.py:168
  3.0 5.1 %collective-permute-start.4 = (bf16[128,2048]{1,0:T(8,128)(2,1)}, bf16[128,2048]{1,0:T(8,128)(2,1)}, u32[]{:S(2)}, u32[]{:S(2)}) collective-permute-start(bf16[128,2048]{1,0:T(8,128)(2,1)} %bitcast.72), channel_id=1, source_target_pairs={{0,1},{3,2},{1,0},{2,3},{4,5},{7,6},{5,4},{6,7},{8,9},{11,10},{9,8... | collective-permute-start | bytes 1572872 | tf_op jit(solution)/shard_map/t_near/ppermute | solution.py:168
  8.6 1.9 %collective-permute-start.1 = (f32[1,128]{1,0:T(1,128)S(1)}, f32[1,128]{1,0:T(1,128)S(1)}, u32[]{:S(2)}, u32[]{:S(2)}) collective-permute-start(f32[1,128]{1,0:T(1,128)S(1)} %bitcast.80), channel_id=1, source_target_pairs={{0,3},{1,2},{2,1},{3,0},{4,7},{5,6},{6,5},{7,4},{8,11},{9,10},{10,... | collective-permute-start | bytes 1544 | tf_op jit(solution)/shard_map/p/ppermute | solution.py:168
  11.6 1.6 %constant_dynamic-update-slice_fusion.1 = bf16[2048,768]{1,0:T(8,128)(2,1)S(1)} fusion(bf16[2048,384]{1,0:T(8,128)(2,1)} %bitcast.4), kind=kLoop, calls=%fused_computation.128 | loop fusion | bytes 3145728
  13.1 1.7 %constant_dynamic-update-slice_fusion = bf16[2048,768]{1,0:T(8,128)(2,1)S(1)} fusion(bf16[2048,768]{1,0:T(8,128)(2,1)S(1)} %constant_dynamic-update-slice_fusion.1, bf16[2048,384]{1,0:T(8,128)(2,1)} %bitcast.8), kind=kLoop, calls=%fused_computation.127 | loop fusion | bytes 3145728 | tf_op jit(solution)/shard_map/concatenate | solution.py:219
  15.9 3.8 %collective-permute-done = f32[1,128]{1,0:T(1,128)S(1)} collective-permute-done((f32[1,128]{1,0:T(1,128)S(1)}, f32[1,128]{1,0:T(1,128)S(1)}, u32[]{:S(2)}, u32[]{:S(2)}) %collective-permute-start) | collective-permute-done | bytes 544 | tf_op jit(solution)/shard_map/p/ppermute | solution.py:168
  19.7 1.3 collective-permute-done.1
  22.3 1.5 %collective-permute-start.8 = (bf16[128,2048]{1,0:T(8,128)(2,1)}, bf16[128,2048]{1,0:T(8,128)(2,1)}, u32[]{:S(2)}, u32[]{:S(2)}) collective-permute-start(bf16[128,2048]{1,0:T(8,128)(2,1)} %collective-permute-done.4), channel_id=1, source_target_pairs={{1,2},{2,1},{5,6},{6,5},{9,10},{10,9},{13,14},{14,13},{17,18},{18,... | collective-permute-start | bytes 1572872 | tf_op jit(solution)/shard_map/t_far_in/ppermute | solution.py:168
  23.8 1.4 %collective-permute-start.10 = (bf16[128,2048]{1,0:T(8,128)(2,1)}, bf16[128,2048]{1,0:T(8,128)(2,1)S(1)}, u32[]{:S(2)}, u32[]{:S(2)}) collective-permute-start(bf16[128,2048]{1,0:T(8,128)(2,1)} %collective-permute-done.3), channel_id=1, source_target_pairs={{1,0},{2,3},{5,4},{6,7},{9,8},{10,11},{13,12},{14,15},{17,16},{18,... | collective-permute-start | bytes 1572872 | tf_op jit(solution)/shard_map/t_mid_out/ppermute | solution.py:168
  25.2 11.5 %collective-permute-done.5 = bf16[128,2048]{1,0:T(8,128)(2,1)} collective-permute-done((bf16[128,2048]{1,0:T(8,128)(2,1)}, bf16[128,2048]{1,0:T(8,128)(2,1)}, u32[]{:S(2)}, u32[]{:S(2)}) %collective-permute-start.5) | collective-permute-done | bytes 524320 | tf_op jit(solution)/shard_map/g_near/ppermute | solution.py:168
  36.7 1.6 %constant_dynamic-update-slice_fusion.3 = bf16[2048,768]{1,0:T(8,128)(2,1)S(1)} fusion(bf16[2048,384]{1,0:T(8,128)(2,1)} %collective-permute-done.6), kind=kLoop, calls=%fused_computation.130 | loop fusion | bytes 3145728
  39.8 1.3 collective-permute-start.13
  41.1 1.7 %constant_dynamic-update-slice_fusion.2 = bf16[2048,768]{1,0:T(8,128)(2,1)S(1)} fusion(bf16[2048,768]{1,0:T(8,128)(2,1)S(1)} %constant_dynamic-update-slice_fusion.3, bf16[2048,384]{1,0:T(8,128)(2,1)} %collective-permute-done.7), kind=kLoop, calls=%fused_computation.129 | loop fusion | bytes 3145728 | tf_op jit(solution)/shard_map/concatenate | solution.py:235
  43.8 3.1 %collective-permute-done.10 = bf16[128,2048]{1,0:T(8,128)(2,1)S(1)} collective-permute-done((bf16[128,2048]{1,0:T(8,128)(2,1)}, bf16[128,2048]{1,0:T(8,128)(2,1)S(1)}, u32[]{:S(2)}, u32[]{:S(2)}) %collective-permute-start.10) | collective-permute-done | bytes 524320 | tf_op jit(solution)/shard_map/t_mid_out/ppermute | solution.py:168
  46.9 1.3 collective-permute-start.14
  50.4 2.1 %fusion.70 = f32[768,128]{1,0:T(8,128)S(1)} fusion(bf16[2048,768]{1,0:T(8,128)(2,1)S(1)} %constant_dynamic-update-slice_fusion, bf16[128,2048]{1,0:T(8,128)(2,1)} %collective-permute-done.4), kind=kOutput, calls=%fused_computation.163 | convolution fusion | flops 402653184 | bytes 4063232 | tf_op jit(solution)/shard_map/ahead/dot_general | solution.py:171
  52.4 2.1 %fusion.71 = f32[768,128]{1,0:T(8,128)S(1)} fusion(bf16[2048,768]{1,0:T(8,128)(2,1)S(1)} %constant_dynamic-update-slice_fusion.2, bf16[128,2048]{1,0:T(8,128)(2,1)} %collective-permute-done.4), kind=kOutput, calls=%fused_computation.164 | convolution fusion | flops 402653184 | bytes 4063232 | tf_op jit(solution)/shard_map/ahead/dot_general | solution.py:171
  54.5 6.7 %collective-permute-done.13 = bf16[128,2048]{1,0:T(8,128)(2,1)S(1)} collective-permute-done((bf16[128,2048]{1,0:T(8,128)(2,1)}, bf16[128,2048]{1,0:T(8,128)(2,1)S(1)}, u32[]{:S(2)}, u32[]{:S(2)}) %collective-permute-start.13) | collective-permute-done | bytes 524320 | tf_op jit(solution)/shard_map/t_far_out/ppermute | solution.py:168
  63.3 1.5 %collective-permute-start.15 = (bf16[128,2048]{1,0:T(8,128)(2,1)S(1)}, bf16[128,2048]{1,0:T(8,128)(2,1)S(1)}, u32[]{:S(2)}, u32[]{:S(2)}) collective-permute-start(bf16[128,2048]{1,0:T(8,128)(2,1)S(1)} %collective-permute-done.11), channel_id=1, source_target_pairs={{1,0},{2,3},{5,4},{6,7},{9,8},{10,11},{13,12},{14,15},{17,16},{18,... | collective-permute-start | bytes 1572872 | tf_op jit(solution)/shard_map/g_mid_out/ppermute | solution.py:168
  64.8 1.6 %fusion.74 = f32[384,128]{1,0:T(8,128)S(1)} fusion(bf16[384,2048]{1,0:T(8,128)(2,1)S(1)} %collective-permute-done.12, bf16[128,2048]{1,0:T(8,128)(2,1)} %bitcast.5), kind=kOutput, calls=%fused_computation.167 | convolution fusion | flops 201326592 | bytes 2293760 | tf_op jit(solution)/shard_map/behind/dot_general | solution.py:171
  66.4 1.7 %multiply_convert_fusion.23 = (bf16[384,128]{1,0:T(8,128)(2,1)S(1)}, bf16[384,128]{1,0:T(8,128)(2,1)S(1)}, f32[128]{0:T(128)S(1)}, bf16[384,128]{1,0:T(8,128)(2,...) fusion(f32[768,128]{1,0:T(8,128)S(1)} %fusion.66, ...), kind=kOutput, calls=%fused_computation.116 | convolution fusion | flops 203194112 | bytes 3671552 | tf_op jit(solution)/shard_map/behind/dot_general | solution.py:171
  68.2 1.2 fusion.65
  69.4 1.2 fusion
  70.6 1.9 %collective-permute-done.14 = bf16[128,2048]{1,0:T(8,128)(2,1)S(1)} collective-permute-done((bf16[128,2048]{1,0:T(8,128)(2,1)S(1)}, bf16[128,2048]{1,0:T(8,128)(2,1)S(1)}, u32[]{:S(2)}, u32[]{:S(2)}) %collective-permute-start.14) | collective-permute-done | bytes 524320 | tf_op jit(solution)/shard_map/g_far_out/ppermute | solution.py:168
  73.9 1.2 fusion.64
  75.1 1.2 fusion.1
  76.3 7.1 %collective-permute-start.16 = (bf16[128,2048]{1,0:T(8,128)(2,1)S(1)}, bf16[128,2048]{1,0:T(8,128)(2,1)S(1)}, u32[]{:S(2)}, u32[]{:S(2)}) collective-permute-start(bf16[128,2048]{1,0:T(8,128)(2,1)S(1)} %fusion.1), channel_id=1, source_target_pairs={{0,1},{3,2},{4,5},{7,6},{8,9},{11,10},{12,13},{15,14},{16,17},{19,... | collective-permute-start | bytes 1572872 | tf_op jit(solution)/shard_map/r5/ppermute | solution.py:168
  84.9 1.2 fusion.63
  86.1 1.2 fusion.2
  87.3 1.6 %fusion.77 = f32[384,128]{1,0:T(8,128)S(1)} fusion(bf16[384,2048]{1,0:T(8,128)(2,1)S(1)} %collective-permute-done.12, bf16[128,2048]{1,0:T(8,128)(2,1)} %collective-permute-done.5), kind=kOutput, calls=%fused_computation.170 | convolution fusion | flops 201326592 | bytes 2293760 | tf_op jit(solution)/shard_map/behind/dot_general | solution.py:171
  88.9 1.7 %multiply_convert_fusion.5 = (bf16[384,128]{1,0:T(8,128)(2,1)S(1)}, bf16[384,128]{1,0:T(8,128)(2,1)S(1)}, f32[128]{0:T(128)S(1)}, bf16[384,128]{1,0:T(8,128)(2,1...) fusion(f32[768,128]{1,0:T(8,128)S(1)} %fusion.70, ...), kind=kOutput, calls=%fused_computation.80 | convolution fusion | flops 203194112 | bytes 3671552 | tf_op jit(solution)/shard_map/behind/dot_general | solution.py:171
  90.7 1.2 fusion.62
  91.9 1.5 %collective-permute-start.17 = (bf16[128,2048]{1,0:T(8,128)(2,1)S(1)}, bf16[128,2048]{1,0:T(8,128)(2,1)S(1)}, u32[]{:S(2)}, u32[]{:S(2)}) collective-permute-start(bf16[128,2048]{1,0:T(8,128)(2,1)S(1)} %fusion.2), channel_id=1, source_target_pairs={{0,1},{3,2},{4,5},{7,6},{8,9},{11,10},{12,13},{15,14},{16,17},{19,... | collective-permute-start | bytes 1572872 | tf_op jit(solution)/shard_map/r4/ppermute | solution.py:168
  93.4 1.2 fusion.3
  95.6 2.2 %convolution_convert_fusion.1 = bf16[384,2048]{1,0:T(8,128)(2,1)S(1)} fusion(bf16[128,2048]{1,0:T(8,128)(2,1)S(1)} %broadcast_select_fusion.1, bf16[128,2048]{1,0:T(8,128)(2,1)S(1)} %broadcast_select_fusion, bf16[128,2048]{1,0:T(8,128)(2,1)} %collective-permute-done.5, bf16[128,2048]{1,0:T(8,128)(2,1)} %bitcast.5, ...), kind=kOutput, calls=%fused_computation.4 | convolution fusion | flops 816054272 | bytes 4063232 | tf_op jit(solution)/shard_map/weight_grads/dot_general | solution.py:171
  97.9 2.9 %convolution_convert_fusion = bf16[2048,768]{1,0:T(8,128)(2,1)S(1)} fusion(bf16[128,2048]{1,0:T(8,128)(2,1)S(1)} %broadcast_select_fusion.2, bf16[128,2048]{1,0:T(8,128)(2,1)S(1)} %broadcast_select_fusion.3, bf16[128,2048]{1,0:T(8,128)(2,1)} %collective-permute-done.4, bf16[128,2048]{1,0:T(8,128)(2,1)S(1)} %bitcast.75, ...), kind=kOutput, calls=%fused_computation | convolution fusion | flops 1623719936 | bytes 6029312 | tf_op jit(solution)/shard_map/weight_grads/dot_general | solution.py:171
  100.8 3.2 %collective-permute-done.17 = bf16[128,2048]{1,0:T(8,128)(2,1)S(1)} collective-permute-done((bf16[128,2048]{1,0:T(8,128)(2,1)S(1)}, bf16[128,2048]{1,0:T(8,128)(2,1)S(1)}, u32[]{:S(2)}, u32[]{:S(2)}) %collective-permute-start.17) | collective-permute-done | bytes 524320 | tf_op jit(solution)/shard_map/r4/ppermute | solution.py:168
  104.9 4.9 %collective-permute-start.21 = (bf16[128,2048]{1,0:T(8,128)(2,1)S(1)}, bf16[128,2048]{1,0:T(8,128)(2,1)S(1)}, u32[]{:S(2)}, u32[]{:S(2)}) collective-permute-start(bf16[128,2048]{1,0:T(8,128)(2,1)S(1)} %add.182), channel_id=1, source_target_pairs={{0,1},{3,2},{1,0},{2,3},{4,5},{7,6},{5,4},{6,7},{8,9},{11,10},{9,8... | collective-permute-start | bytes 1572872 | tf_op jit(solution)/shard_map/r1/ppermute | solution.py:168
  110.4 1.8 %collective-permute-done.19 = bf16[384,2048]{1,0:T(8,128)(2,1)S(1)} collective-permute-done((bf16[384,2048]{1,0:T(8,128)(2,1)S(1)}, bf16[384,2048]{1,0:T(8,128)(2,1)S(1)}, u32[]{:S(2)}, u32[]{:S(2)}) %collective-permute-start.19) | collective-permute-done | bytes 1572896 | tf_op jit(solution)/shard_map/got_dn/ppermute | solution.py:168
  112.3 3.4 %add_convert_fusion.2 = bf16[384,2048]{1,0:T(8,128)(2,1)} fusion(bf16[384,2048]{1,0:T(8,128)(2,1)S(1)} %collective-permute-done.19, bf16[128,2048]{1,0:T(8,128)(2,1)S(1)} %broadcast_select_fusion.1, bf16[128,2048]{1,0:T(8,128)(2,1)S(1)} %broadcast_select_fusion, bf16[128,2048]{1,0:T(8,128)(2,1)} %collective-permute-done.5, bf16[128,2048]{1,0:T(8,128)(2,1)} %bitcast.5, ...), kind=kOutput, calls=%fused_computation.3 | convolution fusion | flops 817627136 | bytes 5636096 | tf_op jit(solution)/shard_map/weight_grads/dot_general | solution.py:171
  115.6 6.3 %collective-permute-done.21 = bf16[128,2048]{1,0:T(8,128)(2,1)S(1)} collective-permute-done((bf16[128,2048]{1,0:T(8,128)(2,1)S(1)}, bf16[128,2048]{1,0:T(8,128)(2,1)S(1)}, u32[]{:S(2)}, u32[]{:S(2)}) %collective-permute-start.21) | collective-permute-done | bytes 524320 | tf_op jit(solution)/shard_map/r1/ppermute | solution.py:168
  122.1 2.5 %collective-permute-start.23 = (bf16[128,2048]{1,0:T(8,128)(2,1)S(1)}, bf16[128,2048]{1,0:T(8,128)(2,1)S(1)}, u32[]{:S(2)}, u32[]{:S(2)}) collective-permute-start(bf16[128,2048]{1,0:T(8,128)(2,1)S(1)} %add_convert_fusion.3), channel_id=1, source_target_pairs={{0,24},{8,0},{16,8},{24,16},{1,25},{9,1},{17,9},{25,17},{2,26},{10... | collective-permute-start | bytes 1572872 | tf_op jit(solution)/shard_map/up/ppermute | solution.py:168
  126.1 2.5 %add_convert_fusion.1 = bf16[2048,384]{1,0:T(8,128)(2,1)} fusion(bf16[512,2048]{1,0:T(8,128)(2,1)S(1)} %constant_dynamic-update-slice_fusion.4, bf16[2048,768]{1,0:T(8,128)(2,1)S(1)} %collective-permute-done.20, bf16[768,512]{1,0:T(8,128)(2,1)S(1)} %constant_dynamic-update-slice_fusion.8), kind=kOutput, calls=%fused_computation.2 | convolution fusion | flops 807665664 | bytes 5636096 | tf_op jit(solution)/shard_map/weight_grads/dot_general | solution.py:171
  128.6 2.5 %add_convert_fusion = bf16[2048,384]{1,0:T(8,128)(2,1)} fusion(bf16[512,2048]{1,0:T(8,128)(2,1)S(1)} %constant_dynamic-update-slice_fusion.4, bf16[2048,768]{1,0:T(8,128)(2,1)S(1)} %collective-permute-done.20, bf16[768,512]{1,0:T(8,128)(2,1)S(1)} %constant_dynamic-update-slice_fusion.8), kind=kOutput, calls=%fused_computation.1 | convolution fusion | flops 807665664 | bytes 5636096 | tf_op jit(solution)/shard_map/weight_grads/dot_general | solution.py:171
  131.1 2.5 %collective-permute-start.26 = (f32[1,128]{1,0:T(1,128)S(1)}, f32[1,128]{1,0:T(1,128)S(1)}, u32[]{:S(2)}, u32[]{:S(2)}) collective-permute-start(f32[1,128]{1,0:T(1,128)S(1)} %add_bitcast_fusion.2), channel_id=1, source_target_pairs={{0,3},{1,2},{2,1},{3,0},{4,7},{5,6},{6,5},{7,4},{8,11},{9,10},{10,... | collective-permute-start | bytes 1544 | tf_op jit(solution)/shard_map/dot/ppermute | solution.py:168
  133.6 2.6 %collective-permute-start.25 = (f32[1,128]{1,0:T(1,128)S(1)}, f32[1,128]{1,0:T(1,128)S(1)}, u32[]{:S(2)}, u32[]{:S(2)}) collective-permute-start(f32[1,128]{1,0:T(1,128)S(1)} %add_bitcast_fusion.1), channel_id=1, source_target_pairs={{0,2},{1,3},{2,0},{3,1},{4,6},{5,7},{6,4},{7,5},{8,10},{9,11},{10,... | collective-permute-start | bytes 1544 | tf_op jit(solution)/shard_map/dot/ppermute | solution.py:168
  136.5 1.6 %collective-permute-done.25 = f32[1,128]{1,0:T(1,128)S(1)} collective-permute-done((f32[1,128]{1,0:T(1,128)S(1)}, f32[1,128]{1,0:T(1,128)S(1)}, u32[]{:S(2)}, u32[]{:S(2)}) %collective-permute-start.25) | collective-permute-done | bytes 544 | tf_op jit(solution)/shard_map/dot/ppermute | solution.py:168
  138.0 1.7 %collective-permute-done.24 = f32[1,128]{1,0:T(1,128)S(1)} collective-permute-done((f32[1,128]{1,0:T(1,128)S(1)}, f32[1,128]{1,0:T(1,128)S(1)}, u32[]{:S(2)}, u32[]{:S(2)}) %collective-permute-start.24) | collective-permute-done | bytes 544 | tf_op jit(solution)/shard_map/dot/ppermute | solution.py:168
  (77 shorter events, 20.1 us)
Async XLA Ops:
  1.4 13.5 %copy-start = (bf16[1,128,2048]{2,1,0:T(8,128)(2,1)S(1)}, bf16[1,128,2048]{2,1,0:T(8,128)(2,1)}, u32[]{:S(2)}) copy-start(bf16[1,128,2048]{2,1,0:T(8,128)(2,1)} %param.7) | copy-start | bytes 1572868
  1.4 19.6 %collective-permute-start.3 = (bf16[128,2048]{1,0:T(8,128)(2,1)}, bf16[128,2048]{1,0:T(8,128)(2,1)}, u32[]{:S(2)}, u32[]{:S(2)}) collective-permute-start(bf16[128,2048]{1,0:T(8,128)(2,1)} %bitcast.71), channel_id=1, source_target_pairs={{1,2},{2,1},{5,6},{6,5},{9,10},{10,9},{13,14},{14,13},{17,18},{18,... | collective-permute-start | bytes 1572872 | tf_op jit(solution)/shard_map/t_mid_in/ppermute | solution.py:168
  3.0 18.0 %collective-permute-start.4 = (bf16[128,2048]{1,0:T(8,128)(2,1)}, bf16[128,2048]{1,0:T(8,128)(2,1)}, u32[]{:S(2)}, u32[]{:S(2)}) collective-permute-start(bf16[128,2048]{1,0:T(8,128)(2,1)} %bitcast.72), channel_id=1, source_target_pairs={{0,1},{3,2},{1,0},{2,3},{4,5},{7,6},{5,4},{6,7},{8,9},{11,10},{9,8... | collective-permute-start | bytes 1572872 | tf_op jit(solution)/shard_map/t_near/ppermute | solution.py:168
  8.1 11.6 %collective-permute-start = (f32[1,128]{1,0:T(1,128)S(1)}, f32[1,128]{1,0:T(1,128)S(1)}, u32[]{:S(2)}, u32[]{:S(2)}) collective-permute-start(f32[1,128]{1,0:T(1,128)S(1)} %bitcast.81), channel_id=1, source_target_pairs={{0,2},{1,3},{2,0},{3,1},{4,6},{5,7},{6,4},{7,5},{8,10},{9,11},{10,... | collective-permute-start | bytes 1544 | tf_op jit(solution)/shard_map/p/ppermute | solution.py:168
  8.6 12.4 %collective-permute-start.1 = (f32[1,128]{1,0:T(1,128)S(1)}, f32[1,128]{1,0:T(1,128)S(1)}, u32[]{:S(2)}, u32[]{:S(2)}) collective-permute-start(f32[1,128]{1,0:T(1,128)S(1)} %bitcast.80), channel_id=1, source_target_pairs={{0,3},{1,2},{2,1},{3,0},{4,7},{5,6},{6,5},{7,4},{8,11},{9,10},{10,... | collective-permute-start | bytes 1544 | tf_op jit(solution)/shard_map/p/ppermute | solution.py:168
  10.5 10.5 %collective-permute-start.2 = (f32[1,128]{1,0:T(1,128)S(1)}, f32[1,128]{1,0:T(1,128)S(1)}, u32[]{:S(2)}, u32[]{:S(2)}) collective-permute-start(f32[1,128]{1,0:T(1,128)S(1)} %bitcast.79), channel_id=1, source_target_pairs={{0,1},{1,0},{2,3},{3,2},{4,5},{5,4},{6,7},{7,6},{8,9},{9,8},{10,11... | collective-permute-start | bytes 1544 | tf_op jit(solution)/shard_map/p/ppermute | solution.py:168
  21.0 15.7 %collective-permute-start.6 = (bf16[2048,384]{1,0:T(8,128)(2,1)}, bf16[2048,384]{1,0:T(8,128)(2,1)}, u32[]{:S(2)}, u32[]{:S(2)}) collective-permute-start(bf16[2048,384]{1,0:T(8,128)(2,1)} %bitcast.4), channel_id=1, source_target_pairs={{0,4},{4,0},{1,5},{5,1},{2,6},{6,2},{3,7},{7,3},{8,12},{12,8},{9,1... | collective-permute-start | bytes 4718600 | tf_op jit(solution)/shard_map/sib_g/ppermute | solution.py:168
  21.1 15.6 %collective-permute-start.7 = (bf16[2048,384]{1,0:T(8,128)(2,1)}, bf16[2048,384]{1,0:T(8,128)(2,1)}, u32[]{:S(2)}, u32[]{:S(2)}) collective-permute-start(bf16[2048,384]{1,0:T(8,128)(2,1)} %bitcast.8), channel_id=1, source_target_pairs={{0,4},{4,0},{1,5},{5,1},{2,6},{6,2},{3,7},{7,3},{8,12},{12,8},{9,1... | collective-permute-start | bytes 4718600 | tf_op jit(solution)/shard_map/sib_u/ppermute | solution.py:168
  21.6 15.1 %collective-permute-start.5 = (bf16[128,2048]{1,0:T(8,128)(2,1)}, bf16[128,2048]{1,0:T(8,128)(2,1)}, u32[]{:S(2)}, u32[]{:S(2)}) collective-permute-start(bf16[128,2048]{1,0:T(8,128)(2,1)} %bitcast.5), channel_id=1, source_target_pairs={{0,1},{3,2},{1,0},{2,3},{4,5},{7,6},{5,4},{6,7},{8,9},{11,10},{9,8... | collective-permute-start | bytes 1572872 | tf_op jit(solution)/shard_map/g_near/ppermute | solution.py:168
  22.3 14.4 %collective-permute-start.8 = (bf16[128,2048]{1,0:T(8,128)(2,1)}, bf16[128,2048]{1,0:T(8,128)(2,1)}, u32[]{:S(2)}, u32[]{:S(2)}) collective-permute-start(bf16[128,2048]{1,0:T(8,128)(2,1)} %collective-permute-done.4), channel_id=1, source_target_pairs={{1,2},{2,1},{5,6},{6,5},{9,10},{10,9},{13,14},{14,13},{17,18},{18,... | collective-permute-start | bytes 1572872 | tf_op jit(solution)/shard_map/t_far_in/ppermute | solution.py:168
  23.8 15.9 %copy-start.3 = (bf16[1,1,384,2048]{3,2,1,0:T(8,128)(2,1)S(1)}, bf16[1,1,384,2048]{3,2,1,0:T(8,128)(2,1)}, u32[]{:S(2)}) copy-start(bf16[1,1,384,2048]{3,2,1,0:T(8,128)(2,1)} %param.13) | copy-start | bytes 4718596
  23.8 19.0 %copy-start.1 = (bf16[1,128,2048]{2,1,0:T(8,128)(2,1)S(1)}, bf16[1,128,2048]{2,1,0:T(8,128)(2,1)}, u32[]{:S(2)}) copy-start(bf16[1,128,2048]{2,1,0:T(8,128)(2,1)} %param.7) | copy-start | bytes 1572868
  23.8 23.2 %collective-permute-start.10 = (bf16[128,2048]{1,0:T(8,128)(2,1)}, bf16[128,2048]{1,0:T(8,128)(2,1)S(1)}, u32[]{:S(2)}, u32[]{:S(2)}) collective-permute-start(bf16[128,2048]{1,0:T(8,128)(2,1)} %collective-permute-done.3), channel_id=1, source_target_pairs={{1,0},{2,3},{5,4},{6,7},{9,8},{10,11},{13,12},{14,15},{17,16},{18,... | collective-permute-start | bytes 1572872 | tf_op jit(solution)/shard_map/t_mid_out/ppermute | solution.py:168
  38.3 8.7 %collective-permute-start.9 = (bf16[128,2048]{1,0:T(8,128)(2,1)}, bf16[128,2048]{1,0:T(8,128)(2,1)S(1)}, u32[]{:S(2)}, u32[]{:S(2)}) collective-permute-start(bf16[128,2048]{1,0:T(8,128)(2,1)} %collective-permute-done.5), channel_id=1, source_target_pairs={{1,2},{2,1},{5,6},{6,5},{9,10},{10,9},{13,14},{14,13},{17,18},{18,... | collective-permute-start | bytes 1572872 | tf_op jit(solution)/shard_map/g_far_in/ppermute | solution.py:168
  39.0 15.5 %collective-permute-start.11 = (bf16[128,2048]{1,0:T(8,128)(2,1)}, bf16[128,2048]{1,0:T(8,128)(2,1)S(1)}, u32[]{:S(2)}, u32[]{:S(2)}) collective-permute-start(bf16[128,2048]{1,0:T(8,128)(2,1)} %bitcast.5), channel_id=1, source_target_pairs={{1,2},{2,1},{5,6},{6,5},{9,10},{10,9},{13,14},{14,13},{17,18},{18,... | collective-permute-start | bytes 1572872 | tf_op jit(solution)/shard_map/g_mid_in/ppermute | solution.py:168
  39.7 21.6 %collective-permute-start.12 = (bf16[384,2048]{1,0:T(8,128)(2,1)S(1)}, bf16[384,2048]{1,0:T(8,128)(2,1)S(1)}, u32[]{:S(2)}, u32[]{:S(2)}) collective-permute-start(bf16[384,2048]{1,0:T(8,128)(2,1)S(1)} %bitcast.85), channel_id=1, source_target_pairs={{0,4},{4,0},{1,5},{5,1},{2,6},{6,2},{3,7},{7,3},{8,12},{12,8},{9,1... | collective-permute-start | bytes 4718600 | tf_op jit(solution)/shard_map/sib_d/ppermute | solution.py:168
  39.8 21.5 %collective-permute-start.13 = (bf16[128,2048]{1,0:T(8,128)(2,1)}, bf16[128,2048]{1,0:T(8,128)(2,1)S(1)}, u32[]{:S(2)}, u32[]{:S(2)}) collective-permute-start(bf16[128,2048]{1,0:T(8,128)(2,1)} %collective-permute-done.8), channel_id=1, source_target_pairs={{1,0},{2,3},{5,4},{6,7},{9,8},{10,11},{13,12},{14,15},{17,16},{18,... | collective-permute-start | bytes 1572872 | tf_op jit(solution)/shard_map/t_far_out/ppermute | solution.py:168
  46.9 25.5 %collective-permute-start.14 = (bf16[128,2048]{1,0:T(8,128)(2,1)S(1)}, bf16[128,2048]{1,0:T(8,128)(2,1)S(1)}, u32[]{:S(2)}, u32[]{:S(2)}) collective-permute-start(bf16[128,2048]{1,0:T(8,128)(2,1)S(1)} %collective-permute-done.9), channel_id=1, source_target_pairs={{1,0},{2,3},{5,4},{6,7},{9,8},{10,11},{13,12},{14,15},{17,16},{18,... | collective-permute-start | bytes 1572872 | tf_op jit(solution)/shard_map/g_far_out/ppermute | solution.py:168
  63.3 20.2 %collective-permute-start.15 = (bf16[128,2048]{1,0:T(8,128)(2,1)S(1)}, bf16[128,2048]{1,0:T(8,128)(2,1)S(1)}, u32[]{:S(2)}, u32[]{:S(2)}) collective-permute-start(bf16[128,2048]{1,0:T(8,128)(2,1)S(1)} %collective-permute-done.11), channel_id=1, source_target_pairs={{1,0},{2,3},{5,4},{6,7},{9,8},{10,11},{13,12},{14,15},{17,16},{18,... | collective-permute-start | bytes 1572872 | tf_op jit(solution)/shard_map/g_mid_out/ppermute | solution.py:168
  76.3 18.3 %collective-permute-start.16 = (bf16[128,2048]{1,0:T(8,128)(2,1)S(1)}, bf16[128,2048]{1,0:T(8,128)(2,1)S(1)}, u32[]{:S(2)}, u32[]{:S(2)}) collective-permute-start(bf16[128,2048]{1,0:T(8,128)(2,1)S(1)} %fusion.1), channel_id=1, source_target_pairs={{0,1},{3,2},{4,5},{7,6},{8,9},{11,10},{12,13},{15,14},{16,17},{19,... | collective-permute-start | bytes 1572872 | tf_op jit(solution)/shard_map/r5/ppermute | solution.py:168
  91.9 12.1 %collective-permute-start.17 = (bf16[128,2048]{1,0:T(8,128)(2,1)S(1)}, bf16[128,2048]{1,0:T(8,128)(2,1)S(1)}, u32[]{:S(2)}, u32[]{:S(2)}) collective-permute-start(bf16[128,2048]{1,0:T(8,128)(2,1)S(1)} %fusion.2), channel_id=1, source_target_pairs={{0,1},{3,2},{4,5},{7,6},{8,9},{11,10},{12,13},{15,14},{16,17},{19,... | collective-permute-start | bytes 1572872 | tf_op jit(solution)/shard_map/r4/ppermute | solution.py:168
  94.7 9.4 %collective-permute-start.18 = (bf16[128,2048]{1,0:T(8,128)(2,1)S(1)}, bf16[128,2048]{1,0:T(8,128)(2,1)S(1)}, u32[]{:S(2)}, u32[]{:S(2)}) collective-permute-start(bf16[128,2048]{1,0:T(8,128)(2,1)S(1)} %add.180), channel_id=1, source_target_pairs={{1,2},{2,1},{5,6},{6,5},{9,10},{10,9},{13,14},{14,13},{17,18},{18,... | collective-permute-start | bytes 1572872 | tf_op jit(solution)/shard_map/r3/ppermute | solution.py:168
  104.3 8.0 %collective-permute-start.20 = (bf16[2048,768]{1,0:T(8,128)(2,1)S(1)}, bf16[2048,768]{1,0:T(8,128)(2,1)S(1)}, u32[]{:S(2)}, u32[]{:S(2)}) collective-permute-start(bf16[2048,768]{1,0:T(8,128)(2,1)S(1)} %convolution_convert_fusion), channel_id=1, source_target_pairs={{0,4},{4,0},{1,5},{5,1},{2,6},{6,2},{3,7},{7,3},{8,12},{12,8},{9,1... | collective-permute-start | bytes 9437192 | tf_op jit(solution)/shard_map/got_gu/ppermute | solution.py:168
  104.4 7.9 %collective-permute-start.19 = (bf16[384,2048]{1,0:T(8,128)(2,1)S(1)}, bf16[384,2048]{1,0:T(8,128)(2,1)S(1)}, u32[]{:S(2)}, u32[]{:S(2)}) collective-permute-start(bf16[384,2048]{1,0:T(8,128)(2,1)S(1)} %convolution_convert_fusion.1), channel_id=1, source_target_pairs={{0,4},{4,0},{1,5},{5,1},{2,6},{6,2},{3,7},{7,3},{8,12},{12,8},{9,1... | collective-permute-start | bytes 4718600 | tf_op jit(solution)/shard_map/got_dn/ppermute | solution.py:168
  104.9 17.0 %collective-permute-start.21 = (bf16[128,2048]{1,0:T(8,128)(2,1)S(1)}, bf16[128,2048]{1,0:T(8,128)(2,1)S(1)}, u32[]{:S(2)}, u32[]{:S(2)}) collective-permute-start(bf16[128,2048]{1,0:T(8,128)(2,1)S(1)} %add.182), channel_id=1, source_target_pairs={{0,1},{3,2},{1,0},{2,3},{4,5},{7,6},{5,4},{6,7},{8,9},{11,10},{9,8... | collective-permute-start | bytes 1572872 | tf_op jit(solution)/shard_map/r1/ppermute | solution.py:168
  109.7 12.2 %collective-permute-start.22 = (bf16[128,2048]{1,0:T(8,128)(2,1)S(1)}, bf16[128,2048]{1,0:T(8,128)(2,1)S(1)}, u32[]{:S(2)}, u32[]{:S(2)}) collective-permute-start(bf16[128,2048]{1,0:T(8,128)(2,1)S(1)} %add.181), channel_id=1, source_target_pairs={{1,2},{2,1},{5,6},{6,5},{9,10},{10,9},{13,14},{14,13},{17,18},{18,... | collective-permute-start | bytes 1572872 | tf_op jit(solution)/shard_map/r2/ppermute | solution.py:168
  122.1 18.2 %collective-permute-start.23 = (bf16[128,2048]{1,0:T(8,128)(2,1)S(1)}, bf16[128,2048]{1,0:T(8,128)(2,1)S(1)}, u32[]{:S(2)}, u32[]{:S(2)}) collective-permute-start(bf16[128,2048]{1,0:T(8,128)(2,1)S(1)} %add_convert_fusion.3), channel_id=1, source_target_pairs={{0,24},{8,0},{16,8},{24,16},{1,25},{9,1},{17,9},{25,17},{2,26},{10... | collective-permute-start | bytes 1572872 | tf_op jit(solution)/shard_map/up/ppermute | solution.py:168
  128.6 11.1 %copy-start.2 = (s32[1,128,2]{1,2,0:T(2,128)S(1)}, s32[1,128,2]{1,2,0:T(2,128)}, u32[]{:S(2)}) copy-start(s32[1,128,2]{1,2,0:T(2,128)} %param.9) | copy-start | bytes 3076
  131.1 5.3 %collective-permute-start.26 = (f32[1,128]{1,0:T(1,128)S(1)}, f32[1,128]{1,0:T(1,128)S(1)}, u32[]{:S(2)}, u32[]{:S(2)}) collective-permute-start(f32[1,128]{1,0:T(1,128)S(1)} %add_bitcast_fusion.2), channel_id=1, source_target_pairs={{0,3},{1,2},{2,1},{3,0},{4,7},{5,6},{6,5},{7,4},{8,11},{9,10},{10,... | collective-permute-start | bytes 1544 | tf_op jit(solution)/shard_map/dot/ppermute | solution.py:168
  133.6 4.4 %collective-permute-start.25 = (f32[1,128]{1,0:T(1,128)S(1)}, f32[1,128]{1,0:T(1,128)S(1)}, u32[]{:S(2)}, u32[]{:S(2)}) collective-permute-start(f32[1,128]{1,0:T(1,128)S(1)} %add_bitcast_fusion.1), channel_id=1, source_target_pairs={{0,2},{1,3},{2,0},{3,1},{4,6},{5,7},{6,4},{7,5},{8,10},{9,11},{10,... | collective-permute-start | bytes 1544 | tf_op jit(solution)/shard_map/dot/ppermute | solution.py:168
  136.2 3.5 %collective-permute-start.24 = (f32[1,128]{1,0:T(1,128)S(1)}, f32[1,128]{1,0:T(1,128)S(1)}, u32[]{:S(2)}, u32[]{:S(2)}) collective-permute-start(f32[1,128]{1,0:T(1,128)S(1)} %add_bitcast_fusion), channel_id=1, source_target_pairs={{0,1},{1,0},{2,3},{3,2},{4,5},{5,4},{6,7},{7,6},{8,9},{9,8},{10,11... | collective-permute-start | bytes 1544 | tf_op jit(solution)/shard_map/dot/ppermute | solution.py:168

commit v3 on v2

--- a/solution.py
+++ b/solution.py
@@ -1,6 +1,10 @@
+import functools
+
 import jax
 import jax.numpy as jnp
 from jax import lax
+from jax.experimental import pallas as pl
+from jax.experimental.pallas import tpu as pltpu
 from jax.sharding import PartitionSpec as P
 
 
@@ -156,10 +160,38 @@
 F32, BF16 = jnp.float32, jnp.bfloat16
 
 
+def gather_kernel(places, *refs):
+    count = len(places)
+    sources, outs, sems = refs[:count], refs[count:-1], refs[-1]
+    copies = []
+    for i, (source, (out, rows, cols)) in enumerate(zip(sources, places)):
+        target = outs[out].at[pl.ds(rows, source.shape[0]), pl.ds(cols, source.shape[1])]
+        copies.append(pltpu.make_async_copy(source, target, sems.at[i]))
+    for copy in copies:
+        copy.start()
+    for copy in copies:
+        copy.wait()
+
+
+def gather(name, shapes, *pieces):
+    anywhere = pl.BlockSpec(memory_space=pl.ANY)
+    return pl.pallas_call(
+        functools.partial(gather_kernel, [piece[1:] for piece in pieces]),
+        out_shape=[jax.ShapeDtypeStruct(dims, pieces[0][0].dtype) for dims in shapes],
+        in_specs=[anywhere] * len(pieces),
+        out_specs=[pl.BlockSpec(memory_space=pltpu.VMEM)] * len(shapes),
+        scratch_shapes=[pltpu.SemaphoreType.DMA((len(pieces),))],
+        compiler_params=pltpu.CompilerParams(vmem_limit_bytes=16 << 20),
+        cost_estimate=pl.CostEstimate(flops=0, bytes_accessed=1 << 20, transcendentals=0),
+        name=name,
+    )(*(piece[0] for piece in pieces))
+
+
 def line_plan(tokens, out_grad, expert_ids, route_probs, gate_weight, up_weight, down_weight):
     place = lax.axis_index("expert")
     inner = (place == 1) | (place == 2)
     tok, grd = tokens[0], out_grad[0]
+    width = tok.shape[1]
     ids, probs = expert_ids[0], route_probs[0]
     half = gate_weight.shape[3]
 
@@ -182,6 +214,14 @@
         v.update(ready)
         v.update(lax.optimization_barrier(v))
 
+    def drop(*names):
+        for name in names:
+            del v[name]
+
+    def rows_of(x, c):
+        part = x.shape[0] // 2
+        return x[c * part : (c + 1) * part]
+
     def ahead(rows, w):
         with jax.named_scope("ahead"):
             return mm(w, rows, ((0,), (1,)))
@@ -192,13 +232,14 @@
     def behind(grads, parts, p):
         with jax.named_scope("behind"):
             dots, halves, dx = 0.0, [], 0.0
-            for pre, d, w in zip(parts, (v["own_d"], v["sib_d"]), (v["own_w"], v["sib_w"])):
+            both_hidden = mm(v["all_d"], grads, ((1,), (1,)))
+            for side, (pre, w) in enumerate(zip(parts, (v["own_w"], v["sib_w"]))):
                 gate, up = pre[:half], pre[half:]
                 sig = jax.nn.sigmoid(gate)
                 silu = gate * sig
                 act = silu * up
                 by_gate = up * sig * (1.0 + gate * (1.0 - sig))
-                hidden = mm(d, grads, ((1,), (1,)))
+                hidden = both_hidden[side * half :][:half]
                 dots = dots + jnp.sum(act * hidden, axis=0, keepdims=True)
                 scaled = p * hidden
                 both = jnp.concatenate([scaled * by_gate, scaled * silu], axis=0).astype(BF16)
@@ -209,9 +250,6 @@
     columns = [
         jnp.sum(jnp.where(ids == (place ^ k), probs, 0.0), axis=1).reshape(1, -1) for k in range(4)
     ]
-    def tick():
-        return over(v["columns"][0], SWAP, "tick", "dp")
-
     sync(columns=columns)
     t_near = over(v["tok"], PAIRS, "t_near")
     t_mid_in = over(v["tok"], MIDDLE, "t_mid_in")
@@ -220,102 +258,117 @@
     a_own = ahead(v["tok"], own_w)
     sync(own_w=own_w, a_own=a_own)
 
-    sync(t_near=t_near, t_mid_in=t_mid_in, p_near=p_near, p_cross=p_cross, p_flip=p_flip, tick=tick())
+    sync(t_near=t_near, t_mid_in=t_mid_in, p_near=p_near, p_cross=p_cross, p_flip=p_flip)
     g_near = over(v["grd"], PAIRS, "g_near")
     t_mid_out = over(v["t_mid_in"], OUTWARD, "t_mid_out")
     t_far_in = over(v["t_near"], MIDDLE, "t_far_in")
-    sib_g = over(v["gate"], SWAP, "sib_g", "dp")
-    sib_u = over(v["up"], SWAP, "sib_u", "dp")
-
-    sync(g_near=g_near, t_far_in=t_far_in, sib_g=sib_g, sib_u=sib_u)
+    sib_w = over(v["own_w"], SWAP, "sib_w", "dp")
+    sib_d = over(v["own_d"], SWAP, "sib_d", "dp")
+
+    sync(g_near=g_near, t_far_in=t_far_in, sib_w=sib_w, sib_d=sib_d)
     g_far_in = over(v["g_near"], MIDDLE, "g_far_in")
     t_far_out = over(v["t_far_in"], OUTWARD, "t_far_out")
     g_mid_in = over(v["grd"], MIDDLE, "g_mid_in")
-    sib_d = over(v["own_d"], SWAP, "sib_d", "dp")
-    sib_w = jnp.concatenate([v["sib_g"], v["sib_u"]], axis=1)
-    for name in ("gate", "up", "sib_g", "sib_u"):
-        del v[name]
+    sib_w, all_d = gather(
+        "sib_w",
+        [(width, 2 * half), (2 * half, width)],
+        (v["sib_w"], 0, 0, 0),
+        (v["own_d"], 1, 0, 0),
+        (v["sib_d"], 1, half, 0),
+    )
+    drop("gate", "up", "own_d", "sib_d")
     a_own = [v["a_own"], ahead(v["tok"], sib_w)]
-    sync(a_own=a_own, sib_w=sib_w)
-
-    sync(t_mid_out=t_mid_out, g_far_in=g_far_in, tick=tick())
+    sync(a_own=a_own, sib_w=sib_w, all_d=all_d)
+
+    sync(t_mid_out=t_mid_out, g_far_in=g_far_in)
     g_far_out = over(v["g_far_in"], OUTWARD, "g_far_out")
     t_cross = pick(v["t_far_in"], v["t_mid_out"])
     a_near, a_cross = ahead_both(v["t_near"]), ahead_both(t_cross)
-    sync(t_cross=t_cross, a_cross=a_cross, a_near=a_near)
-
-    sync(t_far_out=t_far_out, g_mid_in=g_mid_in, sib_d=sib_d, tick=tick())
+    dx_own, k_own = behind(v["grd"], v["a_own"], v["columns"][0])
+    drop("t_far_in", "t_mid_out", "a_own")
+    sync(t_cross=t_cross, a_cross=a_cross, a_near=a_near, dx_own=dx_own, k_own=k_own)
+
+    sync(t_far_out=t_far_out, g_mid_in=g_mid_in)
     g_mid_out = over(v["g_mid_in"], OUTWARD, "g_mid_out")
     t_flip = pick(v["t_mid_in"], v["t_far_out"])
     a_flip = ahead_both(t_flip)
-    dx_own, k_own = behind(v["grd"], v["a_own"], v["columns"][0])
-    sync(t_flip=t_flip, a_flip=a_flip, dx_own=dx_own, k_own=k_own)
-    sync(tick=tick())
+    dx_near, k_near = behind(v["g_near"], v["a_near"], v["p_near"])
+    drop("t_mid_in", "t_far_out", "a_near", "p_near")
+    sync(t_flip=t_flip, a_flip=a_flip, dx_near=dx_near, k_near=k_near)
 
     sync(g_far_out=g_far_out)
     g_flip = pick(v["g_mid_in"], v["g_far_out"])
     dx_flip, k_flip = behind(g_flip, v["a_flip"], v["p_flip"])
+    drop("g_mid_in", "g_far_out", "a_flip", "p_flip")
     sync(g_flip=g_flip, dx_flip=dx_flip, k_flip=k_flip)
     r5 = over(v["dx_flip"], INWARD, "r5")
 
     sync(g_mid_out=g_mid_out)
     g_cross = pick(v["g_far_in"], v["g_mid_out"])
     dx_cross, k_cross = behind(g_cross, v["a_cross"], v["p_cross"])
+    drop("g_far_in", "g_mid_out", "a_cross", "p_cross")
     sync(g_cross=g_cross, dx_cross=dx_cross, k_cross=k_cross)
     r4 = over(v["dx_cross"], INWARD, "r4")
-    dx_near, k_near = behind(v["g_near"], v["a_near"], v["p_near"])
-    sync(dx_near=dx_near, k_near=k_near)
-
-    sync(r5=r5, tick=tick())
+    order = ("tok", "t_near", "t_cross", "t_flip")
+    rows = jnp.concatenate([v[name].T for name in order], axis=1)
+    grads = jnp.concatenate([v[name] for name in ("grd", "g_near", "g_cross", "g_flip")], axis=0)
+    drop(*order, "grd", "g_near", "g_cross", "g_flip")
+    sync(rows=rows, grads=grads)
+
+    sync(r5=r5)
     back = v["dx_cross"] + v["r5"]
+    drop("dx_cross", "r5")
     sync(back=back)
     r3 = over(v["back"], MIDDLE, "r3")
-
-    def kept(which, side):
-        slots = [v["k_" + name][1][side][which] for name in ("own", "near", "cross", "flip")]
+    drop("own_w", "sib_w", "all_d", "back")
+
+    def kept(which, side, first=0, last=None):
+        slots = [v["k_" + name][1][side][which][first:last] for name in ("own", "near", "cross", "flip")]
         return jnp.concatenate(slots, axis=1)
 
-    def all_rows():
-        return jnp.concatenate([v["tok"], v["t_near"], v["t_cross"], v["t_flip"]], axis=0)
-
-    def all_grads():
-        return jnp.concatenate([v["grd"], v["g_near"], v["g_cross"], v["g_flip"]], axis=0)
-
     with jax.named_scope("weight_grads"):
-        sib_gu = mm(all_rows(), kept(0, 1), ((0,), (1,))).astype(BF16)
-        sib_dn = mm(kept(1, 1), all_grads(), ((1,), (0,))).astype(BF16)
+        sib_gu = mm(v["rows"], kept(0, 1), ((1,), (1,))).astype(BF16)
+        sib_dn = mm(kept(1, 1), v["grads"], ((1,), (0,))).astype(BF16)
     sync(sib_gu=sib_gu, sib_dn=sib_dn)
 
-    sync(r4=r4, tick=tick())
+    sync(r4=r4)
     back = v["dx_flip"] + v["r4"]
+    drop("dx_flip", "r4")
     sync(back=back)
     r2 = over(v["back"], MIDDLE, "r2")
 
     sync(r3=r3)
-    back = v["dx_near"] + v["r3"]
+    back = [rows_of(v["dx_near"], c) + rows_of(v["r3"], c) for c in range(2)]
+    drop("dx_near", "r3")
     sync(back=back)
-    r1 = over(v["back"], PAIRS, "r1")
+    r1 = [over(x, PAIRS, "r1") for x in v["back"]]
+    dots = [small(v["k_" + name][0], k, "dot") for k, name in ((2, "cross"), (3, "flip"))]
+    with jax.named_scope("weight_grads"):
+        own_gu = mm(v["rows"], kept(0, 0), ((1,), (1,))).astype(BF16)
+        own_dn = mm(kept(1, 0), v["grads"], ((1,), (0,))).astype(BF16)
+    sync(own_gu=own_gu, own_dn=own_dn)
+
+
+    def section_hop(r1, c):
+        n = lax.axis_size("section")
+        parts = (v["dx_own"], v["r2"])
+        total = sum(rows_of(x, c).astype(F32) for x in parts) + r1.astype(F32)
+        sync(total=total.astype(BF16))
+        return over(v["total"], [(i, (i - 1) % n) for i in range(n)], "up", "section")
+
+    sync(r2=r2, r1a=r1[0], dots=dots)
+    up_a = section_hop(v["r1a"], 0)
+    sync(r1b=r1[1])
+    up_b = section_hop(v["r1b"], 1)
     got_gu = over(v["sib_gu"], SWAP, "got_gu", "dp")
     got_dn = over(v["sib_dn"], SWAP, "got_dn", "dp")
-
+    upstream = jnp.concatenate([up_a, up_b], axis=0)
     sync(got_dn=got_dn, got_gu=got_gu)
-    with jax.named_scope("weight_grads"):
-        own_n = mm(kept(1, 0), all_grads(), ((1,), (0,))) + v["got_dn"].astype(F32)
-    sync(own_n=own_n.astype(BF16))
-
-    sync(r2=r2, r1=r1, tick=tick())
-    n = lax.axis_size("section")
-    total = v["dx_own"].astype(F32) + v["r1"].astype(F32) + v["r2"].astype(F32)
-    sync(total=total.astype(BF16))
-    upstream = over(v["total"], [(i, (i - 1) % n) for i in range(n)], "up", "section")
-    with jax.named_scope("weight_grads"):
-        hs = kept(0, 0)
-        own_g = mm(all_rows(), hs[:half], ((0,), (1,))) + v["got_gu"][:, :half].astype(F32)
-        own_u = mm(all_rows(), hs[half:], ((0,), (1,))) + v["got_gu"][:, half:].astype(F32)
-    sync(own_g=own_g.astype(BF16), own_u=own_u.astype(BF16))
-    dots = [v["k_own"][0]] + [
-        small(v["k_" + name][0], k, "dot") for k, name in ((1, "near"), (2, "cross"), (3, "flip"))
-    ]
+    own_n = v["own_dn"] + v["got_dn"]
+    own_g = v["own_gu"][:, :half] + v["got_gu"][:, :half]
+    own_u = v["own_gu"][:, half:] + v["got_gu"][:, half:]
+    sync(own_g=own_g, own_u=own_u, own_n=own_n)
+    dots = [v["k_own"][0], small(v["k_near"][0], 1, "dot")] + v["dots"]
     prob_grad = sum(
         jnp.where(ids == (place ^ k), d.reshape(-1, 1), 0.0) for k, d in enumerate(dots)
     )

time: 142 us -> 135 us (0.951)
  matrix products: 42.5 us -> 28.3 us
  other arithmetic: 2.28 us -> 11 us
  local copies, waits for them, and re-layouts: 8.77 us -> 6.61 us
    dot_general x29 -> x24, matrix products: 42.5 us -> 28.3 us  [mm(): return lax.dot_general(a, b, (dims, ((), ())), preferred_element_type=F32)]
    add x1 -> x3, other arithmetic: 0.13 us -> 3.88 us  [the longest x1 2.01 us: line_plan(): own_u = v['own_gu'][:, half:] + v['got_gu'][:, half:]]
    concatenate x3 -> x0, local copies, waits for them, and re-layouts: 1.82 us -> none  [the longest x1 1.72 us: line_plan(): sib_w = jnp.concatenate([v['sib_g'], v['sib_u']], axis=1)]
    concatenate x0 -> x2, other arithmetic: none -> 1.52 us  [the longest x1 1.28 us: line_plan(): jnp.concatenate([v[name] for name in ('grd', 'g_near', 'g_cross', 'g_flip...]
    ppermute x27 -> x28, starting transfers between devices: 43.2 us -> 44.5 us  [over(): return lax.ppermute(x, axis, pairs)]
    unnamed x17 -> x33, local copies, waits for them, and re-layouts: 5.23 us -> 6.29 us
    ppermute x27 -> x28, waiting for transfers between devices: 43.2 us -> 42.5 us  [over(): return lax.ppermute(x, axis, pairs)]
  transfers between devices with their start and end apart: 27 -> 28, of which waited for: 13 -> 12; matrix products, arithmetic and copies ran while one was open for 37% -> 29% of each run, Pallas kernels for 0% -> 0%
where the time goes in v3:
time: 135 us
  starting transfers between devices  44.5 us (33%)
  waiting for transfers between devices  42.5 us (31%)
  matrix products  28.3 us (21%)
  other arithmetic  11 us (8%)
  local copies, waits for them, and re-layouts  6.61 us (5%)
    ppermute x28, starting transfers between devices, over(): return lax.ppermute(x, axis, pairs)  44.5 us
    ppermute x28, waiting for transfers between devices, over(): return lax.ppermute(x, axis, pairs)  42.5 us
    dot_general x24, matrix products, mm(): return lax.dot_general(a, b, (dims, ((), ())), preferred_element_type=F32)  28.3 us
    unnamed x33, local copies, waits for them, and re-layouts  6.29 us
  transfers between devices with their start and end apart: 28, of which 12 were waited for; matrix products, arithmetic and copies ran while one was open for 29% of the time, Pallas kernels for 0%

profile of v3, /device:TPU:0, one launch (start us, length us, event | category | flops | bytes accessed | tf_op | source)
XLA Modules:
  0.0 134.6 jit_solution(1817729342887610935)
XLA Ops:
  1.5 1.6 %collective-permute-start.3 = (bf16[128,2048]{1,0:T(8,128)(2,1)}, bf16[128,2048]{1,0:T(8,128)(2,1)}, u32[]{:S(2)}, u32[]{:S(2)}) collective-permute-start(bf16[128,2048]{1,0:T(8,128)(2,1)} %bitcast.74), channel_id=1, source_target_pairs={{1,2},{2,1},{5,6},{6,5},{9,10},{10,9},{13,14},{14,13},{17,18},{18,... | collective-permute-start | bytes 1572872 | tf_op jit(solution)/shard_map/t_mid_in/ppermute | solution.py:200
  3.1 5.1 %collective-permute-start.4 = (bf16[128,2048]{1,0:T(8,128)(2,1)}, bf16[128,2048]{1,0:T(8,128)(2,1)S(1)}, u32[]{:S(2)}, u32[]{:S(2)}) collective-permute-start(bf16[128,2048]{1,0:T(8,128)(2,1)} %bitcast.75), channel_id=1, source_target_pairs={{0,1},{3,2},{1,0},{2,3},{4,5},{7,6},{5,4},{6,7},{8,9},{11,10},{9,8... | collective-permute-start | bytes 1572872 | tf_op jit(solution)/shard_map/t_near/ppermute | solution.py:200
  8.7 1.9 %collective-permute-start.1 = (f32[1,128]{1,0:T(1,128)S(1)}, f32[1,128]{1,0:T(1,128)S(1)}, u32[]{:S(2)}, u32[]{:S(2)}) collective-permute-start(f32[1,128]{1,0:T(1,128)S(1)} %bitcast.99), channel_id=1, source_target_pairs={{0,3},{1,2},{2,1},{3,0},{4,7},{5,6},{6,5},{7,4},{8,11},{9,10},{10,... | collective-permute-start | bytes 1544 | tf_op jit(solution)/shard_map/p/ppermute | solution.py:200
  10.6 1.0 collective-permute-start.2
  11.7 1.6 %constant_dynamic-update-slice_fusion.1 = bf16[2048,768]{1,0:T(8,128)(2,1)S(1)} fusion(bf16[2048,384]{1,0:T(8,128)(2,1)} %bitcast.86), kind=kLoop, calls=%fused_computation.126 | loop fusion | bytes 3145728
  14.7 5.2 %collective-permute-done = f32[1,128]{1,0:T(1,128)S(1)} collective-permute-done((f32[1,128]{1,0:T(1,128)S(1)}, f32[1,128]{1,0:T(1,128)S(1)}, u32[]{:S(2)}, u32[]{:S(2)}) %collective-permute-start) | collective-permute-done | bytes 544 | tf_op jit(solution)/shard_map/p/ppermute | solution.py:200
  19.9 1.3 collective-permute-done.1
  23.2 1.3 collective-permute-start.10
  24.5 12.1 %collective-permute-done.5 = bf16[128,2048]{1,0:T(8,128)(2,1)} collective-permute-done((bf16[128,2048]{1,0:T(8,128)(2,1)S(1)}, bf16[128,2048]{1,0:T(8,128)(2,1)}, u32[]{:S(2)}, u32[]{:S(2)}) %collective-permute-start.5) | collective-permute-done | bytes 524320 | tf_op jit(solution)/shard_map/g_near/ppermute | solution.py:200
  36.6 1.2 copy-done.2
  37.9 1.5 %collective-permute-start.9 = (bf16[128,2048]{1,0:T(8,128)(2,1)}, bf16[128,2048]{1,0:T(8,128)(2,1)}, u32[]{:S(2)}, u32[]{:S(2)}) collective-permute-start(bf16[128,2048]{1,0:T(8,128)(2,1)} %collective-permute-done.5), channel_id=1, source_target_pairs={{1,2},{2,1},{5,6},{6,5},{9,10},{10,9},{13,14},{14,13},{17,18},{18,... | collective-permute-start | bytes 1572872 | tf_op jit(solution)/shard_map/g_far_in/ppermute | solution.py:200
  40.1 1.3 collective-permute-start.12
  41.4 1.4 %copy-done.1 = bf16[1,1,384,2048]{3,2,1,0:T(8,128)(2,1)S(1)} copy-done((bf16[1,1,384,2048]{3,2,1,0:T(8,128)(2,1)S(1)}, bf16[1,1,384,2048]{3,2,1,0:T(8,128)(2,1)}, u32[]{:S(2)}) %copy-start.1) | copy-done | bytes 1572888
  42.8 1.4 %copy-done.3 = bf16[384,2048]{1,0:T(8,128)(2,1)S(1)} copy-done((bf16[384,2048]{1,0:T(8,128)(2,1)S(1)}, bf16[384,2048]{1,0:T(8,128)(2,1)}, u32[]{:S(2)}) %copy-start.3) | copy-done | bytes 1572888
  48.0 1.0 fusion.52
  49.1 1.1 broadcast_select_fusion.3
  50.2 1.0 fusion.51
  51.2 1.0 fusion.50
  52.3 1.5 %collective-permute-start.13 = (bf16[128,2048]{1,0:T(8,128)(2,1)}, bf16[128,2048]{1,0:T(8,128)(2,1)S(1)}, u32[]{:S(2)}, u32[]{:S(2)}) collective-permute-start(bf16[128,2048]{1,0:T(8,128)(2,1)} %collective-permute-done.9), channel_id=1, source_target_pairs={{1,0},{2,3},{5,4},{6,7},{9,8},{10,11},{13,12},{14,15},{17,16},{18,... | collective-permute-start | bytes 1572872 | tf_op jit(solution)/shard_map/g_far_out/ppermute | solution.py:200
  55.1 1.2 fusion.47
  56.3 1.2 fusion
  58.4 2.0 %fusion.57 = f32[768,128]{1,0:T(8,128)S(1)} fusion(bf16[768,2048]{1,0:T(8,128)(2,1)S(1)} %get-tuple-element.815, bf16[128,2048]{1,0:T(8,128)(2,1)} %collective-permute-done.5), kind=kOutput, calls=%fused_computation.157 | convolution fusion | flops 402653184 | bytes 4063232 | tf_op jit(solution)/shard_map/behind/dot_general | solution.py:203
  60.8 1.2 fusion.46
  63.1 1.0 fusion.55
  64.1 1.3 collective-permute-start.14
  65.4 1.2 fusion.1
  66.7 4.7 %collective-permute-done.13 = bf16[128,2048]{1,0:T(8,128)(2,1)S(1)} collective-permute-done((bf16[128,2048]{1,0:T(8,128)(2,1)}, bf16[128,2048]{1,0:T(8,128)(2,1)S(1)}, u32[]{:S(2)}, u32[]{:S(2)}) %collective-permute-start.13) | collective-permute-done | bytes 524320 | tf_op jit(solution)/shard_map/g_far_out/ppermute | solution.py:200
  72.8 1.2 fusion.45
  74.0 1.2 fusion.2
  75.2 7.4 %collective-permute-start.15 = (bf16[128,2048]{1,0:T(8,128)(2,1)S(1)}, bf16[128,2048]{1,0:T(8,128)(2,1)S(1)}, u32[]{:S(2)}, u32[]{:S(2)}) collective-permute-start(bf16[128,2048]{1,0:T(8,128)(2,1)S(1)} %fusion.2), channel_id=1, source_target_pairs={{0,1},{3,2},{4,5},{7,6},{8,9},{11,10},{12,13},{15,14},{16,17},{19,... | collective-permute-start | bytes 1572872 | tf_op jit(solution)/shard_map/r5/ppermute | solution.py:200
  82.6 2.2 %collective-permute-done.14 = bf16[128,2048]{1,0:T(8,128)(2,1)S(1)} collective-permute-done((bf16[128,2048]{1,0:T(8,128)(2,1)S(1)}, bf16[128,2048]{1,0:T(8,128)(2,1)S(1)}, u32[]{:S(2)}, u32[]{:S(2)}) %collective-permute-start.14) | collective-permute-done | bytes 524320 | tf_op jit(solution)/shard_map/g_mid_out/ppermute | solution.py:200
  86.3 1.2 fusion.44
  87.5 1.2 fusion.3
  88.7 2.5 %collective-permute-start.16 = (bf16[128,2048]{1,0:T(8,128)(2,1)S(1)}, bf16[128,2048]{1,0:T(8,128)(2,1)S(1)}, u32[]{:S(2)}, u32[]{:S(2)}) collective-permute-start(bf16[128,2048]{1,0:T(8,128)(2,1)S(1)} %fusion.3), channel_id=1, source_target_pairs={{0,1},{3,2},{4,5},{7,6},{8,9},{11,10},{12,13},{15,14},{16,17},{19,... | collective-permute-start | bytes 1572872 | tf_op jit(solution)/shard_map/r4/ppermute | solution.py:200
  91.4 1.3 pad_maximum_fusion
  92.7 1.4 %collective-permute-done.15 = bf16[128,2048]{1,0:T(8,128)(2,1)S(1)} collective-permute-done((bf16[128,2048]{1,0:T(8,128)(2,1)S(1)}, bf16[128,2048]{1,0:T(8,128)(2,1)S(1)}, u32[]{:S(2)}, u32[]{:S(2)}) %collective-permute-start.15) | collective-permute-done | bytes 524320 | tf_op jit(solution)/shard_map/r5/ppermute | solution.py:200
  95.9 1.9 %convolution_convert_fusion.1 = bf16[2048,768]{1,0:T(8,128)(2,1)S(1)} fusion(bf16[2048,512]{0,1:T(8,128)(2,1)S(1)} %pad_maximum_fusion.1, bf16[768,128]{1,0:T(8,128)(2,1)S(1)} %pad_maximum_fusion.7, bf16[768,128]{1,0:T(8,128)(2,1)S(1)} %pad_maximum_fusion.9, bf16[768,128]{1,0:T(8,128)(2,1)S(1)} %pad_maximum_fusion.5, bf16[768,128]{1,0:T(8,128)(2,1)S(1)} %get-tuple-element.963), kind=kOutput, calls=%fused_computation.1 | convolution fusion | flops 1615331328 | bytes 6029312 | tf_op jit(solution)/shard_map/weight_grads/dot_general | solution.py:203
  97.8 4.6 %collective-permute-done.16 = bf16[128,2048]{1,0:T(8,128)(2,1)S(1)} collective-permute-done((bf16[128,2048]{1,0:T(8,128)(2,1)S(1)}, bf16[128,2048]{1,0:T(8,128)(2,1)S(1)}, u32[]{:S(2)}, u32[]{:S(2)}) %collective-permute-start.16) | collective-permute-done | bytes 524320 | tf_op jit(solution)/shard_map/r4/ppermute | solution.py:200
  103.3 5.8 %collective-permute-start.20 = (bf16[64,2048]{1,0:T(8,128)(2,1)S(1)}, bf16[64,2048]{1,0:T(8,128)(2,1)S(1)}, u32[]{:S(2)}, u32[]{:S(2)}) collective-permute-start(bf16[64,2048]{1,0:T(8,128)(2,1)S(1)} %get-tuple-element.1046), channel_id=1, source_target_pairs={{0,1},{3,2},{1,0},{2,3},{4,5},{7,6},{5,4},{6,7},{8,9},{11,10},{9,8... | collective-permute-start | bytes 786440 | tf_op jit(solution)/shard_map/r1/ppermute | solution.py:200
  109.1 1.1 collective-permute-start.18
  110.1 1.4 %collective-permute-start.19 = (f32[1,128]{1,0:T(1,128)S(1)}, f32[1,128]{1,0:T(1,128)S(1)}, u32[]{:S(2)}, u32[]{:S(2)}) collective-permute-start(f32[1,128]{1,0:T(1,128)S(1)} %add_bitcast_fusion.1), channel_id=1, source_target_pairs={{0,3},{1,2},{2,1},{3,0},{4,7},{5,6},{6,5},{7,4},{8,11},{9,10},{10,... | collective-permute-start | bytes 1544 | tf_op jit(solution)/shard_map/dot/ppermute | solution.py:200
  112.5 1.9 %convolution_convert_fusion = bf16[2048,768]{1,0:T(8,128)(2,1)S(1)} fusion(bf16[2048,512]{0,1:T(8,128)(2,1)S(1)} %pad_maximum_fusion.1, bf16[768,128]{1,0:T(8,128)(2,1)S(1)} %pad_maximum_fusion.6, bf16[768,128]{1,0:T(8,128)(2,1)S(1)} %pad_maximum_fusion.8, bf16[768,128]{1,0:T(8,128)(2,1)S(1)} %pad_maximum_fusion.4, bf16[768,128]{1,0:T(8,128)(2,1)S(1)} %get-tuple-element.1058), kind=kOutput, calls=%fused_computation | convolution fusion | flops 1615331328 | bytes 6029312 | tf_op jit(solution)/shard_map/weight_grads/dot_general | solution.py:203
  115.4 3.1 %collective-permute-done.18 = f32[1,128]{1,0:T(1,128)S(1)} collective-permute-done((f32[1,128]{1,0:T(1,128)S(1)}, f32[1,128]{1,0:T(1,128)S(1)}, u32[]{:S(2)}, u32[]{:S(2)}) %collective-permute-start.18) | collective-permute-done | bytes 544 | tf_op jit(solution)/shard_map/dot/ppermute | solution.py:200
  119.3 2.5 %collective-permute-start.22 = (bf16[64,2048]{1,0:T(8,128)(2,1)S(1)}, bf16[64,2048]{1,0:T(8,128)(2,1)S(1)}, u32[]{:S(2)}, u32[]{:S(2)}) collective-permute-start(bf16[64,2048]{1,0:T(8,128)(2,1)S(1)} %add_convert_fusion.1), channel_id=1, source_target_pairs={{0,24},{8,0},{16,8},{24,16},{1,25},{9,1},{17,9},{25,17},{2,26},{10... | collective-permute-start | bytes 786440 | tf_op jit(solution)/shard_map/up/ppermute | solution.py:200
  122.3 4.4 %collective-permute-done.25 = bf16[384,2048]{1,0:T(8,128)(2,1)S(1)} collective-permute-done((bf16[384,2048]{1,0:T(8,128)(2,1)S(1)}, bf16[384,2048]{1,0:T(8,128)(2,1)S(1)}, u32[]{:S(2)}, u32[]{:S(2)}) %collective-permute-start.25) | collective-permute-done | bytes 1572896 | tf_op jit(solution)/shard_map/got_dn/ppermute | solution.py:200
  126.7 2.0 %slice_add_fusion = (bf16[2048,384]{1,0:T(8,128)(2,1)}, bf16[2048,384]{1,0:T(8,128)(2,1)}) fusion(bf16[2048,768]{1,0:T(8,128)(2,1)S(1)} %collective-permute-done.26, bf16[2048,768]{1,0:T(8,128)(2,1)S(1)} %convolution_convert_fusion), kind=kLoop, calls=%fused_computation.14 | loop fusion | flops 1572864 | bytes 9437184 | tf_op jit(solution)/shard_map/add | solution.py:369
  128.7 1.8 %add.198 = bf16[384,2048]{1,0:T(8,128)(2,1)} add(bf16[384,2048]{1,0:T(8,128)(2,1)S(1)} %convolution_convert_fusion.2, bf16[384,2048]{1,0:T(8,128)(2,1)S(1)} %collective-permute-done.25) | non-fusion elementwise | flops 786432 | bytes 4718592 | tf_op jit(solution)/shard_map/add | solution.py:367
  131.2 2.0 %collective-permute-done.24 = bf16[64,2048]{1,0:T(8,128)(2,1)S(1)} collective-permute-done((bf16[64,2048]{1,0:T(8,128)(2,1)S(1)}, bf16[64,2048]{1,0:T(8,128)(2,1)S(1)}, u32[]{:S(2)}, u32[]{:S(2)}) %collective-permute-start.24) | collective-permute-done | bytes 262176 | tf_op jit(solution)/shard_map/up/ppermute | solution.py:200
  (102 shorter events, 24.3 us)
Async XLA Ops:
  0.6 12.6 %copy-start.12 = (bf16[1,1,2048,384]{3,2,1,0:T(8,128)(2,1)S(1)}, bf16[1,1,2048,384]{3,2,1,0:T(8,128)(2,1)}, u32[]{:S(2)}) copy-start(bf16[1,1,2048,384]{3,2,1,0:T(8,128)(2,1)} %param.12) | copy-start | bytes 4718596
  1.5 12.1 %copy-start.6 = (bf16[1,128,2048]{2,1,0:T(8,128)(2,1)S(1)}, bf16[1,128,2048]{2,1,0:T(8,128)(2,1)}, u32[]{:S(2)}) copy-start(bf16[1,128,2048]{2,1,0:T(8,128)(2,1)} %param.7) | copy-start | bytes 1572868
  1.5 19.6 %collective-permute-start.3 = (bf16[128,2048]{1,0:T(8,128)(2,1)}, bf16[128,2048]{1,0:T(8,128)(2,1)}, u32[]{:S(2)}, u32[]{:S(2)}) collective-permute-start(bf16[128,2048]{1,0:T(8,128)(2,1)} %bitcast.74), channel_id=1, source_target_pairs={{1,2},{2,1},{5,6},{6,5},{9,10},{10,9},{13,14},{14,13},{17,18},{18,... | collective-permute-start | bytes 1572872 | tf_op jit(solution)/shard_map/t_mid_in/ppermute | solution.py:200
  3.1 18.0 %collective-permute-start.4 = (bf16[128,2048]{1,0:T(8,128)(2,1)}, bf16[128,2048]{1,0:T(8,128)(2,1)S(1)}, u32[]{:S(2)}, u32[]{:S(2)}) collective-permute-start(bf16[128,2048]{1,0:T(8,128)(2,1)} %bitcast.75), channel_id=1, source_target_pairs={{0,1},{3,2},{1,0},{2,3},{4,5},{7,6},{5,4},{6,7},{8,9},{11,10},{9,8... | collective-permute-start | bytes 1572872 | tf_op jit(solution)/shard_map/t_near/ppermute | solution.py:200
  8.2 11.6 %collective-permute-start = (f32[1,128]{1,0:T(1,128)S(1)}, f32[1,128]{1,0:T(1,128)S(1)}, u32[]{:S(2)}, u32[]{:S(2)}) collective-permute-start(f32[1,128]{1,0:T(1,128)S(1)} %bitcast.100), channel_id=1, source_target_pairs={{0,2},{1,3},{2,0},{3,1},{4,6},{5,7},{6,4},{7,5},{8,10},{9,11},{10,... | collective-permute-start | bytes 1544 | tf_op jit(solution)/shard_map/p/ppermute | solution.py:200
  8.7 12.4 %collective-permute-start.1 = (f32[1,128]{1,0:T(1,128)S(1)}, f32[1,128]{1,0:T(1,128)S(1)}, u32[]{:S(2)}, u32[]{:S(2)}) collective-permute-start(f32[1,128]{1,0:T(1,128)S(1)} %bitcast.99), channel_id=1, source_target_pairs={{0,3},{1,2},{2,1},{3,0},{4,7},{5,6},{6,5},{7,4},{8,11},{9,10},{10,... | collective-permute-start | bytes 1544 | tf_op jit(solution)/shard_map/p/ppermute | solution.py:200
  10.6 10.5 %collective-permute-start.2 = (f32[1,128]{1,0:T(1,128)S(1)}, f32[1,128]{1,0:T(1,128)S(1)}, u32[]{:S(2)}, u32[]{:S(2)}) collective-permute-start(f32[1,128]{1,0:T(1,128)S(1)} %bitcast.98), channel_id=1, source_target_pairs={{0,1},{1,0},{2,3},{3,2},{4,5},{5,4},{6,7},{7,6},{8,9},{9,8},{10,11... | collective-permute-start | bytes 1544 | tf_op jit(solution)/shard_map/p/ppermute | solution.py:200
  13.3 8.0 %copy-start = (bf16[1,1,384,2048]{3,2,1,0:T(8,128)(2,1)S(1)}, bf16[1,1,384,2048]{3,2,1,0:T(8,128)(2,1)}, u32[]{:S(2)}) copy-start(bf16[1,1,384,2048]{3,2,1,0:T(8,128)(2,1)} %param.13) | copy-start | bytes 4718596
  13.3 8.4 %copy-start.10 = (bf16[1,128,2048]{2,1,0:T(8,128)(2,1)S(1)}, bf16[1,128,2048]{2,1,0:T(8,128)(2,1)}, u32[]{:S(2)}) copy-start(bf16[1,128,2048]{2,1,0:T(8,128)(2,1)} %param.8) | copy-start | bytes 1572868
  13.6 24.2 %copy-start.4 = (bf16[2048,768]{1,0:T(8,128)(2,1)}, bf16[2048,768]{1,0:T(8,128)(2,1)S(1)}, u32[]{:S(2)}) copy-start(bf16[2048,768]{1,0:T(8,128)(2,1)S(1)} %constant_dynamic-update-slice_fusion) | copy-start | bytes 9437188
  21.1 16.7 %copy-start.8 = (bf16[128,2048]{1,0:T(8,128)(2,1)}, bf16[128,2048]{1,0:T(8,128)(2,1)S(1)}, u32[]{:S(2)}) copy-start(bf16[128,2048]{1,0:T(8,128)(2,1)S(1)} %collective-permute-done.4) | copy-start | bytes 1572868
  21.1 16.7 %collective-permute-start.7 = (bf16[2048,768]{1,0:T(8,128)(2,1)S(1)}, bf16[2048,768]{1,0:T(8,128)(2,1)S(1)}, u32[]{:S(2)}, u32[]{:S(2)}) collective-permute-start(bf16[2048,768]{1,0:T(8,128)(2,1)S(1)} %constant_dynamic-update-slice_fusion), channel_id=1, source_target_pairs={{0,4},{4,0},{1,5},{5,1},{2,6},{6,2},{3,7},{7,3},{8,12},{12,8},{9,1... | collective-permute-start | bytes 9437192 | tf_op jit(solution)/shard_map/sib_w/ppermute | solution.py:200
  21.2 15.4 %collective-permute-start.6 = (bf16[384,2048]{1,0:T(8,128)(2,1)S(1)}, bf16[384,2048]{1,0:T(8,128)(2,1)S(1)}, u32[]{:S(2)}, u32[]{:S(2)}) collective-permute-start(bf16[384,2048]{1,0:T(8,128)(2,1)S(1)} %bitcast.70), channel_id=1, source_target_pairs={{0,4},{4,0},{1,5},{5,1},{2,6},{6,2},{3,7},{7,3},{8,12},{12,8},{9,1... | collective-permute-start | bytes 4718600 | tf_op jit(solution)/shard_map/sib_d/ppermute | solution.py:200
  21.7 14.9 %collective-permute-start.5 = (bf16[128,2048]{1,0:T(8,128)(2,1)S(1)}, bf16[128,2048]{1,0:T(8,128)(2,1)}, u32[]{:S(2)}, u32[]{:S(2)}) collective-permute-start(bf16[128,2048]{1,0:T(8,128)(2,1)S(1)} %bitcast.81), channel_id=1, source_target_pairs={{0,1},{3,2},{1,0},{2,3},{4,5},{7,6},{5,4},{6,7},{8,9},{11,10},{9,8... | collective-permute-start | bytes 1572872 | tf_op jit(solution)/shard_map/g_near/ppermute | solution.py:200
  22.5 14.1 %collective-permute-start.8 = (bf16[128,2048]{1,0:T(8,128)(2,1)S(1)}, bf16[128,2048]{1,0:T(8,128)(2,1)S(1)}, u32[]{:S(2)}, u32[]{:S(2)}) collective-permute-start(bf16[128,2048]{1,0:T(8,128)(2,1)S(1)} %collective-permute-done.4), channel_id=1, source_target_pairs={{1,2},{2,1},{5,6},{6,5},{9,10},{10,9},{13,14},{14,13},{17,18},{18,... | collective-permute-start | bytes 1572872 | tf_op jit(solution)/shard_map/t_far_in/ppermute | solution.py:200
  23.2 23.8 %collective-permute-start.10 = (bf16[128,2048]{1,0:T(8,128)(2,1)}, bf16[128,2048]{1,0:T(8,128)(2,1)}, u32[]{:S(2)}, u32[]{:S(2)}) collective-permute-start(bf16[128,2048]{1,0:T(8,128)(2,1)} %collective-permute-done.3), channel_id=1, source_target_pairs={{1,0},{2,3},{5,4},{6,7},{9,8},{10,11},{13,12},{14,15},{17,16},{18,... | collective-permute-start | bytes 1572872 | tf_op jit(solution)/shard_map/t_mid_out/ppermute | solution.py:200
  36.6 1.3 copy-start.13
  36.6 1.2 copy-start.2
  37.9 9.1 %collective-permute-start.9 = (bf16[128,2048]{1,0:T(8,128)(2,1)}, bf16[128,2048]{1,0:T(8,128)(2,1)}, u32[]{:S(2)}, u32[]{:S(2)}) collective-permute-start(bf16[128,2048]{1,0:T(8,128)(2,1)} %collective-permute-done.5), channel_id=1, source_target_pairs={{1,2},{2,1},{5,6},{6,5},{9,10},{10,9},{13,14},{14,13},{17,18},{18,... | collective-permute-start | bytes 1572872 | tf_op jit(solution)/shard_map/g_far_in/ppermute | solution.py:200
  39.4 18.2 %collective-permute-start.11 = (bf16[128,2048]{1,0:T(8,128)(2,1)}, bf16[128,2048]{1,0:T(8,128)(2,1)S(1)}, u32[]{:S(2)}, u32[]{:S(2)}) collective-permute-start(bf16[128,2048]{1,0:T(8,128)(2,1)} %bitcast.80), channel_id=1, source_target_pairs={{1,2},{2,1},{5,6},{6,5},{9,10},{10,9},{13,14},{14,13},{17,18},{18,... | collective-permute-start | bytes 1572872 | tf_op jit(solution)/shard_map/g_mid_in/ppermute | solution.py:200
  40.1 18.3 %collective-permute-start.12 = (bf16[128,2048]{1,0:T(8,128)(2,1)}, bf16[128,2048]{1,0:T(8,128)(2,1)S(1)}, u32[]{:S(2)}, u32[]{:S(2)}) collective-permute-start(bf16[128,2048]{1,0:T(8,128)(2,1)} %copy-done.13), channel_id=1, source_target_pairs={{1,0},{2,3},{5,4},{6,7},{9,8},{10,11},{13,12},{14,15},{17,16},{18,... | collective-permute-start | bytes 1572872 | tf_op jit(solution)/shard_map/t_far_out/ppermute | solution.py:200
  41.4 1.4 %copy-start.1 = (bf16[1,1,384,2048]{3,2,1,0:T(8,128)(2,1)S(1)}, bf16[1,1,384,2048]{3,2,1,0:T(8,128)(2,1)}, u32[]{:S(2)}) copy-start(bf16[1,1,384,2048]{3,2,1,0:T(8,128)(2,1)} %param.13) | copy-start | bytes 4718596
  42.8 1.4 %copy-start.3 = (bf16[384,2048]{1,0:T(8,128)(2,1)S(1)}, bf16[384,2048]{1,0:T(8,128)(2,1)}, u32[]{:S(2)}) copy-start(bf16[384,2048]{1,0:T(8,128)(2,1)} %copy-done.2) | copy-start | bytes 4718596
  44.2 1.0 copy-start.7
  44.7 2.3 %copy-start.9 = (bf16[128,2048]{1,0:T(8,128)(2,1)S(1)}, bf16[128,2048]{1,0:T(8,128)(2,1)}, u32[]{:S(2)}) copy-start(bf16[128,2048]{1,0:T(8,128)(2,1)} %copy-done.8) | copy-start | bytes 1572868
  45.2 2.8 %copy-start.5 = (bf16[2048,768]{1,0:T(8,128)(2,1)S(1)}, bf16[2048,768]{1,0:T(8,128)(2,1)}, u32[]{:S(2)}) copy-start(bf16[2048,768]{1,0:T(8,128)(2,1)} %copy-done.4) | copy-start | bytes 9437188
  46.3 2.8 %copy-start.14 = (bf16[128,2048]{1,0:T(8,128)(2,1)S(1)}, bf16[128,2048]{1,0:T(8,128)(2,1)}, u32[]{:S(2)}) copy-start(bf16[128,2048]{1,0:T(8,128)(2,1)} %copy-done.13) | copy-start | bytes 1572868
  51.2 2.6 %copy-start.11 = (bf16[1,128,2048]{2,1,0:T(8,128)(2,1)S(1)}, bf16[1,128,2048]{2,1,0:T(8,128)(2,1)}, u32[]{:S(2)}) copy-start(bf16[1,128,2048]{2,1,0:T(8,128)(2,1)} %param.8) | copy-start | bytes 1572868
  52.3 19.1 %collective-permute-start.13 = (bf16[128,2048]{1,0:T(8,128)(2,1)}, bf16[128,2048]{1,0:T(8,128)(2,1)S(1)}, u32[]{:S(2)}, u32[]{:S(2)}) collective-permute-start(bf16[128,2048]{1,0:T(8,128)(2,1)} %collective-permute-done.9), channel_id=1, source_target_pairs={{1,0},{2,3},{5,4},{6,7},{9,8},{10,11},{13,12},{14,15},{17,16},{18,... | collective-permute-start | bytes 1572872 | tf_op jit(solution)/shard_map/g_far_out/ppermute | solution.py:200
  64.1 20.7 %collective-permute-start.14 = (bf16[128,2048]{1,0:T(8,128)(2,1)S(1)}, bf16[128,2048]{1,0:T(8,128)(2,1)S(1)}, u32[]{:S(2)}, u32[]{:S(2)}) collective-permute-start(bf16[128,2048]{1,0:T(8,128)(2,1)S(1)} %collective-permute-done.11), channel_id=1, source_target_pairs={{1,0},{2,3},{5,4},{6,7},{9,8},{10,11},{13,12},{14,15},{17,16},{18,... | collective-permute-start | bytes 1572872 | tf_op jit(solution)/shard_map/g_mid_out/ppermute | solution.py:200
  75.2 18.9 %collective-permute-start.15 = (bf16[128,2048]{1,0:T(8,128)(2,1)S(1)}, bf16[128,2048]{1,0:T(8,128)(2,1)S(1)}, u32[]{:S(2)}, u32[]{:S(2)}) collective-permute-start(bf16[128,2048]{1,0:T(8,128)(2,1)S(1)} %fusion.2), channel_id=1, source_target_pairs={{0,1},{3,2},{4,5},{7,6},{8,9},{11,10},{12,13},{15,14},{16,17},{19,... | collective-permute-start | bytes 1572872 | tf_op jit(solution)/shard_map/r5/ppermute | solution.py:200
  88.7 13.7 %collective-permute-start.16 = (bf16[128,2048]{1,0:T(8,128)(2,1)S(1)}, bf16[128,2048]{1,0:T(8,128)(2,1)S(1)}, u32[]{:S(2)}, u32[]{:S(2)}) collective-permute-start(bf16[128,2048]{1,0:T(8,128)(2,1)S(1)} %fusion.3), channel_id=1, source_target_pairs={{0,1},{3,2},{4,5},{7,6},{8,9},{11,10},{12,13},{15,14},{16,17},{19,... | collective-permute-start | bytes 1572872 | tf_op jit(solution)/shard_map/r4/ppermute | solution.py:200
  94.2 9.0 %collective-permute-start.17 = (bf16[128,2048]{1,0:T(8,128)(2,1)S(1)}, bf16[128,2048]{1,0:T(8,128)(2,1)S(1)}, u32[]{:S(2)}, u32[]{:S(2)}) collective-permute-start(bf16[128,2048]{1,0:T(8,128)(2,1)S(1)} %add.189), channel_id=1, source_target_pairs={{1,2},{2,1},{5,6},{6,5},{9,10},{10,9},{13,14},{14,13},{17,18},{18,... | collective-permute-start | bytes 1572872 | tf_op jit(solution)/shard_map/r3/ppermute | solution.py:200
  102.5 12.9 %collective-permute-start.21 = (bf16[128,2048]{1,0:T(8,128)(2,1)S(1)}, bf16[128,2048]{1,0:T(8,128)(2,1)S(1)}, u32[]{:S(2)}, u32[]{:S(2)}) collective-permute-start(bf16[128,2048]{1,0:T(8,128)(2,1)S(1)} %add.190), channel_id=1, source_target_pairs={{1,2},{2,1},{5,6},{6,5},{9,10},{10,9},{13,14},{14,13},{17,18},{18,... | collective-permute-start | bytes 1572872 | tf_op jit(solution)/shard_map/r2/ppermute | solution.py:200
  103.3 15.2 %collective-permute-start.20 = (bf16[64,2048]{1,0:T(8,128)(2,1)S(1)}, bf16[64,2048]{1,0:T(8,128)(2,1)S(1)}, u32[]{:S(2)}, u32[]{:S(2)}) collective-permute-start(bf16[64,2048]{1,0:T(8,128)(2,1)S(1)} %get-tuple-element.1046), channel_id=1, source_target_pairs={{0,1},{3,2},{1,0},{2,3},{4,5},{7,6},{5,4},{6,7},{8,9},{11,10},{9,8... | collective-permute-start | bytes 786440 | tf_op jit(solution)/shard_map/r1/ppermute | solution.py:200
  109.1 9.4 %collective-permute-start.18 = (f32[1,128]{1,0:T(1,128)S(1)}, f32[1,128]{1,0:T(1,128)S(1)}, u32[]{:S(2)}, u32[]{:S(2)}) collective-permute-start(f32[1,128]{1,0:T(1,128)S(1)} %add_bitcast_fusion), channel_id=1, source_target_pairs={{0,2},{1,3},{2,0},{3,1},{4,6},{5,7},{6,4},{7,5},{8,10},{9,11},{10,... | collective-permute-start | bytes 1544 | tf_op jit(solution)/shard_map/dot/ppermute | solution.py:200
  110.1 8.3 %collective-permute-start.19 = (f32[1,128]{1,0:T(1,128)S(1)}, f32[1,128]{1,0:T(1,128)S(1)}, u32[]{:S(2)}, u32[]{:S(2)}) collective-permute-start(f32[1,128]{1,0:T(1,128)S(1)} %add_bitcast_fusion.1), channel_id=1, source_target_pairs={{0,3},{1,2},{2,1},{3,0},{4,7},{5,6},{6,5},{7,4},{8,11},{9,10},{10,... | collective-permute-start | bytes 1544 | tf_op jit(solution)/shard_map/dot/ppermute | solution.py:200
  111.5 7.1 %collective-permute-start.23 = (bf16[64,2048]{1,0:T(8,128)(2,1)S(1)}, bf16[64,2048]{1,0:T(8,128)(2,1)S(1)}, u32[]{:S(2)}, u32[]{:S(2)}) collective-permute-start(bf16[64,2048]{1,0:T(8,128)(2,1)S(1)} %get-tuple-element.1047), channel_id=1, source_target_pairs={{0,1},{3,2},{1,0},{2,3},{4,5},{7,6},{5,4},{6,7},{8,9},{11,10},{9,8... | collective-permute-start | bytes 786440 | tf_op jit(solution)/shard_map/r1/ppermute | solution.py:200
  118.7 8.0 %collective-permute-start.26 = (bf16[2048,768]{1,0:T(8,128)(2,1)S(1)}, bf16[2048,768]{1,0:T(8,128)(2,1)S(1)}, u32[]{:S(2)}, u32[]{:S(2)}) collective-permute-start(bf16[2048,768]{1,0:T(8,128)(2,1)S(1)} %convolution_convert_fusion.1), channel_id=1, source_target_pairs={{0,4},{4,0},{1,5},{5,1},{2,6},{6,2},{3,7},{7,3},{8,12},{12,8},{9,1... | collective-permute-start | bytes 9437192 | tf_op jit(solution)/shard_map/got_gu/ppermute | solution.py:200
  118.8 7.9 %collective-permute-start.25 = (bf16[384,2048]{1,0:T(8,128)(2,1)S(1)}, bf16[384,2048]{1,0:T(8,128)(2,1)S(1)}, u32[]{:S(2)}, u32[]{:S(2)}) collective-permute-start(bf16[384,2048]{1,0:T(8,128)(2,1)S(1)} %convolution_convert_fusion.3), channel_id=1, source_target_pairs={{0,4},{4,0},{1,5},{5,1},{2,6},{6,2},{3,7},{7,3},{8,12},{12,8},{9,1... | collective-permute-start | bytes 4718600 | tf_op jit(solution)/shard_map/got_dn/ppermute | solution.py:200
  119.3 13.9 %collective-permute-start.22 = (bf16[64,2048]{1,0:T(8,128)(2,1)S(1)}, bf16[64,2048]{1,0:T(8,128)(2,1)S(1)}, u32[]{:S(2)}, u32[]{:S(2)}) collective-permute-start(bf16[64,2048]{1,0:T(8,128)(2,1)S(1)} %add_convert_fusion.1), channel_id=1, source_target_pairs={{0,24},{8,0},{16,8},{24,16},{1,25},{9,1},{17,9},{25,17},{2,26},{10... | collective-permute-start | bytes 786440 | tf_op jit(solution)/shard_map/up/ppermute | solution.py:200
  121.7 11.5 %collective-permute-start.24 = (bf16[64,2048]{1,0:T(8,128)(2,1)S(1)}, bf16[64,2048]{1,0:T(8,128)(2,1)S(1)}, u32[]{:S(2)}, u32[]{:S(2)}) collective-permute-start(bf16[64,2048]{1,0:T(8,128)(2,1)S(1)} %add_convert_fusion), channel_id=1, source_target_pairs={{0,24},{8,0},{16,8},{24,16},{1,25},{9,1},{17,9},{25,17},{2,26},{10... | collective-permute-start | bytes 786440 | tf_op jit(solution)/shard_map/up/ppermute | solution.py:200
  128.7 5.4 %copy-start.15 = (s32[1,128,2]{1,2,0:T(2,128)S(1)}, s32[1,128,2]{1,2,0:T(2,128)}, u32[]{:S(2)}) copy-start(s32[1,128,2]{1,2,0:T(2,128)} %param.9) | copy-start | bytes 3076
  130.5 3.5 %collective-permute-start.27 = (f32[1,128]{1,0:T(1,128)S(1)}, f32[1,128]{1,0:T(1,128)S(1)}, u32[]{:S(2)}, u32[]{:S(2)}) collective-permute-start(f32[1,128]{1,0:T(1,128)S(1)} %add_bitcast_fusion.2), channel_id=1, source_target_pairs={{0,1},{1,0},{2,3},{3,2},{4,5},{5,4},{6,7},{7,6},{8,9},{9,8},{10,11... | collective-permute-start | bytes 1544 | tf_op jit(solution)/shard_map/dot/ppermute | solution.py:200

commit v4 on v3

--- a/solution.py
+++ b/solution.py
@@ -1,4 +1,5 @@
 import functools
+import types
 
 import jax
 import jax.numpy as jnp
@@ -177,7 +178,7 @@
     anywhere = pl.BlockSpec(memory_space=pl.ANY)
     return pl.pallas_call(
         functools.partial(gather_kernel, [piece[1:] for piece in pieces]),
-        out_shape=[jax.ShapeDtypeStruct(dims, pieces[0][0].dtype) for dims in shapes],
+        out_shape=[pltpu.VMEM(dims, pieces[0][0].dtype) for dims in shapes],
         in_specs=[anywhere] * len(pieces),
         out_specs=[pl.BlockSpec(memory_space=pltpu.VMEM)] * len(shapes),
         scratch_shapes=[pltpu.SemaphoreType.DMA((len(pieces),))],
@@ -191,7 +192,7 @@
     place = lax.axis_index("expert")
     inner = (place == 1) | (place == 2)
     tok, grd = tokens[0], out_grad[0]
-    width = tok.shape[1]
+    count, width = tok.shape
     ids, probs = expert_ids[0], route_probs[0]
     half = gate_weight.shape[3]
 
@@ -208,15 +209,13 @@
     def small(x, k, name):
         return over(x, [(i, i ^ k) for i in range(4)], name)
 
-    v = dict(tok=tok, grd=grd, gate=gate_weight[0, 0], up=up_weight[0, 0], own_d=down_weight[0, 0])
+    v = types.SimpleNamespace(
+        tok=tok, grd=grd, gate=gate_weight[0, 0], up=up_weight[0, 0], own_d=down_weight[0, 0]
+    )
 
     def sync(**ready):
-        v.update(ready)
-        v.update(lax.optimization_barrier(v))
-
-    def drop(*names):
-        for name in names:
-            del v[name]
+        vars(v).update(ready)
+        vars(v).update(lax.optimization_barrier(vars(v)))
 
     def rows_of(x, c):
         part = x.shape[0] // 2
@@ -227,13 +226,13 @@
             return mm(w, rows, ((0,), (1,)))
 
     def ahead_both(rows):
-        return [ahead(rows, v["own_w"]), ahead(rows, v["sib_w"])]
+        return [ahead(rows, v.own_w), ahead(rows, v.sib_w)]
 
     def behind(grads, parts, p):
         with jax.named_scope("behind"):
             dots, halves, dx = 0.0, [], 0.0
-            both_hidden = mm(v["all_d"], grads, ((1,), (1,)))
-            for side, (pre, w) in enumerate(zip(parts, (v["own_w"], v["sib_w"]))):
+            both_hidden = mm(v.all_d, grads, ((1,), (1,)))
+            for side, (pre, w) in enumerate(zip(parts, (v.own_w, v.sib_w))):
                 gate, up = pre[:half], pre[half:]
                 sig = jax.nn.sigmoid(gate)
                 silu = gate * sig
@@ -251,133 +250,130 @@
         jnp.sum(jnp.where(ids == (place ^ k), probs, 0.0), axis=1).reshape(1, -1) for k in range(4)
     ]
     sync(columns=columns)
-    t_near = over(v["tok"], PAIRS, "t_near")
-    t_mid_in = over(v["tok"], MIDDLE, "t_mid_in")
-    p_near, p_cross, p_flip = (small(v["columns"][k], k, "p") for k in (1, 2, 3))
-    own_w = jnp.concatenate([v["gate"], v["up"]], axis=1)
-    a_own = ahead(v["tok"], own_w)
-    sync(own_w=own_w, a_own=a_own)
+    t_near = over(v.tok, PAIRS, "t_near")
+    t_mid_in = over(v.tok, MIDDLE, "t_mid_in")
+    p_near, p_cross, p_flip = (small(v.columns[k], k, "p") for k in (1, 2, 3))
+    (own_w,) = gather("own_w", [(width, 2 * half)], (v.gate, 0, 0, 0), (v.up, 0, 0, half))
+    sync(own_w=own_w)
 
     sync(t_near=t_near, t_mid_in=t_mid_in, p_near=p_near, p_cross=p_cross, p_flip=p_flip)
-    g_near = over(v["grd"], PAIRS, "g_near")
-    t_mid_out = over(v["t_mid_in"], OUTWARD, "t_mid_out")
-    t_far_in = over(v["t_near"], MIDDLE, "t_far_in")
-    sib_w = over(v["own_w"], SWAP, "sib_w", "dp")
-    sib_d = over(v["own_d"], SWAP, "sib_d", "dp")
-
-    sync(g_near=g_near, t_far_in=t_far_in, sib_w=sib_w, sib_d=sib_d)
-    g_far_in = over(v["g_near"], MIDDLE, "g_far_in")
-    t_far_out = over(v["t_far_in"], OUTWARD, "t_far_out")
-    g_mid_in = over(v["grd"], MIDDLE, "g_mid_in")
+    g_near = over(v.grd, PAIRS, "g_near")
+    t_mid_out = over(v.t_mid_in, OUTWARD, "t_mid_out")
+    t_far_in = over(v.t_near, MIDDLE, "t_far_in")
+    sib_w = over(v.own_w, SWAP, "sib_w", "dp")
+    sib_d = over(v.own_d, SWAP, "sib_d", "dp")
+    t_two = jnp.concatenate([v.tok, v.t_near], axis=0)
+    a_two = ahead(t_two, v.own_w)
+    sync(t_two=t_two, a_two=a_two)
+
+    sync(g_near=g_near)
+    g_far_in = over(v.g_near, MIDDLE, "g_far_in")
+    sync(t_far_in=t_far_in, sib_w=sib_w, sib_d=sib_d)
+    t_far_out = over(v.t_far_in, OUTWARD, "t_far_out")
     sib_w, all_d = gather(
         "sib_w",
         [(width, 2 * half), (2 * half, width)],
-        (v["sib_w"], 0, 0, 0),
-        (v["own_d"], 1, 0, 0),
-        (v["sib_d"], 1, half, 0),
-    )
-    drop("gate", "up", "own_d", "sib_d")
-    a_own = [v["a_own"], ahead(v["tok"], sib_w)]
-    sync(a_own=a_own, sib_w=sib_w, all_d=all_d)
+        (v.sib_w, 0, 0, 0),
+        (v.own_d, 1, 0, 0),
+        (v.sib_d, 1, half, 0),
+    )
+    del v.gate, v.up, v.own_d, v.sib_d
+    a_two = [v.a_two, ahead(v.t_two, sib_w)]
+    del v.t_two
+    sync(a_two=a_two, sib_w=sib_w, all_d=all_d)
 
     sync(t_mid_out=t_mid_out, g_far_in=g_far_in)
-    g_far_out = over(v["g_far_in"], OUTWARD, "g_far_out")
-    t_cross = pick(v["t_far_in"], v["t_mid_out"])
-    a_near, a_cross = ahead_both(v["t_near"]), ahead_both(t_cross)
-    dx_own, k_own = behind(v["grd"], v["a_own"], v["columns"][0])
-    drop("t_far_in", "t_mid_out", "a_own")
-    sync(t_cross=t_cross, a_cross=a_cross, a_near=a_near, dx_own=dx_own, k_own=k_own)
-
-    sync(t_far_out=t_far_out, g_mid_in=g_mid_in)
-    g_mid_out = over(v["g_mid_in"], OUTWARD, "g_mid_out")
-    t_flip = pick(v["t_mid_in"], v["t_far_out"])
-    a_flip = ahead_both(t_flip)
-    dx_near, k_near = behind(v["g_near"], v["a_near"], v["p_near"])
-    drop("t_mid_in", "t_far_out", "a_near", "p_near")
-    sync(t_flip=t_flip, a_flip=a_flip, dx_near=dx_near, k_near=k_near)
-
+    g_far_out = over(v.g_far_in, OUTWARD, "g_far_out")
+    g_mid_in = over(v.grd, MIDDLE, "g_mid_in")
+
+    two = jnp.concatenate([v.grd, v.g_near], axis=0)
+    dx_two, k_two = behind(two, v.a_two, jnp.concatenate([v.columns[0], v.p_near], axis=1))
+    del v.p_near, v.a_two, v.columns
+    sync(dx_two=dx_two, k_two=k_two)
+
+    sync(t_far_out=t_far_out)
+    t_cross, t_flip = pick(v.t_far_in, v.t_mid_out), pick(v.t_mid_in, v.t_far_out)
+    del v.t_far_in, v.t_mid_out, v.t_mid_in, v.t_far_out
+    a_far = ahead_both(jnp.concatenate([t_cross, t_flip], axis=0))
+    sync(t_cross=t_cross, t_flip=t_flip, a_far=a_far)
+
+    sync(g_mid_in=g_mid_in)
+    g_mid_out = over(v.g_mid_in, OUTWARD, "g_mid_out")
+    rows = jnp.concatenate([v.tok.T, v.t_near.T, v.t_cross.T, v.t_flip.T], axis=1)
+    del v.tok, v.t_near, v.t_cross, v.t_flip
+    sync(rows=rows)
     sync(g_far_out=g_far_out)
-    g_flip = pick(v["g_mid_in"], v["g_far_out"])
-    dx_flip, k_flip = behind(g_flip, v["a_flip"], v["p_flip"])
-    drop("g_mid_in", "g_far_out", "a_flip", "p_flip")
+    g_flip = pick(v.g_mid_in, v.g_far_out)
+    dx_flip, k_flip = behind(g_flip, [a[:, count:] for a in v.a_far], v.p_flip)
+    del v.g_mid_in, v.g_far_out, v.p_flip
     sync(g_flip=g_flip, dx_flip=dx_flip, k_flip=k_flip)
-    r5 = over(v["dx_flip"], INWARD, "r5")
+    r5 = over(v.dx_flip, INWARD, "r5")
 
     sync(g_mid_out=g_mid_out)
-    g_cross = pick(v["g_far_in"], v["g_mid_out"])
-    dx_cross, k_cross = behind(g_cross, v["a_cross"], v["p_cross"])
-    drop("g_far_in", "g_mid_out", "a_cross", "p_cross")
+    g_cross = pick(v.g_far_in, v.g_mid_out)
+    dx_cross, k_cross = behind(g_cross, [a[:, :count] for a in v.a_far], v.p_cross)
+    del v.g_far_in, v.g_mid_out, v.a_far, v.p_cross
     sync(g_cross=g_cross, dx_cross=dx_cross, k_cross=k_cross)
-    r4 = over(v["dx_cross"], INWARD, "r4")
-    order = ("tok", "t_near", "t_cross", "t_flip")
-    rows = jnp.concatenate([v[name].T for name in order], axis=1)
-    grads = jnp.concatenate([v[name] for name in ("grd", "g_near", "g_cross", "g_flip")], axis=0)
-    drop(*order, "grd", "g_near", "g_cross", "g_flip")
-    sync(rows=rows, grads=grads)
+    r4 = over(v.dx_cross, INWARD, "r4")
 
     sync(r5=r5)
-    back = v["dx_cross"] + v["r5"]
-    drop("dx_cross", "r5")
+    back = v.dx_cross + v.r5
+    del v.dx_cross, v.r5
     sync(back=back)
-    r3 = over(v["back"], MIDDLE, "r3")
-    drop("own_w", "sib_w", "all_d", "back")
+    r3 = over(v.back, MIDDLE, "r3")
+    grads = jnp.concatenate([v.grd, v.g_near, v.g_cross, v.g_flip], axis=0)
+    del v.grd, v.g_near, v.g_cross, v.g_flip
+    sync(grads=grads)
+    del v.own_w, v.sib_w, v.all_d, v.back
 
     def kept(which, side, first=0, last=None):
-        slots = [v["k_" + name][1][side][which][first:last] for name in ("own", "near", "cross", "flip")]
+        slots = [k[1][side][which][first:last] for k in (v.k_two, v.k_cross, v.k_flip)]
         return jnp.concatenate(slots, axis=1)
 
     with jax.named_scope("weight_grads"):
-        sib_gu = mm(v["rows"], kept(0, 1), ((1,), (1,))).astype(BF16)
-        sib_dn = mm(kept(1, 1), v["grads"], ((1,), (0,))).astype(BF16)
+        sib_gu = mm(v.rows, kept(0, 1), ((1,), (1,))).astype(BF16)
+        sib_dn = mm(kept(1, 1), v.grads, ((1,), (0,))).astype(BF16)
     sync(sib_gu=sib_gu, sib_dn=sib_dn)
 
     sync(r4=r4)
-    back = v["dx_flip"] + v["r4"]
-    drop("dx_flip", "r4")
-    sync(back=back)
-    r2 = over(v["back"], MIDDLE, "r2")
-
     sync(r3=r3)
-    back = [rows_of(v["dx_near"], c) + rows_of(v["r3"], c) for c in range(2)]
-    drop("dx_near", "r3")
-    sync(back=back)
-    r1 = [over(x, PAIRS, "r1") for x in v["back"]]
-    dots = [small(v["k_" + name][0], k, "dot") for k, name in ((2, "cross"), (3, "flip"))]
+    back_mid = v.dx_flip + v.r4
+    back = v.dx_two[count:] + v.r3
+    del v.dx_flip, v.r4, v.r3
+    sync(back=back, back_mid=back_mid)
+    r1 = over(v.back, PAIRS, "r1")
+    r2 = over(v.back_mid, MIDDLE, "r2")
+    got_gu = over(v.sib_gu, SWAP, "got_gu", "dp")
+    got_dn = over(v.sib_dn, SWAP, "got_dn", "dp")
     with jax.named_scope("weight_grads"):
-        own_gu = mm(v["rows"], kept(0, 0), ((1,), (1,))).astype(BF16)
-        own_dn = mm(kept(1, 0), v["grads"], ((1,), (0,))).astype(BF16)
+        own_gu = mm(v.rows, kept(0, 0), ((1,), (1,))).astype(BF16)
+        own_dn = mm(kept(1, 0), v.grads, ((1,), (0,))).astype(BF16)
     sync(own_gu=own_gu, own_dn=own_dn)
 
 
-    def section_hop(r1, c):
-        n = lax.axis_size("section")
-        parts = (v["dx_own"], v["r2"])
-        total = sum(rows_of(x, c).astype(F32) for x in parts) + r1.astype(F32)
-        sync(total=total.astype(BF16))
-        return over(v["total"], [(i, (i - 1) % n) for i in range(n)], "up", "section")
-
-    sync(r2=r2, r1a=r1[0], dots=dots)
-    up_a = section_hop(v["r1a"], 0)
-    sync(r1b=r1[1])
-    up_b = section_hop(v["r1b"], 1)
-    got_gu = over(v["sib_gu"], SWAP, "got_gu", "dp")
-    got_dn = over(v["sib_dn"], SWAP, "got_dn", "dp")
-    upstream = jnp.concatenate([up_a, up_b], axis=0)
+    sync(r1=r1)
+    sync(r2=r2)
+    n = lax.axis_size("section")
+    total = sum(x.astype(F32) for x in (v.dx_two[:count], v.r1, v.r2))
+    sync(total=total.astype(BF16))
+    upstream = over(v.total, [(i, (i - 1) % n) for i in range(n)], "up", "section")
     sync(got_dn=got_dn, got_gu=got_gu)
-    own_n = v["own_dn"] + v["got_dn"]
-    own_g = v["own_gu"][:, :half] + v["got_gu"][:, :half]
-    own_u = v["own_gu"][:, half:] + v["got_gu"][:, half:]
+    own_n = v.own_dn + v.got_dn
+    own_g = v.own_gu[:, :half] + v.got_gu[:, :half]
+    own_u = v.own_gu[:, half:] + v.got_gu[:, half:]
     sync(own_g=own_g, own_u=own_u, own_n=own_n)
-    dots = [v["k_own"][0], small(v["k_near"][0], 1, "dot")] + v["dots"]
+    two = v.k_two[0]
+    dots = (two[:, count:], v.k_cross[0], v.k_flip[0])
+    dots = [two[:, :count]] + [small(d, k, "dot") for k, d in enumerate(dots, 1)]
     prob_grad = sum(
         jnp.where(ids == (place ^ k), d.reshape(-1, 1), 0.0) for k, d in enumerate(dots)
     )
     return (
         upstream[None],
         prob_grad[None],
-        v["own_g"][None, None],
-        v["own_u"][None, None],
-        v["own_n"][None, None],
+        v.own_g[None, None],
+        v.own_u[None, None],
+        v.own_n[None, None],
     )
 
 

time: 135 us -> 132 us (0.978)
  waiting for transfers between devices: 42.5 us -> 50.6 us
  matrix products: 28.3 us -> 21.4 us
  starting transfers between devices: 44.5 us -> 38.3 us
  Pallas kernels: 0.45 us -> 3.19 us
  local copies, waits for them, and re-layouts: 6.61 us -> 4.77 us
    ppermute x28 -> x26, waiting for transfers between devices: 42.5 us -> 50.6 us  [over(): return lax.ppermute(x, axis, pairs)]
    dot_general x24 -> x17, matrix products: 28.3 us -> 21.4 us  [mm(): return lax.dot_general(a, b, (dims, ((), ())), preferred_element_type=F32)]
    ppermute x28 -> x26, starting transfers between devices: 44.5 us -> 38.3 us  [over(): return lax.ppermute(x, axis, pairs)]
    pallas_call x1 -> x2, Pallas kernels: 0.45 us -> 3.19 us  [gather(): pl.pallas_call(functools.partial(gather_kernel, [piece[1:] for piece in p...]
    unnamed x33 -> x22, local copies, waits for them, and re-layouts: 6.29 us -> 3.68 us
  transfers between devices with their start and end apart: 28 -> 26, of which waited for: 12 -> 11; matrix products, arithmetic and copies ran while one was open for 29% -> 25% of each run, Pallas kernels for 0% -> 2%
where the time goes in v4:
time: 132 us; the launch traced here: 131 us
  waiting for transfers between devices  50.6 us (38%)
  starting transfers between devices  38.3 us (29%)
  matrix products  21.4 us (16%)
  other arithmetic  11.3 us (9%)
  local copies, waits for them, and re-layouts  4.77 us (4%)
  Pallas kernels  3.19 us (2%)
    ppermute x26, waiting for transfers between devices, over(): return lax.ppermute(x, axis, pairs)  50.6 us
    ppermute x26, starting transfers between devices, over(): return lax.ppermute(x, axis, pairs)  38.3 us
    dot_general x17, matrix products, mm(): return lax.dot_general(a, b, (dims, ((), ())), preferred_element_type=F32)  21.4 us
    unnamed x22, local copies, waits for them, and re-layouts  3.68 us
    pallas_call x2, Pallas kernels, gather(): pl.pallas_call(functools.partial(gather_kernel, [piece[1:] for piece in p...  3.19 us
  transfers between devices with their start and end apart: 26, of which 11 were waited for; matrix products, arithmetic and copies ran while one was open for 25% of the time, Pallas kernels for 2%

profile of v4, /device:TPU:0, one launch (start us, length us, event | category | flops | bytes accessed | tf_op | source)
XLA Modules:
  0.0 130.8 jit_solution(2280565343381650729)
XLA Ops:
  1.4 1.5 %collective-permute-start.3 = (bf16[128,2048]{1,0:T(8,128)(2,1)}, bf16[128,2048]{1,0:T(8,128)(2,1)}, u32[]{:S(2)}, u32[]{:S(2)}) collective-permute-start(bf16[128,2048]{1,0:T(8,128)(2,1)} %bitcast.53), channel_id=1, source_target_pairs={{1,2},{2,1},{5,6},{6,5},{9,10},{10,9},{13,14},{14,13},{17,18},{18,... | collective-permute-start | bytes 1572872 | tf_op jit(solution)/shard_map/t_mid_in/ppermute | solution.py:201
  2.8 5.1 %collective-permute-start.4 = (bf16[128,2048]{1,0:T(8,128)(2,1)}, bf16[128,2048]{1,0:T(8,128)(2,1)}, u32[]{:S(2)}, u32[]{:S(2)}) collective-permute-start(bf16[128,2048]{1,0:T(8,128)(2,1)} %bitcast.54), channel_id=1, source_target_pairs={{0,1},{3,2},{1,0},{2,3},{4,5},{7,6},{5,4},{6,7},{8,9},{11,10},{9,8... | collective-permute-start | bytes 1572872 | tf_op jit(solution)/shard_map/t_near/ppermute | solution.py:201
  8.4 1.9 %collective-permute-start.1 = (f32[1,128]{1,0:T(1,128)S(1)}, f32[1,128]{1,0:T(1,128)S(1)}, u32[]{:S(2)}, u32[]{:S(2)}) collective-permute-start(f32[1,128]{1,0:T(1,128)S(1)} %bitcast.78), channel_id=1, source_target_pairs={{0,3},{1,2},{2,1},{3,0},{4,7},{5,6},{6,5},{7,4},{8,11},{9,10},{10,... | collective-permute-start | bytes 1544 | tf_op jit(solution)/shard_map/p/ppermute | solution.py:201
  10.4 1.0 collective-permute-start.2
  11.4 1.4 %copy-done = bf16[1,1,2048,384]{3,2,1,0:T(8,128)(2,1)S(1)} copy-done((bf16[1,1,2048,384]{3,2,1,0:T(8,128)(2,1)S(1)}, bf16[1,1,2048,384]{3,2,1,0:T(8,128)(2,1)}, u32[]{:S(2)}) %copy-start) | copy-done | bytes 1572888
  12.8 1.4 %copy-done.1 = bf16[1,1,2048,384]{3,2,1,0:T(8,128)(2,1)S(1)} copy-done((bf16[1,1,2048,384]{3,2,1,0:T(8,128)(2,1)S(1)}, bf16[1,1,2048,384]{3,2,1,0:T(8,128)(2,1)}, u32[]{:S(2)}) %copy-start.1) | copy-done | bytes 1572888
  14.6 5.0 %collective-permute-done = f32[1,128]{1,0:T(1,128)S(1)} collective-permute-done((f32[1,128]{1,0:T(1,128)S(1)}, f32[1,128]{1,0:T(1,128)S(1)}, u32[]{:S(2)}, u32[]{:S(2)}) %collective-permute-start) | collective-permute-done | bytes 544 | tf_op jit(solution)/shard_map/p/ppermute | solution.py:201
  19.6 1.3 collective-permute-done.1
  22.2 1.5 %collective-permute-start.8 = (bf16[128,2048]{1,0:T(8,128)(2,1)}, bf16[128,2048]{1,0:T(8,128)(2,1)}, u32[]{:S(2)}, u32[]{:S(2)}) collective-permute-start(bf16[128,2048]{1,0:T(8,128)(2,1)} %collective-permute-done.4), channel_id=1, source_target_pairs={{1,2},{2,1},{5,6},{6,5},{9,10},{10,9},{13,14},{14,13},{17,18},{18,... | collective-permute-start | bytes 1572872 | tf_op jit(solution)/shard_map/t_far_in/ppermute | solution.py:201
  23.7 1.1 constant_dynamic-update-slice_fusion
  24.8 1.3 collective-permute-start.10
  26.1 1.9 %fusion.45 = f32[768,256]{1,0:T(8,128)} fusion(bf16[2048,768]{1,0:T(8,128)(2,1)S(1)} %own_w.1, bf16[256,2048]{1,0:T(8,128)(2,1)S(1)} %constant_dynamic-update-slice_fusion), kind=kOutput, calls=%fused_computation.126 | convolution fusion | flops 805306368 | bytes 4980736 | tf_op jit(solution)/shard_map/ahead/dot_general | solution.py:204
  28.0 8.3 %collective-permute-done.5 = bf16[128,2048]{1,0:T(8,128)(2,1)} collective-permute-done((bf16[128,2048]{1,0:T(8,128)(2,1)S(1)}, bf16[128,2048]{1,0:T(8,128)(2,1)}, u32[]{:S(2)}, u32[]{:S(2)}) %collective-permute-start.5) | collective-permute-done | bytes 524320 | tf_op jit(solution)/shard_map/g_near/ppermute | solution.py:201
  36.3 1.5 %collective-permute-start.9 = (bf16[128,2048]{1,0:T(8,128)(2,1)}, bf16[128,2048]{1,0:T(8,128)(2,1)}, u32[]{:S(2)}, u32[]{:S(2)}) collective-permute-start(bf16[128,2048]{1,0:T(8,128)(2,1)} %collective-permute-done.5), channel_id=1, source_target_pairs={{1,2},{2,1},{5,6},{6,5},{9,10},{10,9},{13,14},{14,13},{17,18},{18,... | collective-permute-start | bytes 1572872 | tf_op jit(solution)/shard_map/g_far_in/ppermute | solution.py:201
  37.8 1.4 %collective-permute-start.11 = (bf16[128,2048]{1,0:T(8,128)(2,1)}, bf16[128,2048]{1,0:T(8,128)(2,1)S(1)}, u32[]{:S(2)}, u32[]{:S(2)}) collective-permute-start(bf16[128,2048]{1,0:T(8,128)(2,1)} %collective-permute-done.8), channel_id=1, source_target_pairs={{1,0},{2,3},{5,4},{6,7},{9,8},{10,11},{13,12},{14,15},{17,16},{18,... | collective-permute-start | bytes 1572872 | tf_op jit(solution)/shard_map/t_far_out/ppermute | solution.py:201
  39.2 2.9 %sib_w.1 = (bf16[2048,768]{1,0:T(8,128)(2,1)S(1)}, bf16[768,2048]{1,0:T(8,128)(2,1)S(1)}) custom-call(bf16[2048,768]{1,0:T(8,128)(2,1)} %collective-permute-done.7.refs_0_, bf16[384,2048]{1,0:T(8,128)(2,1)} %bitcast.6.refs_1_, bf16[384,2048]{1,0:T(8,128)(2,1)} %collective-permute-done.6.refs_2_), custom_call_target="tpu_custom_call" | custom-call | bytes 1048576 | tf_op jit(solution)/shard_map/sib_w/pallas_call | solution.py:179
  42.1 1.0 fusion.46
  43.2 4.4 %collective-permute-done.10 = bf16[128,2048]{1,0:T(8,128)(2,1)} collective-permute-done((bf16[128,2048]{1,0:T(8,128)(2,1)}, bf16[128,2048]{1,0:T(8,128)(2,1)}, u32[]{:S(2)}, u32[]{:S(2)}) %collective-permute-start.10) | collective-permute-done | bytes 524320 | tf_op jit(solution)/shard_map/t_mid_out/ppermute | solution.py:201
  48.3 1.3 collective-permute-start.13
  49.6 2.1 %fusion.3 = f32[768,256]{1,0:T(8,128)S(1)} fusion(bf16[768,2048]{1,0:T(8,128)(2,1)S(1)} %get-tuple-element.700, bf16[128,2048]{1,0:T(8,128)(2,1)} %collective-permute-done.5, bf16[128,2048]{1,0:T(8,128)(2,1)S(1)} %bitcast.65), kind=kOutput, calls=%fused_computation.14 | convolution fusion | flops 807403520 | bytes 4980736 | tf_op jit(solution)/shard_map/behind/dot_general | solution.py:204
  52.4 1.0 fusion.44
  53.5 1.1 fusion
  54.6 4.1 %collective-permute-done.11 = bf16[128,2048]{1,0:T(8,128)(2,1)S(1)} collective-permute-done((bf16[128,2048]{1,0:T(8,128)(2,1)}, bf16[128,2048]{1,0:T(8,128)(2,1)S(1)}, u32[]{:S(2)}, u32[]{:S(2)}) %collective-permute-start.11) | collective-permute-done | bytes 524320 | tf_op jit(solution)/shard_map/t_far_out/ppermute | solution.py:201
  58.8 1.1 broadcast_select_fusion.3
  59.9 1.0 fusion.18
  61.9 1.5 %collective-permute-start.14 = (bf16[128,2048]{1,0:T(8,128)(2,1)S(1)}, bf16[128,2048]{1,0:T(8,128)(2,1)S(1)}, u32[]{:S(2)}, u32[]{:S(2)}) collective-permute-start(bf16[128,2048]{1,0:T(8,128)(2,1)S(1)} %collective-permute-done.12), channel_id=1, source_target_pairs={{1,0},{2,3},{5,4},{6,7},{9,8},{10,11},{13,12},{14,15},{17,16},{18,... | collective-permute-start | bytes 1572872 | tf_op jit(solution)/shard_map/g_mid_out/ppermute | solution.py:201
  63.4 1.3 pad_maximum_fusion
  64.7 5.2 %collective-permute-done.13 = bf16[128,2048]{1,0:T(8,128)(2,1)S(1)} collective-permute-done((bf16[128,2048]{1,0:T(8,128)(2,1)}, bf16[128,2048]{1,0:T(8,128)(2,1)S(1)}, u32[]{:S(2)}, u32[]{:S(2)}) %collective-permute-start.13) | collective-permute-done | bytes 524320 | tf_op jit(solution)/shard_map/g_far_out/ppermute | solution.py:201
  71.4 1.2 fusion.43
  72.6 1.2 fusion.1
  73.8 1.6 %collective-permute-start.15 = (bf16[128,2048]{1,0:T(8,128)(2,1)S(1)}, bf16[128,2048]{1,0:T(8,128)(2,1)S(1)}, u32[]{:S(2)}, u32[]{:S(2)}) collective-permute-start(bf16[128,2048]{1,0:T(8,128)(2,1)S(1)} %fusion.1), channel_id=1, source_target_pairs={{0,1},{3,2},{4,5},{7,6},{8,9},{11,10},{12,13},{15,14},{16,17},{19,... | collective-permute-start | bytes 1572872 | tf_op jit(solution)/shard_map/r5/ppermute | solution.py:201
  75.4 4.9 %collective-permute-done.14 = bf16[128,2048]{1,0:T(8,128)(2,1)S(1)} collective-permute-done((bf16[128,2048]{1,0:T(8,128)(2,1)S(1)}, bf16[128,2048]{1,0:T(8,128)(2,1)S(1)}, u32[]{:S(2)}, u32[]{:S(2)}) %collective-permute-start.14) | collective-permute-done | bytes 524320 | tf_op jit(solution)/shard_map/g_mid_out/ppermute | solution.py:201
  81.7 1.2 fusion.42
  82.9 1.2 fusion.2
  84.1 2.5 %collective-permute-start.16 = (bf16[128,2048]{1,0:T(8,128)(2,1)S(1)}, bf16[128,2048]{1,0:T(8,128)(2,1)S(1)}, u32[]{:S(2)}, u32[]{:S(2)}) collective-permute-start(bf16[128,2048]{1,0:T(8,128)(2,1)S(1)} %fusion.2), channel_id=1, source_target_pairs={{0,1},{3,2},{4,5},{7,6},{8,9},{11,10},{12,13},{15,14},{16,17},{19,... | collective-permute-start | bytes 1572872 | tf_op jit(solution)/shard_map/r4/ppermute | solution.py:201
  87.5 1.3 pad_maximum_fusion.1
  89.8 1.9 %convolution_convert_fusion.1 = bf16[2048,768]{1,0:T(8,128)(2,1)S(1)} fusion(bf16[2048,512]{0,1:T(8,128)(2,1)S(1)} %pad_maximum_fusion, bf16[768,128]{1,0:T(8,128)(2,1)S(1)} %pad_maximum_fusion.8, bf16[768,128]{1,0:T(8,128)(2,1)S(1)} %pad_maximum_fusion.10, bf16[768,256]{1,0:T(8,128)(2,1)S(1)} %get-tuple-element.810), kind=kOutput, calls=%fused_computation.1 | convolution fusion | flops 1614544896 | bytes 6029312 | tf_op jit(solution)/shard_map/weight_grads/dot_general | solution.py:204
  91.6 5.5 %collective-permute-done.16 = bf16[128,2048]{1,0:T(8,128)(2,1)S(1)} collective-permute-done((bf16[128,2048]{1,0:T(8,128)(2,1)S(1)}, bf16[128,2048]{1,0:T(8,128)(2,1)S(1)}, u32[]{:S(2)}, u32[]{:S(2)}) %collective-permute-start.16) | collective-permute-done | bytes 524320 | tf_op jit(solution)/shard_map/r4/ppermute | solution.py:201
  97.9 3.9 %collective-permute-start.18 = (bf16[128,2048]{1,0:T(8,128)(2,1)S(1)}, bf16[128,2048]{1,0:T(8,128)(2,1)S(1)}, u32[]{:S(2)}, u32[]{:S(2)}) collective-permute-start(bf16[128,2048]{1,0:T(8,128)(2,1)S(1)} %slice_add_fusion.2), channel_id=1, source_target_pairs={{0,1},{3,2},{1,0},{2,3},{4,5},{7,6},{5,4},{6,7},{8,9},{11,10},{9,8... | collective-permute-start | bytes 1572872 | tf_op jit(solution)/shard_map/r1/ppermute | solution.py:201
  103.8 1.9 %convolution_convert_fusion = bf16[2048,768]{1,0:T(8,128)(2,1)S(1)} fusion(bf16[2048,512]{0,1:T(8,128)(2,1)S(1)} %pad_maximum_fusion, bf16[768,128]{1,0:T(8,128)(2,1)S(1)} %pad_maximum_fusion.7, bf16[768,128]{1,0:T(8,128)(2,1)S(1)} %pad_maximum_fusion.9, bf16[768,256]{1,0:T(8,128)(2,1)S(1)} %get-tuple-element.872), kind=kOutput, calls=%fused_computation | convolution fusion | flops 1614544896 | bytes 6029312 | tf_op jit(solution)/shard_map/weight_grads/dot_general | solution.py:204
  105.6 8.4 %collective-permute-done.18 = bf16[128,2048]{1,0:T(8,128)(2,1)S(1)} collective-permute-done((bf16[128,2048]{1,0:T(8,128)(2,1)S(1)}, bf16[128,2048]{1,0:T(8,128)(2,1)S(1)}, u32[]{:S(2)}, u32[]{:S(2)}) %collective-permute-start.18) | collective-permute-done | bytes 524320 | tf_op jit(solution)/shard_map/r1/ppermute | solution.py:201
  114.3 2.5 %collective-permute-start.20 = (bf16[128,2048]{1,0:T(8,128)(2,1)S(1)}, bf16[128,2048]{1,0:T(8,128)(2,1)S(1)}, u32[]{:S(2)}, u32[]{:S(2)}) collective-permute-start(bf16[128,2048]{1,0:T(8,128)(2,1)S(1)} %add_convert_fusion), channel_id=1, source_target_pairs={{0,24},{8,0},{16,8},{24,16},{1,25},{9,1},{17,9},{25,17},{2,26},{10... | collective-permute-start | bytes 1572872 | tf_op jit(solution)/shard_map/up/ppermute | solution.py:201
  116.8 2.2 %slice_add_fusion = (bf16[2048,384]{1,0:T(8,128)(2,1)}, bf16[2048,384]{1,0:T(8,128)(2,1)}) fusion(bf16[2048,768]{1,0:T(8,128)(2,1)S(1)} %collective-permute-done.22, bf16[2048,768]{1,0:T(8,128)(2,1)S(1)} %convolution_convert_fusion), kind=kLoop, calls=%fused_computation.12 | loop fusion | flops 1572864 | bytes 9437184 | tf_op jit(solution)/shard_map/add | solution.py:363
  119.0 1.8 %add.150 = bf16[384,2048]{1,0:T(8,128)(2,1)} add(bf16[384,2048]{1,0:T(8,128)(2,1)S(1)} %convolution_convert_fusion.2, bf16[384,2048]{1,0:T(8,128)(2,1)S(1)} %collective-permute-done.21) | non-fusion elementwise | flops 786432 | bytes 4718592 | tf_op jit(solution)/shard_map/add | solution.py:361
  120.8 2.5 %collective-permute-start.25 = (f32[1,128]{1,0:T(1,128)S(1)}, f32[1,128]{1,0:T(1,128)S(1)}, u32[]{:S(2)}, u32[]{:S(2)}) collective-permute-start(f32[1,128]{1,0:T(1,128)S(1)} %add_bitcast_fusion.1), channel_id=1, source_target_pairs={{0,3},{1,2},{2,1},{3,0},{4,7},{5,6},{6,5},{7,4},{8,11},{9,10},{10,... | collective-permute-start | bytes 1544 | tf_op jit(solution)/shard_map/dot/ppermute | solution.py:201
  123.3 2.6 %collective-permute-start.24 = (f32[1,128]{1,0:T(1,128)S(1)}, f32[1,128]{1,0:T(1,128)S(1)}, u32[]{:S(2)}, u32[]{:S(2)}) collective-permute-start(f32[1,128]{1,0:T(1,128)S(1)} %add_bitcast_fusion), channel_id=1, source_target_pairs={{0,2},{1,3},{2,0},{3,1},{4,6},{5,7},{6,4},{7,5},{8,10},{9,11},{10,... | collective-permute-start | bytes 1544 | tf_op jit(solution)/shard_map/dot/ppermute | solution.py:201
  126.0 1.7 %collective-permute-done.20 = bf16[128,2048]{1,0:T(8,128)(2,1)S(1)} collective-permute-done((bf16[128,2048]{1,0:T(8,128)(2,1)S(1)}, bf16[128,2048]{1,0:T(8,128)(2,1)S(1)}, u32[]{:S(2)}, u32[]{:S(2)}) %collective-permute-start.20) | collective-permute-done | bytes 524320 | tf_op jit(solution)/shard_map/up/ppermute | solution.py:201
  127.7 1.7 %collective-permute-done.23 = f32[1,128]{1,0:T(1,128)S(1)} collective-permute-done((f32[1,128]{1,0:T(1,128)S(1)}, f32[1,128]{1,0:T(1,128)S(1)}, u32[]{:S(2)}, u32[]{:S(2)}) %collective-permute-start.23) | collective-permute-done | bytes 544 | tf_op jit(solution)/shard_map/dot/ppermute | solution.py:201
  (76 shorter events, 14.6 us)
Async XLA Ops:
  1.4 19.5 %collective-permute-start.3 = (bf16[128,2048]{1,0:T(8,128)(2,1)}, bf16[128,2048]{1,0:T(8,128)(2,1)}, u32[]{:S(2)}, u32[]{:S(2)}) collective-permute-start(bf16[128,2048]{1,0:T(8,128)(2,1)} %bitcast.53), channel_id=1, source_target_pairs={{1,2},{2,1},{5,6},{6,5},{9,10},{10,9},{13,14},{14,13},{17,18},{18,... | collective-permute-start | bytes 1572872 | tf_op jit(solution)/shard_map/t_mid_in/ppermute | solution.py:201
  2.8 18.0 %collective-permute-start.4 = (bf16[128,2048]{1,0:T(8,128)(2,1)}, bf16[128,2048]{1,0:T(8,128)(2,1)}, u32[]{:S(2)}, u32[]{:S(2)}) collective-permute-start(bf16[128,2048]{1,0:T(8,128)(2,1)} %bitcast.54), channel_id=1, source_target_pairs={{0,1},{3,2},{1,0},{2,3},{4,5},{7,6},{5,4},{6,7},{8,9},{11,10},{9,8... | collective-permute-start | bytes 1572872 | tf_op jit(solution)/shard_map/t_near/ppermute | solution.py:201
  7.9 11.6 %collective-permute-start = (f32[1,128]{1,0:T(1,128)S(1)}, f32[1,128]{1,0:T(1,128)S(1)}, u32[]{:S(2)}, u32[]{:S(2)}) collective-permute-start(f32[1,128]{1,0:T(1,128)S(1)} %bitcast.79), channel_id=1, source_target_pairs={{0,2},{1,3},{2,0},{3,1},{4,6},{5,7},{6,4},{7,5},{8,10},{9,11},{10,... | collective-permute-start | bytes 1544 | tf_op jit(solution)/shard_map/p/ppermute | solution.py:201
  8.4 12.4 %collective-permute-start.1 = (f32[1,128]{1,0:T(1,128)S(1)}, f32[1,128]{1,0:T(1,128)S(1)}, u32[]{:S(2)}, u32[]{:S(2)}) collective-permute-start(f32[1,128]{1,0:T(1,128)S(1)} %bitcast.78), channel_id=1, source_target_pairs={{0,3},{1,2},{2,1},{3,0},{4,7},{5,6},{6,5},{7,4},{8,11},{9,10},{10,... | collective-permute-start | bytes 1544 | tf_op jit(solution)/shard_map/p/ppermute | solution.py:201
  10.4 10.5 %collective-permute-start.2 = (f32[1,128]{1,0:T(1,128)S(1)}, f32[1,128]{1,0:T(1,128)S(1)}, u32[]{:S(2)}, u32[]{:S(2)}) collective-permute-start(f32[1,128]{1,0:T(1,128)S(1)} %bitcast.76), channel_id=1, source_target_pairs={{0,1},{1,0},{2,3},{3,2},{4,5},{5,4},{6,7},{7,6},{8,9},{9,8},{10,11... | collective-permute-start | bytes 1544 | tf_op jit(solution)/shard_map/p/ppermute | solution.py:201
  11.4 1.4 %copy-start = (bf16[1,1,2048,384]{3,2,1,0:T(8,128)(2,1)S(1)}, bf16[1,1,2048,384]{3,2,1,0:T(8,128)(2,1)}, u32[]{:S(2)}) copy-start(bf16[1,1,2048,384]{3,2,1,0:T(8,128)(2,1)} %param.11) | copy-start | bytes 4718596
  12.8 1.4 %copy-start.1 = (bf16[1,1,2048,384]{3,2,1,0:T(8,128)(2,1)S(1)}, bf16[1,1,2048,384]{3,2,1,0:T(8,128)(2,1)}, u32[]{:S(2)}) copy-start(bf16[1,1,2048,384]{3,2,1,0:T(8,128)(2,1)} %param.12) | copy-start | bytes 4718596
  14.2 7.2 %copy-start.5 = (bf16[1,128,2048]{2,1,0:T(8,128)(2,1)S(1)}, bf16[1,128,2048]{2,1,0:T(8,128)(2,1)}, u32[]{:S(2)}) copy-start(bf16[1,128,2048]{2,1,0:T(8,128)(2,1)} %param.8) | copy-start | bytes 1572868
  14.2 9.4 %copy-start.3 = (bf16[1,128,2048]{2,1,0:T(8,128)(2,1)S(1)}, bf16[1,128,2048]{2,1,0:T(8,128)(2,1)}, u32[]{:S(2)}) copy-start(bf16[1,128,2048]{2,1,0:T(8,128)(2,1)} %param.7) | copy-start | bytes 1572868
  20.9 16.9 %collective-permute-start.7 = (bf16[2048,768]{1,0:T(8,128)(2,1)S(1)}, bf16[2048,768]{1,0:T(8,128)(2,1)}, u32[]{:S(2)}, u32[]{:S(2)}) collective-permute-start(bf16[2048,768]{1,0:T(8,128)(2,1)S(1)} %own_w.1), channel_id=1, source_target_pairs={{0,4},{4,0},{1,5},{5,1},{2,6},{6,2},{3,7},{7,3},{8,12},{12,8},{9,1... | collective-permute-start | bytes 9437192 | tf_op jit(solution)/shard_map/sib_w/ppermute | solution.py:201
  20.9 16.9 %collective-permute-start.6 = (bf16[384,2048]{1,0:T(8,128)(2,1)}, bf16[384,2048]{1,0:T(8,128)(2,1)}, u32[]{:S(2)}, u32[]{:S(2)}) collective-permute-start(bf16[384,2048]{1,0:T(8,128)(2,1)} %bitcast.6.refs_1_), channel_id=1, source_target_pairs={{0,4},{4,0},{1,5},{5,1},{2,6},{6,2},{3,7},{7,3},{8,12},{12,8},{9,1... | collective-permute-start | bytes 4718600 | tf_op jit(solution)/shard_map/sib_d/ppermute | solution.py:201
  21.4 14.9 %collective-permute-start.5 = (bf16[128,2048]{1,0:T(8,128)(2,1)S(1)}, bf16[128,2048]{1,0:T(8,128)(2,1)}, u32[]{:S(2)}, u32[]{:S(2)}) collective-permute-start(bf16[128,2048]{1,0:T(8,128)(2,1)S(1)} %bitcast.63), channel_id=1, source_target_pairs={{0,1},{3,2},{1,0},{2,3},{4,5},{7,6},{5,4},{6,7},{8,9},{11,10},{9,8... | collective-permute-start | bytes 1572872 | tf_op jit(solution)/shard_map/g_near/ppermute | solution.py:201
  22.2 15.6 %collective-permute-start.8 = (bf16[128,2048]{1,0:T(8,128)(2,1)}, bf16[128,2048]{1,0:T(8,128)(2,1)}, u32[]{:S(2)}, u32[]{:S(2)}) collective-permute-start(bf16[128,2048]{1,0:T(8,128)(2,1)} %collective-permute-done.4), channel_id=1, source_target_pairs={{1,2},{2,1},{5,6},{6,5},{9,10},{10,9},{13,14},{14,13},{17,18},{18,... | collective-permute-start | bytes 1572872 | tf_op jit(solution)/shard_map/t_far_in/ppermute | solution.py:201
  24.8 11.6 %copy-start.7 = (bf16[256,2048]{1,0:T(8,128)(2,1)}, bf16[256,2048]{1,0:T(8,128)(2,1)S(1)}, u32[]{:S(2)}) copy-start(bf16[256,2048]{1,0:T(8,128)(2,1)S(1)} %constant_dynamic-update-slice_fusion) | copy-start | bytes 3145732
  24.8 22.8 %collective-permute-start.10 = (bf16[128,2048]{1,0:T(8,128)(2,1)}, bf16[128,2048]{1,0:T(8,128)(2,1)}, u32[]{:S(2)}, u32[]{:S(2)}) collective-permute-start(bf16[128,2048]{1,0:T(8,128)(2,1)} %collective-permute-done.3), channel_id=1, source_target_pairs={{1,0},{2,3},{5,4},{6,7},{9,8},{10,11},{13,12},{14,15},{17,16},{18,... | collective-permute-start | bytes 1572872 | tf_op jit(solution)/shard_map/t_mid_out/ppermute | solution.py:201
  36.3 11.2 %collective-permute-start.9 = (bf16[128,2048]{1,0:T(8,128)(2,1)}, bf16[128,2048]{1,0:T(8,128)(2,1)}, u32[]{:S(2)}, u32[]{:S(2)}) collective-permute-start(bf16[128,2048]{1,0:T(8,128)(2,1)} %collective-permute-done.5), channel_id=1, source_target_pairs={{1,2},{2,1},{5,6},{6,5},{9,10},{10,9},{13,14},{14,13},{17,18},{18,... | collective-permute-start | bytes 1572872 | tf_op jit(solution)/shard_map/g_far_in/ppermute | solution.py:201
  37.8 4.3 %copy-start.8 = (bf16[256,2048]{1,0:T(8,128)(2,1)S(1)}, bf16[256,2048]{1,0:T(8,128)(2,1)}, u32[]{:S(2)}) copy-start(bf16[256,2048]{1,0:T(8,128)(2,1)} %copy-done.7) | copy-start | bytes 3145732
  37.8 20.9 %collective-permute-start.11 = (bf16[128,2048]{1,0:T(8,128)(2,1)}, bf16[128,2048]{1,0:T(8,128)(2,1)S(1)}, u32[]{:S(2)}, u32[]{:S(2)}) collective-permute-start(bf16[128,2048]{1,0:T(8,128)(2,1)} %collective-permute-done.8), channel_id=1, source_target_pairs={{1,0},{2,3},{5,4},{6,7},{9,8},{10,11},{13,12},{14,15},{17,16},{18,... | collective-permute-start | bytes 1572872 | tf_op jit(solution)/shard_map/t_far_out/ppermute | solution.py:201
  42.1 5.5 %copy-start.6 = (bf16[1,128,2048]{2,1,0:T(8,128)(2,1)S(1)}, bf16[1,128,2048]{2,1,0:T(8,128)(2,1)}, u32[]{:S(2)}) copy-start(bf16[1,128,2048]{2,1,0:T(8,128)(2,1)} %param.8) | copy-start | bytes 1572868
  43.1 8.5 %copy-start.2 = (f32[768,256]{1,0:T(8,128)S(1)}, f32[768,256]{1,0:T(8,128)}, u32[]{:S(2)}) copy-start(f32[768,256]{1,0:T(8,128)} %fusion.45) | copy-start | bytes 2359300
  47.6 14.4 %collective-permute-start.12 = (bf16[128,2048]{1,0:T(8,128)(2,1)S(1)}, bf16[128,2048]{1,0:T(8,128)(2,1)S(1)}, u32[]{:S(2)}, u32[]{:S(2)}) collective-permute-start(bf16[128,2048]{1,0:T(8,128)(2,1)S(1)} %bitcast.64), channel_id=1, source_target_pairs={{1,2},{2,1},{5,6},{6,5},{9,10},{10,9},{13,14},{14,13},{17,18},{18,... | collective-permute-start | bytes 1572872 | tf_op jit(solution)/shard_map/g_mid_in/ppermute | solution.py:201
  48.3 21.7 %collective-permute-start.13 = (bf16[128,2048]{1,0:T(8,128)(2,1)}, bf16[128,2048]{1,0:T(8,128)(2,1)S(1)}, u32[]{:S(2)}, u32[]{:S(2)}) collective-permute-start(bf16[128,2048]{1,0:T(8,128)(2,1)} %collective-permute-done.9), channel_id=1, source_target_pairs={{1,0},{2,3},{5,4},{6,7},{9,8},{10,11},{13,12},{14,15},{17,16},{18,... | collective-permute-start | bytes 1572872 | tf_op jit(solution)/shard_map/g_far_out/ppermute | solution.py:201
  60.9 2.5 %copy-start.4 = (bf16[1,128,2048]{2,1,0:T(8,128)(2,1)S(1)}, bf16[1,128,2048]{2,1,0:T(8,128)(2,1)}, u32[]{:S(2)}) copy-start(bf16[1,128,2048]{2,1,0:T(8,128)(2,1)} %param.7) | copy-start | bytes 1572868
  61.9 18.3 %collective-permute-start.14 = (bf16[128,2048]{1,0:T(8,128)(2,1)S(1)}, bf16[128,2048]{1,0:T(8,128)(2,1)S(1)}, u32[]{:S(2)}, u32[]{:S(2)}) collective-permute-start(bf16[128,2048]{1,0:T(8,128)(2,1)S(1)} %collective-permute-done.12), channel_id=1, source_target_pairs={{1,0},{2,3},{5,4},{6,7},{9,8},{10,11},{13,12},{14,15},{17,16},{18,... | collective-permute-start | bytes 1572872 | tf_op jit(solution)/shard_map/g_mid_out/ppermute | solution.py:201
  73.8 12.9 %collective-permute-start.15 = (bf16[128,2048]{1,0:T(8,128)(2,1)S(1)}, bf16[128,2048]{1,0:T(8,128)(2,1)S(1)}, u32[]{:S(2)}, u32[]{:S(2)}) collective-permute-start(bf16[128,2048]{1,0:T(8,128)(2,1)S(1)} %fusion.1), channel_id=1, source_target_pairs={{0,1},{3,2},{4,5},{7,6},{8,9},{11,10},{12,13},{15,14},{16,17},{19,... | collective-permute-start | bytes 1572872 | tf_op jit(solution)/shard_map/r5/ppermute | solution.py:201
  84.1 13.1 %collective-permute-start.16 = (bf16[128,2048]{1,0:T(8,128)(2,1)S(1)}, bf16[128,2048]{1,0:T(8,128)(2,1)S(1)}, u32[]{:S(2)}, u32[]{:S(2)}) collective-permute-start(bf16[128,2048]{1,0:T(8,128)(2,1)S(1)} %fusion.2), channel_id=1, source_target_pairs={{0,1},{3,2},{4,5},{7,6},{8,9},{11,10},{12,13},{15,14},{16,17},{19,... | collective-permute-start | bytes 1572872 | tf_op jit(solution)/shard_map/r4/ppermute | solution.py:201
  86.8 10.4 %collective-permute-start.17 = (bf16[128,2048]{1,0:T(8,128)(2,1)S(1)}, bf16[128,2048]{1,0:T(8,128)(2,1)S(1)}, u32[]{:S(2)}, u32[]{:S(2)}) collective-permute-start(bf16[128,2048]{1,0:T(8,128)(2,1)S(1)} %add.144), channel_id=1, source_target_pairs={{1,2},{2,1},{5,6},{6,5},{9,10},{10,9},{13,14},{14,13},{17,18},{18,... | collective-permute-start | bytes 1572872 | tf_op jit(solution)/shard_map/r3/ppermute | solution.py:201
  97.4 19.4 %collective-permute-start.22 = (bf16[2048,768]{1,0:T(8,128)(2,1)S(1)}, bf16[2048,768]{1,0:T(8,128)(2,1)S(1)}, u32[]{:S(2)}, u32[]{:S(2)}) collective-permute-start(bf16[2048,768]{1,0:T(8,128)(2,1)S(1)} %convolution_convert_fusion.1), channel_id=1, source_target_pairs={{0,4},{4,0},{1,5},{5,1},{2,6},{6,2},{3,7},{7,3},{8,12},{12,8},{9,1... | collective-permute-start | bytes 9437192 | tf_op jit(solution)/shard_map/got_gu/ppermute | solution.py:201
  97.4 19.3 %collective-permute-start.21 = (bf16[384,2048]{1,0:T(8,128)(2,1)S(1)}, bf16[384,2048]{1,0:T(8,128)(2,1)S(1)}, u32[]{:S(2)}, u32[]{:S(2)}) collective-permute-start(bf16[384,2048]{1,0:T(8,128)(2,1)S(1)} %convolution_convert_fusion.3), channel_id=1, source_target_pairs={{0,4},{4,0},{1,5},{5,1},{2,6},{6,2},{3,7},{7,3},{8,12},{12,8},{9,1... | collective-permute-start | bytes 4718600 | tf_op jit(solution)/shard_map/got_dn/ppermute | solution.py:201
  97.9 16.1 %collective-permute-start.18 = (bf16[128,2048]{1,0:T(8,128)(2,1)S(1)}, bf16[128,2048]{1,0:T(8,128)(2,1)S(1)}, u32[]{:S(2)}, u32[]{:S(2)}) collective-permute-start(bf16[128,2048]{1,0:T(8,128)(2,1)S(1)} %slice_add_fusion.2), channel_id=1, source_target_pairs={{0,1},{3,2},{1,0},{2,3},{4,5},{7,6},{5,4},{6,7},{8,9},{11,10},{9,8... | collective-permute-start | bytes 1572872 | tf_op jit(solution)/shard_map/r1/ppermute | solution.py:201
  101.9 12.2 %collective-permute-start.19 = (bf16[128,2048]{1,0:T(8,128)(2,1)S(1)}, bf16[128,2048]{1,0:T(8,128)(2,1)S(1)}, u32[]{:S(2)}, u32[]{:S(2)}) collective-permute-start(bf16[128,2048]{1,0:T(8,128)(2,1)S(1)} %add.146), channel_id=1, source_target_pairs={{1,2},{2,1},{5,6},{6,5},{9,10},{10,9},{13,14},{14,13},{17,18},{18,... | collective-permute-start | bytes 1572872 | tf_op jit(solution)/shard_map/r2/ppermute | solution.py:201
  114.3 13.4 %collective-permute-start.20 = (bf16[128,2048]{1,0:T(8,128)(2,1)S(1)}, bf16[128,2048]{1,0:T(8,128)(2,1)S(1)}, u32[]{:S(2)}, u32[]{:S(2)}) collective-permute-start(bf16[128,2048]{1,0:T(8,128)(2,1)S(1)} %add_convert_fusion), channel_id=1, source_target_pairs={{0,24},{8,0},{16,8},{24,16},{1,25},{9,1},{17,9},{25,17},{2,26},{10... | collective-permute-start | bytes 1572872 | tf_op jit(solution)/shard_map/up/ppermute | solution.py:201
  119.0 10.4 %copy-start.9 = (s32[1,128,2]{1,2,0:T(2,128)S(1)}, s32[1,128,2]{1,2,0:T(2,128)}, u32[]{:S(2)}) copy-start(s32[1,128,2]{1,2,0:T(2,128)} %param.9) | copy-start | bytes 3076
  120.8 6.9 %collective-permute-start.25 = (f32[1,128]{1,0:T(1,128)S(1)}, f32[1,128]{1,0:T(1,128)S(1)}, u32[]{:S(2)}, u32[]{:S(2)}) collective-permute-start(f32[1,128]{1,0:T(1,128)S(1)} %add_bitcast_fusion.1), channel_id=1, source_target_pairs={{0,3},{1,2},{2,1},{3,0},{4,7},{5,6},{6,5},{7,4},{8,11},{9,10},{10,... | collective-permute-start | bytes 1544 | tf_op jit(solution)/shard_map/dot/ppermute | solution.py:201
  123.3 4.4 %collective-permute-start.24 = (f32[1,128]{1,0:T(1,128)S(1)}, f32[1,128]{1,0:T(1,128)S(1)}, u32[]{:S(2)}, u32[]{:S(2)}) collective-permute-start(f32[1,128]{1,0:T(1,128)S(1)} %add_bitcast_fusion), channel_id=1, source_target_pairs={{0,2},{1,3},{2,0},{3,1},{4,6},{5,7},{6,4},{7,5},{8,10},{9,11},{10,... | collective-permute-start | bytes 1544 | tf_op jit(solution)/shard_map/dot/ppermute | solution.py:201
  125.9 3.5 %collective-permute-start.23 = (f32[1,128]{1,0:T(1,128)S(1)}, f32[1,128]{1,0:T(1,128)S(1)}, u32[]{:S(2)}, u32[]{:S(2)}) collective-permute-start(f32[1,128]{1,0:T(1,128)S(1)} %get-tuple-element.957), channel_id=1, source_target_pairs={{0,1},{1,0},{2,3},{3,2},{4,5},{5,4},{6,7},{7,6},{8,9},{9,8},{10,11... | collective-permute-start | bytes 1544 | tf_op jit(solution)/shard_map/dot/ppermute | solution.py:201

commit v5 on v4

--- a/solution.py
+++ b/solution.py
@@ -249,7 +249,7 @@
     columns = [
         jnp.sum(jnp.where(ids == (place ^ k), probs, 0.0), axis=1).reshape(1, -1) for k in range(4)
     ]
-    sync(columns=columns)
+    v.columns = columns
     t_near = over(v.tok, PAIRS, "t_near")
     t_mid_in = over(v.tok, MIDDLE, "t_mid_in")
     p_near, p_cross, p_flip = (small(v.columns[k], k, "p") for k in (1, 2, 3))
@@ -282,14 +282,22 @@
     del v.t_two
     sync(a_two=a_two, sib_w=sib_w, all_d=all_d)
 
-    sync(t_mid_out=t_mid_out, g_far_in=g_far_in)
-    g_far_out = over(v.g_far_in, OUTWARD, "g_far_out")
-    g_mid_in = over(v.grd, MIDDLE, "g_mid_in")
-
     two = jnp.concatenate([v.grd, v.g_near], axis=0)
     dx_two, k_two = behind(two, v.a_two, jnp.concatenate([v.columns[0], v.p_near], axis=1))
     del v.p_near, v.a_two, v.columns
     sync(dx_two=dx_two, k_two=k_two)
+    n = lax.axis_size("section")
+
+    def home(x, pairs, name):
+        steps = [(4 * i + a, (i - 1) % n * 4 + b) for i in range(n) for a, b in pairs]
+        return over(x, steps, name, ("section", "expert"))
+
+    up_own = over(v.dx_two[:count], [(i, (i - 1) % n) for i in range(n)], "up", "section")
+    up_near = home(v.dx_two[count:], INWARD, "up")
+
+    sync(t_mid_out=t_mid_out, g_far_in=g_far_in)
+    g_far_out = over(v.g_far_in, OUTWARD, "g_far_out")
+    g_mid_in = over(v.grd, MIDDLE, "g_mid_in")
 
     sync(t_far_out=t_far_out)
     t_cross, t_flip = pick(v.t_far_in, v.t_mid_out), pick(v.t_mid_in, v.t_far_out)
@@ -316,7 +324,7 @@
     sync(g_cross=g_cross, dx_cross=dx_cross, k_cross=k_cross)
     r4 = over(v.dx_cross, INWARD, "r4")
 
-    sync(r5=r5)
+    sync(r5=r5, up_own=up_own, up_near=up_near)
     back = v.dx_cross + v.r5
     del v.dx_cross, v.r5
     sync(back=back)
@@ -333,7 +341,9 @@
     with jax.named_scope("weight_grads"):
         sib_gu = mm(v.rows, kept(0, 1), ((1,), (1,))).astype(BF16)
         sib_dn = mm(kept(1, 1), v.grads, ((1,), (0,))).astype(BF16)
-    sync(sib_gu=sib_gu, sib_dn=sib_dn)
+        own_gu = mm(v.rows, kept(0, 0), ((1,), (1,))).astype(BF16)
+        own_dn = mm(kept(1, 0), v.grads, ((1,), (0,))).astype(BF16)
+    sync(sib_gu=sib_gu, sib_dn=sib_dn, own_gu=own_gu, own_dn=own_dn)
 
     sync(r4=r4)
     sync(r3=r3)
@@ -341,22 +351,12 @@
     back = v.dx_two[count:] + v.r3
     del v.dx_flip, v.r4, v.r3
     sync(back=back, back_mid=back_mid)
-    r1 = over(v.back, PAIRS, "r1")
-    r2 = over(v.back_mid, MIDDLE, "r2")
+    r1 = home(v.back, OUTWARD, "r1")
+    r2 = home(v.back_mid, MIDDLE, "r2")
     got_gu = over(v.sib_gu, SWAP, "got_gu", "dp")
     got_dn = over(v.sib_dn, SWAP, "got_dn", "dp")
-    with jax.named_scope("weight_grads"):
-        own_gu = mm(v.rows, kept(0, 0), ((1,), (1,))).astype(BF16)
-        own_dn = mm(kept(1, 0), v.grads, ((1,), (0,))).astype(BF16)
-    sync(own_gu=own_gu, own_dn=own_dn)
-
-
-    sync(r1=r1)
-    sync(r2=r2)
-    n = lax.axis_size("section")
-    total = sum(x.astype(F32) for x in (v.dx_two[:count], v.r1, v.r2))
-    sync(total=total.astype(BF16))
-    upstream = over(v.total, [(i, (i - 1) % n) for i in range(n)], "up", "section")
+
+
     sync(got_dn=got_dn, got_gu=got_gu)
     own_n = v.own_dn + v.got_dn
     own_g = v.own_gu[:, :half] + v.got_gu[:, :half]
@@ -365,9 +365,12 @@
     two = v.k_two[0]
     dots = (two[:, count:], v.k_cross[0], v.k_flip[0])
     dots = [two[:, :count]] + [small(d, k, "dot") for k, d in enumerate(dots, 1)]
+    sync(dots=dots)
     prob_grad = sum(
-        jnp.where(ids == (place ^ k), d.reshape(-1, 1), 0.0) for k, d in enumerate(dots)
-    )
+        jnp.where(ids == (place ^ k), d.reshape(-1, 1), 0.0) for k, d in enumerate(v.dots)
+    )
+    sync(r1=r1, r2=r2)
+    upstream = sum(x.astype(F32) for x in (v.up_own, v.up_near, v.r1, v.r2)).astype(BF16)
     return (
         upstream[None],
         prob_grad[None],

time: 132 us -> 122 us (0.924)
  waiting for transfers between devices: 50.6 us -> 39.6 us
  starting transfers between devices: 38.3 us -> 42.8 us
  matrix products: 21.4 us -> 19.6 us
  other arithmetic: 11.3 us -> 9.89 us
    ppermute x26 -> x27, waiting for transfers between devices: 50.6 us -> 39.6 us  [over(): return lax.ppermute(x, axis, pairs)]
    ppermute x26 -> x27, starting transfers between devices: 38.3 us -> 42.8 us  [over(): return lax.ppermute(x, axis, pairs)]
    dot_general x17, matrix products: 21.4 us -> 19.6 us  [mm(): return lax.dot_general(a, b, (dims, ((), ())), preferred_element_type=F32)]
    unnamed x22 -> x11, local copies, waits for them, and re-layouts: 3.68 us -> 3.91 us
  transfers between devices with their start and end apart: 26 -> 27, of which waited for: 11 -> 9; matrix products, arithmetic and copies ran while one was open for 25% -> 25% of each run, Pallas kernels for 2% -> 3%
where the time goes in v5:
time: 122 us; the launch traced here: 121 us
  starting transfers between devices  42.8 us (35%)
  waiting for transfers between devices  39.6 us (32%)
  matrix products  19.6 us (16%)
  other arithmetic  9.89 us (8%)
  local copies, waits for them, and re-layouts  5.1 us (4%)
  Pallas kernels  3.19 us (3%)
    ppermute x27, starting transfers between devices, over(): return lax.ppermute(x, axis, pairs)  42.8 us
    ppermute x27, waiting for transfers between devices, over(): return lax.ppermute(x, axis, pairs)  39.6 us
    dot_general x17, matrix products, mm(): return lax.dot_general(a, b, (dims, ((), ())), preferred_element_type=F32)  19.6 us
    unnamed x11, local copies, waits for them, and re-layouts  3.91 us
    pallas_call x2, Pallas kernels, gather(): pl.pallas_call(functools.partial(gather_kernel, [piece[1:] for piece in p...  3.19 us
  transfers between devices with their start and end apart: 27, of which 9 were waited for; matrix products, arithmetic and copies ran while one was open for 25% of the time, Pallas kernels for 3%

profile of v5, /device:TPU:0, one launch (start us, length us, event | category | flops | bytes accessed | tf_op | source)
XLA Modules:
  0.0 121.4 jit_solution(14679493694399759027)
XLA Ops:
  0.6 1.5 %collective-permute-start.3 = (bf16[128,2048]{1,0:T(8,128)(2,1)}, bf16[128,2048]{1,0:T(8,128)(2,1)}, u32[]{:S(2)}, u32[]{:S(2)}) collective-permute-start(bf16[128,2048]{1,0:T(8,128)(2,1)} %bitcast.53), channel_id=1, source_target_pairs={{1,2},{2,1},{5,6},{6,5},{9,10},{10,9},{13,14},{14,13},{17,18},{18,... | collective-permute-start | bytes 1572872 | tf_op jit(solution)/shard_map/t_mid_in/ppermute | solution.py:201
  2.1 5.1 %collective-permute-start.4 = (bf16[128,2048]{1,0:T(8,128)(2,1)}, bf16[128,2048]{1,0:T(8,128)(2,1)}, u32[]{:S(2)}, u32[]{:S(2)}) collective-permute-start(bf16[128,2048]{1,0:T(8,128)(2,1)} %bitcast.54), channel_id=1, source_target_pairs={{0,1},{3,2},{1,0},{2,3},{4,5},{7,6},{5,4},{6,7},{8,9},{11,10},{9,8... | collective-permute-start | bytes 1572872 | tf_op jit(solution)/shard_map/t_near/ppermute | solution.py:201
  8.5 1.9 %collective-permute-start.1 = (f32[1,128]{1,0:T(1,128)S(1)}, f32[1,128]{1,0:T(1,128)S(1)}, u32[]{:S(2)}, u32[]{:S(2)}) collective-permute-start(f32[1,128]{1,0:T(1,128)S(1)} %bitcast.79), channel_id=1, source_target_pairs={{0,3},{1,2},{2,1},{3,0},{4,7},{5,6},{6,5},{7,4},{8,11},{9,10},{10,... | collective-permute-start | bytes 1544 | tf_op jit(solution)/shard_map/p/ppermute | solution.py:201
  10.4 1.1 collective-permute-start.2
  11.5 1.4 %copy-done = bf16[1,1,2048,384]{3,2,1,0:T(8,128)(2,1)S(1)} copy-done((bf16[1,1,2048,384]{3,2,1,0:T(8,128)(2,1)S(1)}, bf16[1,1,2048,384]{3,2,1,0:T(8,128)(2,1)}, u32[]{:S(2)}) %copy-start) | copy-done | bytes 1572888
  12.9 1.4 %copy-done.1 = bf16[1,1,2048,384]{3,2,1,0:T(8,128)(2,1)S(1)} copy-done((bf16[1,1,2048,384]{3,2,1,0:T(8,128)(2,1)S(1)}, bf16[1,1,2048,384]{3,2,1,0:T(8,128)(2,1)}, u32[]{:S(2)}) %copy-start.1) | copy-done | bytes 1572888
  14.6 4.2 %collective-permute-done = f32[1,128]{1,0:T(1,128)S(1)} collective-permute-done((f32[1,128]{1,0:T(1,128)S(1)}, f32[1,128]{1,0:T(1,128)S(1)}, u32[]{:S(2)}, u32[]{:S(2)}) %collective-permute-start) | collective-permute-done | bytes 544 | tf_op jit(solution)/shard_map/p/ppermute | solution.py:201
  18.9 1.3 %collective-permute-done.1 = f32[1,128]{1,0:T(1,128)S(1)} collective-permute-done((f32[1,128]{1,0:T(1,128)S(1)}, f32[1,128]{1,0:T(1,128)S(1)}, u32[]{:S(2)}, u32[]{:S(2)}) %collective-permute-start.1) | collective-permute-done | bytes 544 | tf_op jit(solution)/shard_map/p/ppermute | solution.py:201
  22.1 1.3 %collective-permute-start.10 = (bf16[128,2048]{1,0:T(8,128)(2,1)}, bf16[128,2048]{1,0:T(8,128)(2,1)S(1)}, u32[]{:S(2)}, u32[]{:S(2)}) collective-permute-start(bf16[128,2048]{1,0:T(8,128)(2,1)} %collective-permute-done.3), channel_id=1, source_target_pairs={{1,0},{2,3},{5,4},{6,7},{9,8},{10,11},{13,12},{14,15},{17,16},{18,... | collective-permute-start | bytes 1572872 | tf_op jit(solution)/shard_map/t_mid_out/ppermute | solution.py:201
  23.4 1.1 constant_dynamic-update-slice_fusion.1
  24.5 1.1 constant_dynamic-update-slice_fusion
  25.6 1.0 fusion.48
  26.6 9.1 %collective-permute-done.5 = bf16[128,2048]{1,0:T(8,128)(2,1)S(1)} collective-permute-done((bf16[128,2048]{1,0:T(8,128)(2,1)}, bf16[128,2048]{1,0:T(8,128)(2,1)S(1)}, u32[]{:S(2)}, u32[]{:S(2)}) %collective-permute-start.5) | collective-permute-done | bytes 524320 | tf_op jit(solution)/shard_map/g_near/ppermute | solution.py:201
  36.4 1.3 %collective-permute-start.11 = (bf16[128,2048]{1,0:T(8,128)(2,1)S(1)}, bf16[128,2048]{1,0:T(8,128)(2,1)S(1)}, u32[]{:S(2)}, u32[]{:S(2)}) collective-permute-start(bf16[128,2048]{1,0:T(8,128)(2,1)S(1)} %collective-permute-done.8), channel_id=1, source_target_pairs={{1,0},{2,3},{5,4},{6,7},{9,8},{10,11},{13,12},{14,15},{17,16},{18,... | collective-permute-start | bytes 1572872 | tf_op jit(solution)/shard_map/t_far_out/ppermute | solution.py:201
  37.7 2.9 %sib_w.1 = (bf16[2048,768]{1,0:T(8,128)(2,1)S(1)}, bf16[768,2048]{1,0:T(8,128)(2,1)S(1)}) custom-call(bf16[2048,768]{1,0:T(8,128)(2,1)} %collective-permute-done.7.refs_0_, bf16[384,2048]{1,0:T(8,128)(2,1)} %bitcast.6.refs_1_, bf16[384,2048]{1,0:T(8,128)(2,1)} %collective-permute-done.6.refs_2_), custom_call_target="tpu_custom_call" | custom-call | bytes 1048576 | tf_op jit(solution)/shard_map/sib_w/pallas_call | solution.py:179
  40.6 1.0 fusion.49
  41.8 1.0 fusion.3
  43.4 1.0 fusion.45
  44.4 1.1 fusion
  45.6 1.4 %collective-permute-done.10 = bf16[128,2048]{1,0:T(8,128)(2,1)S(1)} collective-permute-done((bf16[128,2048]{1,0:T(8,128)(2,1)}, bf16[128,2048]{1,0:T(8,128)(2,1)S(1)}, u32[]{:S(2)}, u32[]{:S(2)}) %collective-permute-start.10) | collective-permute-done | bytes 524320 | tf_op jit(solution)/shard_map/t_mid_out/ppermute | solution.py:201
  47.6 1.3 %collective-permute-start.13 = (bf16[128,2048]{1,0:T(8,128)(2,1)S(1)}, bf16[128,2048]{1,0:T(8,128)(2,1)S(1)}, u32[]{:S(2)}, u32[]{:S(2)}) collective-permute-start(bf16[128,2048]{1,0:T(8,128)(2,1)S(1)} %collective-permute-done.9), channel_id=1, source_target_pairs={{1,0},{2,3},{5,4},{6,7},{9,8},{10,11},{13,12},{14,15},{17,16},{18,... | collective-permute-start | bytes 1572872 | tf_op jit(solution)/shard_map/g_far_out/ppermute | solution.py:201
  49.0 10.0 %collective-permute-start.16 = (bf16[128,2048]{1,0:T(8,128)(2,1)S(1)}, bf16[128,2048]{1,0:T(8,128)(2,1)S(1)}, u32[]{:S(2)}, u32[]{:S(2)}) collective-permute-start(bf16[128,2048]{1,0:T(8,128)(2,1)S(1)} %get-tuple-element.900), channel_id=1, source_target_pairs={{0,25},{3,26},{8,1},{11,2},{16,9},{19,10},{24,17},{27,18},{4,29},{... | collective-permute-start | bytes 1572872 | tf_op jit(solution)/shard_map/up/ppermute | solution.py:201
  59.8 1.0 fusion.18
  60.9 1.0 fusion.17
  61.9 1.5 %collective-permute-start.14 = (bf16[128,2048]{1,0:T(8,128)(2,1)S(1)}, bf16[128,2048]{1,0:T(8,128)(2,1)S(1)}, u32[]{:S(2)}, u32[]{:S(2)}) collective-permute-start(bf16[128,2048]{1,0:T(8,128)(2,1)S(1)} %collective-permute-done.12), channel_id=1, source_target_pairs={{1,0},{2,3},{5,4},{6,7},{9,8},{10,11},{13,12},{14,15},{17,16},{18,... | collective-permute-start | bytes 1572872 | tf_op jit(solution)/shard_map/g_mid_out/ppermute | solution.py:201
  63.4 1.3 %pad_maximum_fusion = bf16[2048,512]{0,1:T(8,128)(2,1)S(1)} fusion(bf16[2048,128]{0,1:T(8,128)(2,1)S(1)} %bitcast.57, bf16[2048,128]{0,1:T(8,128)(2,1)S(1)} %bitcast.58, bf16[2048,128]{0,1:T(8,128)(2,1)} %bitcast.12, bf16[2048,128]{0,1:T(8,128)(2,1)S(1)} %bitcast.56), kind=kLoop, calls=%fused_computation.10 | loop fusion | flops 8388608 | bytes 4194304 | tf_op jit(solution)/shard_map/concatenate | solution.py:310
  64.7 4.7 %collective-permute-done.13 = bf16[128,2048]{1,0:T(8,128)(2,1)S(1)} collective-permute-done((bf16[128,2048]{1,0:T(8,128)(2,1)S(1)}, bf16[128,2048]{1,0:T(8,128)(2,1)S(1)}, u32[]{:S(2)}, u32[]{:S(2)}) %collective-permute-start.13) | collective-permute-done | bytes 524320 | tf_op jit(solution)/shard_map/g_far_out/ppermute | solution.py:201
  70.9 1.2 fusion.44
  72.1 1.2 fusion.1
  73.3 1.5 %collective-permute-start.15 = (bf16[128,2048]{1,0:T(8,128)(2,1)S(1)}, bf16[128,2048]{1,0:T(8,128)(2,1)S(1)}, u32[]{:S(2)}, u32[]{:S(2)}) collective-permute-start(bf16[128,2048]{1,0:T(8,128)(2,1)S(1)} %fusion.1), channel_id=1, source_target_pairs={{0,1},{3,2},{4,5},{7,6},{8,9},{11,10},{12,13},{15,14},{16,17},{19,... | collective-permute-start | bytes 1572872 | tf_op jit(solution)/shard_map/r5/ppermute | solution.py:201
  74.8 5.0 %collective-permute-done.14 = bf16[128,2048]{1,0:T(8,128)(2,1)S(1)} collective-permute-done((bf16[128,2048]{1,0:T(8,128)(2,1)S(1)}, bf16[128,2048]{1,0:T(8,128)(2,1)S(1)}, u32[]{:S(2)}, u32[]{:S(2)}) %collective-permute-start.14) | collective-permute-done | bytes 524320 | tf_op jit(solution)/shard_map/g_mid_out/ppermute | solution.py:201
  81.2 1.2 fusion.43
  82.4 1.2 fusion.2
  83.6 1.5 %collective-permute-start.18 = (bf16[128,2048]{1,0:T(8,128)(2,1)S(1)}, bf16[128,2048]{1,0:T(8,128)(2,1)S(1)}, u32[]{:S(2)}, u32[]{:S(2)}) collective-permute-start(bf16[128,2048]{1,0:T(8,128)(2,1)S(1)} %fusion.2), channel_id=1, source_target_pairs={{0,1},{3,2},{4,5},{7,6},{8,9},{11,10},{12,13},{15,14},{16,17},{19,... | collective-permute-start | bytes 1572872 | tf_op jit(solution)/shard_map/r4/ppermute | solution.py:201
  86.2 1.0 convolution_convert_fusion.3
  87.2 1.9 %convolution_convert_fusion.1 = bf16[2048,768]{1,0:T(8,128)(2,1)S(1)} fusion(bf16[2048,512]{0,1:T(8,128)(2,1)S(1)} %pad_maximum_fusion, bf16[768,128]{1,0:T(8,128)(2,1)S(1)} %pad_maximum_fusion.7, bf16[768,128]{1,0:T(8,128)(2,1)S(1)} %pad_maximum_fusion.9, bf16[768,256]{1,0:T(8,128)(2,1)S(1)} %get-tuple-element.776), kind=kOutput, calls=%fused_computation.1 | convolution fusion | flops 1614544896 | bytes 6029312 | tf_op jit(solution)/shard_map/weight_grads/dot_general | solution.py:204
  89.1 1.0 convolution_convert_fusion.2
  90.1 1.9 %convolution_convert_fusion = bf16[2048,768]{1,0:T(8,128)(2,1)S(1)} fusion(bf16[2048,512]{0,1:T(8,128)(2,1)S(1)} %pad_maximum_fusion, bf16[768,128]{1,0:T(8,128)(2,1)S(1)} %pad_maximum_fusion.8, bf16[768,128]{1,0:T(8,128)(2,1)S(1)} %pad_maximum_fusion.10, bf16[768,256]{1,0:T(8,128)(2,1)S(1)} %get-tuple-element.778), kind=kOutput, calls=%fused_computation | convolution fusion | flops 1614544896 | bytes 6029312 | tf_op jit(solution)/shard_map/weight_grads/dot_general | solution.py:204
  92.0 3.8 %collective-permute-done.18 = bf16[128,2048]{1,0:T(8,128)(2,1)S(1)} collective-permute-done((bf16[128,2048]{1,0:T(8,128)(2,1)S(1)}, bf16[128,2048]{1,0:T(8,128)(2,1)S(1)}, u32[]{:S(2)}, u32[]{:S(2)}) %collective-permute-start.18) | collective-permute-done | bytes 524320 | tf_op jit(solution)/shard_map/r4/ppermute | solution.py:201
  96.6 1.3 %collective-permute-start.25 = (bf16[128,2048]{1,0:T(8,128)(2,1)S(1)}, bf16[128,2048]{1,0:T(8,128)(2,1)S(1)}, u32[]{:S(2)}, u32[]{:S(2)}) collective-permute-start(bf16[128,2048]{1,0:T(8,128)(2,1)S(1)} %slice_add_fusion.2), channel_id=1, source_target_pairs={{1,24},{2,27},{9,0},{10,3},{17,8},{18,11},{25,16},{26,19},{5,28},{... | collective-permute-start | bytes 1572872 | tf_op jit(solution)/shard_map/r1/ppermute | solution.py:201
  98.5 5.4 %collective-permute-done.20 = bf16[384,2048]{1,0:T(8,128)(2,1)S(1)} collective-permute-done((bf16[384,2048]{1,0:T(8,128)(2,1)S(1)}, bf16[384,2048]{1,0:T(8,128)(2,1)S(1)}, u32[]{:S(2)}, u32[]{:S(2)}) %collective-permute-start.20) | collective-permute-done | bytes 1572896 | tf_op jit(solution)/shard_map/got_dn/ppermute | solution.py:201
  104.0 2.0 %slice_add_fusion = (bf16[2048,384]{1,0:T(8,128)(2,1)}, bf16[2048,384]{1,0:T(8,128)(2,1)}) fusion(bf16[2048,768]{1,0:T(8,128)(2,1)S(1)} %collective-permute-done.21, bf16[2048,768]{1,0:T(8,128)(2,1)S(1)} %convolution_convert_fusion.1), kind=kLoop, calls=%fused_computation.12 | loop fusion | flops 1572864 | bytes 9437184 | tf_op jit(solution)/shard_map/add | solution.py:363
  106.0 1.9 %add.151 = bf16[384,2048]{1,0:T(8,128)(2,1)} add(bf16[384,2048]{1,0:T(8,128)(2,1)S(1)} %convolution_convert_fusion.3, bf16[384,2048]{1,0:T(8,128)(2,1)S(1)} %collective-permute-done.20) | non-fusion elementwise | flops 786432 | bytes 4718592 | tf_op jit(solution)/shard_map/add | solution.py:361
  107.8 4.7 %collective-permute-start.22 = (f32[1,128]{1,0:T(1,128)S(1)}, f32[1,128]{1,0:T(1,128)S(1)}, u32[]{:S(2)}, u32[]{:S(2)}) collective-permute-start(f32[1,128]{1,0:T(1,128)S(1)} %get-tuple-element.904), channel_id=1, source_target_pairs={{0,1},{1,0},{2,3},{3,2},{4,5},{5,4},{6,7},{7,6},{8,9},{9,8},{10,11... | collective-permute-start | bytes 1544 | tf_op jit(solution)/shard_map/dot/ppermute | solution.py:201
  112.5 1.0 collective-permute-start.23
  113.5 1.5 %collective-permute-start.24 = (f32[1,128]{1,0:T(1,128)S(1)}, f32[1,128]{1,0:T(1,128)S(1)}, u32[]{:S(2)}, u32[]{:S(2)}) collective-permute-start(f32[1,128]{1,0:T(1,128)S(1)} %add_bitcast_fusion.1), channel_id=1, source_target_pairs={{0,3},{1,2},{2,1},{3,0},{4,7},{5,6},{6,5},{7,4},{8,11},{9,10},{10,... | collective-permute-start | bytes 1544 | tf_op jit(solution)/shard_map/dot/ppermute | solution.py:201
  115.0 4.7 %collective-permute-done.23 = f32[1,128]{1,0:T(1,128)S(1)} collective-permute-done((f32[1,128]{1,0:T(1,128)S(1)}, f32[1,128]{1,0:T(1,128)S(1)}, u32[]{:S(2)}, u32[]{:S(2)}) %collective-permute-start.23) | collective-permute-done | bytes 544 | tf_op jit(solution)/shard_map/dot/ppermute | solution.py:201
  119.7 1.1 fusion.19
  (68 shorter events, 12.5 us)
Async XLA Ops:
  0.6 19.5 %collective-permute-start.3 = (bf16[128,2048]{1,0:T(8,128)(2,1)}, bf16[128,2048]{1,0:T(8,128)(2,1)}, u32[]{:S(2)}, u32[]{:S(2)}) collective-permute-start(bf16[128,2048]{1,0:T(8,128)(2,1)} %bitcast.53), channel_id=1, source_target_pairs={{1,2},{2,1},{5,6},{6,5},{9,10},{10,9},{13,14},{14,13},{17,18},{18,... | collective-permute-start | bytes 1572872 | tf_op jit(solution)/shard_map/t_mid_in/ppermute | solution.py:201
  2.1 18.0 %collective-permute-start.4 = (bf16[128,2048]{1,0:T(8,128)(2,1)}, bf16[128,2048]{1,0:T(8,128)(2,1)}, u32[]{:S(2)}, u32[]{:S(2)}) collective-permute-start(bf16[128,2048]{1,0:T(8,128)(2,1)} %bitcast.54), channel_id=1, source_target_pairs={{0,1},{3,2},{1,0},{2,3},{4,5},{7,6},{5,4},{6,7},{8,9},{11,10},{9,8... | collective-permute-start | bytes 1572872 | tf_op jit(solution)/shard_map/t_near/ppermute | solution.py:201
  7.9 10.9 %collective-permute-start = (f32[1,128]{1,0:T(1,128)S(1)}, f32[1,128]{1,0:T(1,128)S(1)}, u32[]{:S(2)}, u32[]{:S(2)}) collective-permute-start(f32[1,128]{1,0:T(1,128)S(1)} %bitcast.80), channel_id=1, source_target_pairs={{0,2},{1,3},{2,0},{3,1},{4,6},{5,7},{6,4},{7,5},{8,10},{9,11},{10,... | collective-permute-start | bytes 1544 | tf_op jit(solution)/shard_map/p/ppermute | solution.py:201
  8.5 11.6 %collective-permute-start.1 = (f32[1,128]{1,0:T(1,128)S(1)}, f32[1,128]{1,0:T(1,128)S(1)}, u32[]{:S(2)}, u32[]{:S(2)}) collective-permute-start(f32[1,128]{1,0:T(1,128)S(1)} %bitcast.79), channel_id=1, source_target_pairs={{0,3},{1,2},{2,1},{3,0},{4,7},{5,6},{6,5},{7,4},{8,11},{9,10},{10,... | collective-permute-start | bytes 1544 | tf_op jit(solution)/shard_map/p/ppermute | solution.py:201
  10.4 9.8 %collective-permute-start.2 = (f32[1,128]{1,0:T(1,128)S(1)}, f32[1,128]{1,0:T(1,128)S(1)}, u32[]{:S(2)}, u32[]{:S(2)}) collective-permute-start(f32[1,128]{1,0:T(1,128)S(1)} %bitcast.78), channel_id=1, source_target_pairs={{0,1},{1,0},{2,3},{3,2},{4,5},{5,4},{6,7},{7,6},{8,9},{9,8},{10,11... | collective-permute-start | bytes 1544 | tf_op jit(solution)/shard_map/p/ppermute | solution.py:201
  11.5 1.4 %copy-start = (bf16[1,1,2048,384]{3,2,1,0:T(8,128)(2,1)S(1)}, bf16[1,1,2048,384]{3,2,1,0:T(8,128)(2,1)}, u32[]{:S(2)}) copy-start(bf16[1,1,2048,384]{3,2,1,0:T(8,128)(2,1)} %param.11) | copy-start | bytes 4718596
  12.9 1.4 %copy-start.1 = (bf16[1,1,2048,384]{3,2,1,0:T(8,128)(2,1)S(1)}, bf16[1,1,2048,384]{3,2,1,0:T(8,128)(2,1)}, u32[]{:S(2)}) copy-start(bf16[1,1,2048,384]{3,2,1,0:T(8,128)(2,1)} %param.12) | copy-start | bytes 4718596
  20.1 16.3 %collective-permute-start.7 = (bf16[2048,768]{1,0:T(8,128)(2,1)S(1)}, bf16[2048,768]{1,0:T(8,128)(2,1)}, u32[]{:S(2)}, u32[]{:S(2)}) collective-permute-start(bf16[2048,768]{1,0:T(8,128)(2,1)S(1)} %own_w.1), channel_id=1, source_target_pairs={{0,4},{4,0},{1,5},{5,1},{2,6},{6,2},{3,7},{7,3},{8,12},{12,8},{9,1... | collective-permute-start | bytes 9437192 | tf_op jit(solution)/shard_map/sib_w/ppermute | solution.py:201
  20.2 16.2 %collective-permute-start.6 = (bf16[384,2048]{1,0:T(8,128)(2,1)}, bf16[384,2048]{1,0:T(8,128)(2,1)}, u32[]{:S(2)}, u32[]{:S(2)}) collective-permute-start(bf16[384,2048]{1,0:T(8,128)(2,1)} %bitcast.6.refs_1_), channel_id=1, source_target_pairs={{0,4},{4,0},{1,5},{5,1},{2,6},{6,2},{3,7},{7,3},{8,12},{12,8},{9,1... | collective-permute-start | bytes 4718600 | tf_op jit(solution)/shard_map/sib_d/ppermute | solution.py:201
  20.7 15.0 %collective-permute-start.5 = (bf16[128,2048]{1,0:T(8,128)(2,1)}, bf16[128,2048]{1,0:T(8,128)(2,1)S(1)}, u32[]{:S(2)}, u32[]{:S(2)}) collective-permute-start(bf16[128,2048]{1,0:T(8,128)(2,1)} %bitcast.62), channel_id=1, source_target_pairs={{0,1},{3,2},{1,0},{2,3},{4,5},{7,6},{5,4},{6,7},{8,9},{11,10},{9,8... | collective-permute-start | bytes 1572872 | tf_op jit(solution)/shard_map/g_near/ppermute | solution.py:201
  21.5 15.0 %collective-permute-start.8 = (bf16[128,2048]{1,0:T(8,128)(2,1)}, bf16[128,2048]{1,0:T(8,128)(2,1)S(1)}, u32[]{:S(2)}, u32[]{:S(2)}) collective-permute-start(bf16[128,2048]{1,0:T(8,128)(2,1)} %collective-permute-done.4), channel_id=1, source_target_pairs={{1,2},{2,1},{5,6},{6,5},{9,10},{10,9},{13,14},{14,13},{17,18},{18,... | collective-permute-start | bytes 1572872 | tf_op jit(solution)/shard_map/t_far_in/ppermute | solution.py:201
  22.1 24.8 %collective-permute-start.10 = (bf16[128,2048]{1,0:T(8,128)(2,1)}, bf16[128,2048]{1,0:T(8,128)(2,1)S(1)}, u32[]{:S(2)}, u32[]{:S(2)}) collective-permute-start(bf16[128,2048]{1,0:T(8,128)(2,1)} %collective-permute-done.3), channel_id=1, source_target_pairs={{1,0},{2,3},{5,4},{6,7},{9,8},{10,11},{13,12},{14,15},{17,16},{18,... | collective-permute-start | bytes 1572872 | tf_op jit(solution)/shard_map/t_mid_out/ppermute | solution.py:201
  35.7 11.2 %collective-permute-start.9 = (bf16[128,2048]{1,0:T(8,128)(2,1)S(1)}, bf16[128,2048]{1,0:T(8,128)(2,1)S(1)}, u32[]{:S(2)}, u32[]{:S(2)}) collective-permute-start(bf16[128,2048]{1,0:T(8,128)(2,1)S(1)} %collective-permute-done.5), channel_id=1, source_target_pairs={{1,2},{2,1},{5,6},{6,5},{9,10},{10,9},{13,14},{14,13},{17,18},{18,... | collective-permute-start | bytes 1572872 | tf_op jit(solution)/shard_map/g_far_in/ppermute | solution.py:201
  36.4 23.3 %collective-permute-start.11 = (bf16[128,2048]{1,0:T(8,128)(2,1)S(1)}, bf16[128,2048]{1,0:T(8,128)(2,1)S(1)}, u32[]{:S(2)}, u32[]{:S(2)}) collective-permute-start(bf16[128,2048]{1,0:T(8,128)(2,1)S(1)} %collective-permute-done.8), channel_id=1, source_target_pairs={{1,0},{2,3},{5,4},{6,7},{9,8},{10,11},{13,12},{14,15},{17,16},{18,... | collective-permute-start | bytes 1572872 | tf_op jit(solution)/shard_map/t_far_out/ppermute | solution.py:201
  40.6 1.2 copy-start.3
  47.0 15.0 %collective-permute-start.12 = (bf16[128,2048]{1,0:T(8,128)(2,1)S(1)}, bf16[128,2048]{1,0:T(8,128)(2,1)S(1)}, u32[]{:S(2)}, u32[]{:S(2)}) collective-permute-start(bf16[128,2048]{1,0:T(8,128)(2,1)S(1)} %bitcast.64), channel_id=1, source_target_pairs={{1,2},{2,1},{5,6},{6,5},{9,10},{10,9},{13,14},{14,13},{17,18},{18,... | collective-permute-start | bytes 1572872 | tf_op jit(solution)/shard_map/g_mid_in/ppermute | solution.py:201
  47.6 21.8 %collective-permute-start.13 = (bf16[128,2048]{1,0:T(8,128)(2,1)S(1)}, bf16[128,2048]{1,0:T(8,128)(2,1)S(1)}, u32[]{:S(2)}, u32[]{:S(2)}) collective-permute-start(bf16[128,2048]{1,0:T(8,128)(2,1)S(1)} %collective-permute-done.9), channel_id=1, source_target_pairs={{1,0},{2,3},{5,4},{6,7},{9,8},{10,11},{13,12},{14,15},{17,16},{18,... | collective-permute-start | bytes 1572872 | tf_op jit(solution)/shard_map/g_far_out/ppermute | solution.py:201
  49.0 36.1 %collective-permute-start.16 = (bf16[128,2048]{1,0:T(8,128)(2,1)S(1)}, bf16[128,2048]{1,0:T(8,128)(2,1)S(1)}, u32[]{:S(2)}, u32[]{:S(2)}) collective-permute-start(bf16[128,2048]{1,0:T(8,128)(2,1)S(1)} %get-tuple-element.900), channel_id=1, source_target_pairs={{0,25},{3,26},{8,1},{11,2},{16,9},{19,10},{24,17},{27,18},{4,29},{... | collective-permute-start | bytes 1572872 | tf_op jit(solution)/shard_map/up/ppermute | solution.py:201
  59.1 26.0 %collective-permute-start.17 = (bf16[128,2048]{1,0:T(8,128)(2,1)S(1)}, bf16[128,2048]{1,0:T(8,128)(2,1)S(1)}, u32[]{:S(2)}, u32[]{:S(2)}) collective-permute-start(bf16[128,2048]{1,0:T(8,128)(2,1)S(1)} %get-tuple-element.899), channel_id=1, source_target_pairs={{0,24},{8,0},{16,8},{24,16},{1,25},{9,1},{17,9},{25,17},{2,26},{10... | collective-permute-start | bytes 1572872 | tf_op jit(solution)/shard_map/up/ppermute | solution.py:201
  60.9 2.5 %copy-start.2 = (bf16[1,128,2048]{2,1,0:T(8,128)(2,1)S(1)}, bf16[1,128,2048]{2,1,0:T(8,128)(2,1)}, u32[]{:S(2)}) copy-start(bf16[1,128,2048]{2,1,0:T(8,128)(2,1)} %param.7) | copy-start | bytes 1572868
  61.9 17.9 %collective-permute-start.14 = (bf16[128,2048]{1,0:T(8,128)(2,1)S(1)}, bf16[128,2048]{1,0:T(8,128)(2,1)S(1)}, u32[]{:S(2)}, u32[]{:S(2)}) collective-permute-start(bf16[128,2048]{1,0:T(8,128)(2,1)S(1)} %collective-permute-done.12), channel_id=1, source_target_pairs={{1,0},{2,3},{5,4},{6,7},{9,8},{10,11},{13,12},{14,15},{17,16},{18,... | collective-permute-start | bytes 1572872 | tf_op jit(solution)/shard_map/g_mid_out/ppermute | solution.py:201
  73.3 11.8 %collective-permute-start.15 = (bf16[128,2048]{1,0:T(8,128)(2,1)S(1)}, bf16[128,2048]{1,0:T(8,128)(2,1)S(1)}, u32[]{:S(2)}, u32[]{:S(2)}) collective-permute-start(bf16[128,2048]{1,0:T(8,128)(2,1)S(1)} %fusion.1), channel_id=1, source_target_pairs={{0,1},{3,2},{4,5},{7,6},{8,9},{11,10},{12,13},{15,14},{16,17},{19,... | collective-permute-start | bytes 1572872 | tf_op jit(solution)/shard_map/r5/ppermute | solution.py:201
  83.6 12.2 %collective-permute-start.18 = (bf16[128,2048]{1,0:T(8,128)(2,1)S(1)}, bf16[128,2048]{1,0:T(8,128)(2,1)S(1)}, u32[]{:S(2)}, u32[]{:S(2)}) collective-permute-start(bf16[128,2048]{1,0:T(8,128)(2,1)S(1)} %fusion.2), channel_id=1, source_target_pairs={{0,1},{3,2},{4,5},{7,6},{8,9},{11,10},{12,13},{15,14},{16,17},{19,... | collective-permute-start | bytes 1572872 | tf_op jit(solution)/shard_map/r4/ppermute | solution.py:201
  85.3 10.5 %collective-permute-start.19 = (bf16[128,2048]{1,0:T(8,128)(2,1)S(1)}, bf16[128,2048]{1,0:T(8,128)(2,1)S(1)}, u32[]{:S(2)}, u32[]{:S(2)}) collective-permute-start(bf16[128,2048]{1,0:T(8,128)(2,1)S(1)} %add.147), channel_id=1, source_target_pairs={{1,2},{2,1},{5,6},{6,5},{9,10},{10,9},{13,14},{14,13},{17,18},{18,... | collective-permute-start | bytes 1572872 | tf_op jit(solution)/shard_map/r3/ppermute | solution.py:201
  96.0 8.0 %collective-permute-start.21 = (bf16[2048,768]{1,0:T(8,128)(2,1)S(1)}, bf16[2048,768]{1,0:T(8,128)(2,1)S(1)}, u32[]{:S(2)}, u32[]{:S(2)}) collective-permute-start(bf16[2048,768]{1,0:T(8,128)(2,1)S(1)} %convolution_convert_fusion), channel_id=1, source_target_pairs={{0,4},{4,0},{1,5},{5,1},{2,6},{6,2},{3,7},{7,3},{8,12},{12,8},{9,1... | collective-permute-start | bytes 9437192 | tf_op jit(solution)/shard_map/got_gu/ppermute | solution.py:201
  96.1 7.9 %collective-permute-start.20 = (bf16[384,2048]{1,0:T(8,128)(2,1)S(1)}, bf16[384,2048]{1,0:T(8,128)(2,1)S(1)}, u32[]{:S(2)}, u32[]{:S(2)}) collective-permute-start(bf16[384,2048]{1,0:T(8,128)(2,1)S(1)} %convolution_convert_fusion.2), channel_id=1, source_target_pairs={{0,4},{4,0},{1,5},{5,1},{2,6},{6,2},{3,7},{7,3},{8,12},{12,8},{9,1... | collective-permute-start | bytes 4718600 | tf_op jit(solution)/shard_map/got_dn/ppermute | solution.py:201
  96.6 23.1 %collective-permute-start.25 = (bf16[128,2048]{1,0:T(8,128)(2,1)S(1)}, bf16[128,2048]{1,0:T(8,128)(2,1)S(1)}, u32[]{:S(2)}, u32[]{:S(2)}) collective-permute-start(bf16[128,2048]{1,0:T(8,128)(2,1)S(1)} %slice_add_fusion.2), channel_id=1, source_target_pairs={{1,24},{2,27},{9,0},{10,3},{17,8},{18,11},{25,16},{26,19},{5,28},{... | collective-permute-start | bytes 1572872 | tf_op jit(solution)/shard_map/r1/ppermute | solution.py:201
  97.8 21.8 %collective-permute-start.26 = (bf16[128,2048]{1,0:T(8,128)(2,1)S(1)}, bf16[128,2048]{1,0:T(8,128)(2,1)S(1)}, u32[]{:S(2)}, u32[]{:S(2)}) collective-permute-start(bf16[128,2048]{1,0:T(8,128)(2,1)S(1)} %add.149), channel_id=1, source_target_pairs={{1,26},{2,25},{9,2},{10,1},{17,10},{18,9},{25,18},{26,17},{5,30},{... | collective-permute-start | bytes 1572872 | tf_op jit(solution)/shard_map/r2/ppermute | solution.py:201
  106.0 14.8 %copy-start.4 = (s32[1,128,2]{1,2,0:T(2,128)S(1)}, s32[1,128,2]{1,2,0:T(2,128)}, u32[]{:S(2)}) copy-start(s32[1,128,2]{1,2,0:T(2,128)} %param.9) | copy-start | bytes 3076
  107.8 7.2 %collective-permute-start.22 = (f32[1,128]{1,0:T(1,128)S(1)}, f32[1,128]{1,0:T(1,128)S(1)}, u32[]{:S(2)}, u32[]{:S(2)}) collective-permute-start(f32[1,128]{1,0:T(1,128)S(1)} %get-tuple-element.904), channel_id=1, source_target_pairs={{0,1},{1,0},{2,3},{3,2},{4,5},{5,4},{6,7},{7,6},{8,9},{9,8},{10,11... | collective-permute-start | bytes 1544 | tf_op jit(solution)/shard_map/dot/ppermute | solution.py:201
  112.5 7.2 %collective-permute-start.23 = (f32[1,128]{1,0:T(1,128)S(1)}, f32[1,128]{1,0:T(1,128)S(1)}, u32[]{:S(2)}, u32[]{:S(2)}) collective-permute-start(f32[1,128]{1,0:T(1,128)S(1)} %add_bitcast_fusion), channel_id=1, source_target_pairs={{0,2},{1,3},{2,0},{3,1},{4,6},{5,7},{6,4},{7,5},{8,10},{9,11},{10,... | collective-permute-start | bytes 1544 | tf_op jit(solution)/shard_map/dot/ppermute | solution.py:201
  113.5 6.2 %collective-permute-start.24 = (f32[1,128]{1,0:T(1,128)S(1)}, f32[1,128]{1,0:T(1,128)S(1)}, u32[]{:S(2)}, u32[]{:S(2)}) collective-permute-start(f32[1,128]{1,0:T(1,128)S(1)} %add_bitcast_fusion.1), channel_id=1, source_target_pairs={{0,3},{1,2},{2,1},{3,0},{4,7},{5,6},{6,5},{7,4},{8,11},{9,10},{10,... | collective-permute-start | bytes 1544 | tf_op jit(solution)/shard_map/dot/ppermute | solution.py:201

commit v6 on v5

--- a/solution.py
+++ b/solution.py
@@ -294,6 +294,7 @@
 
     up_own = over(v.dx_two[:count], [(i, (i - 1) % n) for i in range(n)], "up", "section")
     up_near = home(v.dx_two[count:], INWARD, "up")
+    d_near = small(v.k_two[0][:, count:], 1, "dot")
 
     sync(t_mid_out=t_mid_out, g_far_in=g_far_in)
     g_far_out = over(v.g_far_in, OUTWARD, "g_far_out")
@@ -324,7 +325,7 @@
     sync(g_cross=g_cross, dx_cross=dx_cross, k_cross=k_cross)
     r4 = over(v.dx_cross, INWARD, "r4")
 
-    sync(r5=r5, up_own=up_own, up_near=up_near)
+    sync(r5=r5, up_own=up_own, up_near=up_near, d_near=d_near)
     back = v.dx_cross + v.r5
     del v.dx_cross, v.r5
     sync(back=back)
@@ -362,15 +363,13 @@
     own_g = v.own_gu[:, :half] + v.got_gu[:, :half]
     own_u = v.own_gu[:, half:] + v.got_gu[:, half:]
     sync(own_g=own_g, own_u=own_u, own_n=own_n)
-    two = v.k_two[0]
-    dots = (two[:, count:], v.k_cross[0], v.k_flip[0])
-    dots = [two[:, :count]] + [small(d, k, "dot") for k, d in enumerate(dots, 1)]
-    sync(dots=dots)
-    prob_grad = sum(
-        jnp.where(ids == (place ^ k), d.reshape(-1, 1), 0.0) for k, d in enumerate(v.dots)
-    )
+    dots = [small(v.k_cross[0], 2, "dot"), small(v.k_flip[0], 3, "dot")]
     sync(r1=r1, r2=r2)
     upstream = sum(x.astype(F32) for x in (v.up_own, v.up_near, v.r1, v.r2)).astype(BF16)
+    dots = [v.k_two[0][:, :count], v.d_near] + dots
+    prob_grad = sum(
+        jnp.where(ids == (place ^ k), d.reshape(-1, 1), 0.0) for k, d in enumerate(dots)
+    )
     return (
         upstream[None],
         prob_grad[None],

time: 122 us -> 121 us (level)
  waiting for transfers between devices: 39.6 us -> 37.3 us
  starting transfers between devices: 42.8 us -> 44.1 us
    ppermute x27, waiting for transfers between devices: 39.6 us -> 37.3 us  [over(): return lax.ppermute(x, axis, pairs)]
    ppermute x27, starting transfers between devices: 42.8 us -> 44.1 us  [over(): return lax.ppermute(x, axis, pairs)]
  transfers between devices with their start and end apart: 27 -> 27, of which waited for: 9 -> 9; matrix products, arithmetic and copies ran while one was open for 25% -> 26% of each run, Pallas kernels for 3% -> 3%
where the time goes in v6:
time: 121 us; the launch traced here: 120 us
  starting transfers between devices  44.1 us (36%)
  waiting for transfers between devices  37.3 us (31%)
  matrix products  19.6 us (16%)
  other arithmetic  9.83 us (8%)
  local copies, waits for them, and re-layouts  5.1 us (4%)
  Pallas kernels  3.19 us (3%)
    ppermute x27, starting transfers between devices, over(): return lax.ppermute(x, axis, pairs)  44.1 us
    ppermute x27, waiting for transfers between devices, over(): return lax.ppermute(x, axis, pairs)  37.3 us
    dot_general x17, matrix products, mm(): return lax.dot_general(a, b, (dims, ((), ())), preferred_element_type=F32)  19.6 us
    unnamed x11, local copies, waits for them, and re-layouts  3.91 us
    pallas_call x2, Pallas kernels, gather(): pl.pallas_call(functools.partial(gather_kernel, [piece[1:] for piece in p...  3.19 us
  transfers between devices with their start and end apart: 27, of which 9 were waited for; matrix products, arithmetic and copies ran while one was open for 26% of the time, Pallas kernels for 3%

profile of v6, /device:TPU:0, one launch (start us, length us, event | category | flops | bytes accessed | tf_op | source)
XLA Modules:
  0.0 120.3 jit_solution(4735796719026228546)
XLA Ops:
  0.6 1.5 %collective-permute-start.3 = (bf16[128,2048]{1,0:T(8,128)(2,1)}, bf16[128,2048]{1,0:T(8,128)(2,1)}, u32[]{:S(2)}, u32[]{:S(2)}) collective-permute-start(bf16[128,2048]{1,0:T(8,128)(2,1)} %bitcast.54), channel_id=1, source_target_pairs={{1,2},{2,1},{5,6},{6,5},{9,10},{10,9},{13,14},{14,13},{17,18},{18,... | collective-permute-start | bytes 1572872 | tf_op jit(solution)/shard_map/t_mid_in/ppermute | solution.py:201
  2.1 5.1 %collective-permute-start.4 = (bf16[128,2048]{1,0:T(8,128)(2,1)}, bf16[128,2048]{1,0:T(8,128)(2,1)}, u32[]{:S(2)}, u32[]{:S(2)}) collective-permute-start(bf16[128,2048]{1,0:T(8,128)(2,1)} %bitcast.55), channel_id=1, source_target_pairs={{0,1},{3,2},{1,0},{2,3},{4,5},{7,6},{5,4},{6,7},{8,9},{11,10},{9,8... | collective-permute-start | bytes 1572872 | tf_op jit(solution)/shard_map/t_near/ppermute | solution.py:201
  8.5 1.9 %collective-permute-start.1 = (f32[1,128]{1,0:T(1,128)S(1)}, f32[1,128]{1,0:T(1,128)S(1)}, u32[]{:S(2)}, u32[]{:S(2)}) collective-permute-start(f32[1,128]{1,0:T(1,128)S(1)} %bitcast.80), channel_id=1, source_target_pairs={{0,3},{1,2},{2,1},{3,0},{4,7},{5,6},{6,5},{7,4},{8,11},{9,10},{10,... | collective-permute-start | bytes 1544 | tf_op jit(solution)/shard_map/p/ppermute | solution.py:201
  10.4 1.1 collective-permute-start.2
  11.5 1.4 %copy-done = bf16[1,1,2048,384]{3,2,1,0:T(8,128)(2,1)S(1)} copy-done((bf16[1,1,2048,384]{3,2,1,0:T(8,128)(2,1)S(1)}, bf16[1,1,2048,384]{3,2,1,0:T(8,128)(2,1)}, u32[]{:S(2)}) %copy-start) | copy-done | bytes 1572888
  12.9 1.4 %copy-done.1 = bf16[1,1,2048,384]{3,2,1,0:T(8,128)(2,1)S(1)} copy-done((bf16[1,1,2048,384]{3,2,1,0:T(8,128)(2,1)S(1)}, bf16[1,1,2048,384]{3,2,1,0:T(8,128)(2,1)}, u32[]{:S(2)}) %copy-start.1) | copy-done | bytes 1572888
  14.6 4.2 %collective-permute-done = f32[1,128]{1,0:T(1,128)S(1)} collective-permute-done((f32[1,128]{1,0:T(1,128)S(1)}, f32[1,128]{1,0:T(1,128)S(1)}, u32[]{:S(2)}, u32[]{:S(2)}) %collective-permute-start) | collective-permute-done | bytes 544 | tf_op jit(solution)/shard_map/p/ppermute | solution.py:201
  18.9 1.3 %collective-permute-done.1 = f32[1,128]{1,0:T(1,128)S(1)} collective-permute-done((f32[1,128]{1,0:T(1,128)S(1)}, f32[1,128]{1,0:T(1,128)S(1)}, u32[]{:S(2)}, u32[]{:S(2)}) %collective-permute-start.1) | collective-permute-done | bytes 544 | tf_op jit(solution)/shard_map/p/ppermute | solution.py:201
  22.1 1.3 %collective-permute-start.11 = (bf16[128,2048]{1,0:T(8,128)(2,1)}, bf16[128,2048]{1,0:T(8,128)(2,1)S(1)}, u32[]{:S(2)}, u32[]{:S(2)}) collective-permute-start(bf16[128,2048]{1,0:T(8,128)(2,1)} %collective-permute-done.3), channel_id=1, source_target_pairs={{1,0},{2,3},{5,4},{6,7},{9,8},{10,11},{13,12},{14,15},{17,16},{18,... | collective-permute-start | bytes 1572872 | tf_op jit(solution)/shard_map/t_mid_out/ppermute | solution.py:201
  23.4 1.1 constant_dynamic-update-slice_fusion.1
  24.5 1.1 constant_dynamic-update-slice_fusion
  25.6 1.0 fusion.47
  26.6 9.1 %collective-permute-done.5 = bf16[128,2048]{1,0:T(8,128)(2,1)S(1)} collective-permute-done((bf16[128,2048]{1,0:T(8,128)(2,1)}, bf16[128,2048]{1,0:T(8,128)(2,1)S(1)}, u32[]{:S(2)}, u32[]{:S(2)}) %collective-permute-start.5) | collective-permute-done | bytes 524320 | tf_op jit(solution)/shard_map/g_near/ppermute | solution.py:201
  36.4 1.3 %collective-permute-start.12 = (bf16[128,2048]{1,0:T(8,128)(2,1)S(1)}, bf16[128,2048]{1,0:T(8,128)(2,1)S(1)}, u32[]{:S(2)}, u32[]{:S(2)}) collective-permute-start(bf16[128,2048]{1,0:T(8,128)(2,1)S(1)} %collective-permute-done.8), channel_id=1, source_target_pairs={{1,0},{2,3},{5,4},{6,7},{9,8},{10,11},{13,12},{14,15},{17,16},{18,... | collective-permute-start | bytes 1572872 | tf_op jit(solution)/shard_map/t_far_out/ppermute | solution.py:201
  37.7 2.9 %sib_w.1 = (bf16[2048,768]{1,0:T(8,128)(2,1)S(1)}, bf16[768,2048]{1,0:T(8,128)(2,1)S(1)}) custom-call(bf16[2048,768]{1,0:T(8,128)(2,1)} %collective-permute-done.7.refs_0_, bf16[384,2048]{1,0:T(8,128)(2,1)} %bitcast.6.refs_1_, bf16[384,2048]{1,0:T(8,128)(2,1)} %collective-permute-done.6.refs_2_), custom_call_target="tpu_custom_call" | custom-call | bytes 1048576 | tf_op jit(solution)/shard_map/sib_w/pallas_call | solution.py:179
  40.6 1.0 fusion.48
  41.8 1.0 fusion.3
  43.4 1.0 fusion.45
  44.4 1.1 fusion
  45.6 2.7 %collective-permute-start.9 = (f32[1,128]{1,0:T(1,128)S(1)}, f32[1,128]{1,0:T(1,128)S(1)}, u32[]{:S(2)}, u32[]{:S(2)}) collective-permute-start(f32[1,128]{1,0:T(1,128)S(1)} %slice.101), channel_id=1, source_target_pairs={{0,1},{1,0},{2,3},{3,2},{4,5},{5,4},{6,7},{7,6},{8,9},{9,8},{10,11... | collective-permute-start | bytes 1544 | tf_op jit(solution)/shard_map/dot/ppermute | solution.py:201
  49.0 1.3 %collective-permute-start.14 = (bf16[128,2048]{1,0:T(8,128)(2,1)S(1)}, bf16[128,2048]{1,0:T(8,128)(2,1)S(1)}, u32[]{:S(2)}, u32[]{:S(2)}) collective-permute-start(bf16[128,2048]{1,0:T(8,128)(2,1)S(1)} %collective-permute-done.10), channel_id=1, source_target_pairs={{1,0},{2,3},{5,4},{6,7},{9,8},{10,11},{13,12},{14,15},{17,16},{18,... | collective-permute-start | bytes 1572872 | tf_op jit(solution)/shard_map/g_far_out/ppermute | solution.py:201
  50.4 8.7 %collective-permute-start.17 = (bf16[128,2048]{1,0:T(8,128)(2,1)S(1)}, bf16[128,2048]{1,0:T(8,128)(2,1)S(1)}, u32[]{:S(2)}, u32[]{:S(2)}) collective-permute-start(bf16[128,2048]{1,0:T(8,128)(2,1)S(1)} %get-tuple-element.904), channel_id=1, source_target_pairs={{0,25},{3,26},{8,1},{11,2},{16,9},{19,10},{24,17},{27,18},{4,29},{... | collective-permute-start | bytes 1572872 | tf_op jit(solution)/shard_map/up/ppermute | solution.py:201
  59.1 1.5 %collective-permute-start.18 = (bf16[128,2048]{1,0:T(8,128)(2,1)S(1)}, bf16[128,2048]{1,0:T(8,128)(2,1)S(1)}, u32[]{:S(2)}, u32[]{:S(2)}) collective-permute-start(bf16[128,2048]{1,0:T(8,128)(2,1)S(1)} %get-tuple-element.903), channel_id=1, source_target_pairs={{0,24},{8,0},{16,8},{24,16},{1,25},{9,1},{17,9},{25,17},{2,26},{10... | collective-permute-start | bytes 1572872 | tf_op jit(solution)/shard_map/up/ppermute | solution.py:201
  60.8 1.0 fusion.18
  61.8 1.0 fusion.17
  62.9 1.5 %collective-permute-start.15 = (bf16[128,2048]{1,0:T(8,128)(2,1)S(1)}, bf16[128,2048]{1,0:T(8,128)(2,1)S(1)}, u32[]{:S(2)}, u32[]{:S(2)}) collective-permute-start(bf16[128,2048]{1,0:T(8,128)(2,1)S(1)} %collective-permute-done.13), channel_id=1, source_target_pairs={{1,0},{2,3},{5,4},{6,7},{9,8},{10,11},{13,12},{14,15},{17,16},{18,... | collective-permute-start | bytes 1572872 | tf_op jit(solution)/shard_map/g_mid_out/ppermute | solution.py:201
  64.3 1.3 %pad_maximum_fusion = bf16[2048,512]{0,1:T(8,128)(2,1)S(1)} fusion(bf16[2048,128]{0,1:T(8,128)(2,1)S(1)} %bitcast.58, bf16[2048,128]{0,1:T(8,128)(2,1)S(1)} %bitcast.59, bf16[2048,128]{0,1:T(8,128)(2,1)} %bitcast.12, bf16[2048,128]{0,1:T(8,128)(2,1)S(1)} %bitcast.57), kind=kLoop, calls=%fused_computation.10 | loop fusion | flops 8388608 | bytes 4194304 | tf_op jit(solution)/shard_map/concatenate | solution.py:311
  65.6 3.8 %collective-permute-done.14 = bf16[128,2048]{1,0:T(8,128)(2,1)S(1)} collective-permute-done((bf16[128,2048]{1,0:T(8,128)(2,1)S(1)}, bf16[128,2048]{1,0:T(8,128)(2,1)S(1)}, u32[]{:S(2)}, u32[]{:S(2)}) %collective-permute-start.14) | collective-permute-done | bytes 524320 | tf_op jit(solution)/shard_map/g_far_out/ppermute | solution.py:201
  70.9 1.2 fusion.44
  72.1 1.2 %fusion.1 = bf16[128,2048]{1,0:T(8,128)(2,1)S(1)} fusion(f32[128,2048]{1,0:T(8,128)S(1)} %fusion.44, bf16[2048,768]{1,0:T(8,128)(2,1)S(1)} %own_w.1, bf16[384,128]{1,0:T(8,128)(2,1)S(1)} %get-tuple-element.901, bf16[384,128]{1,0:T(8,128)(2,1)S(1)} %get-tuple-element.902), kind=kOutput, calls=%fused_computation.8 | convolution fusion | flops 403570688 | bytes 4915200 | tf_op jit(solution)/shard_map/behind/dot_general | solution.py:204
  73.3 1.5 %collective-permute-start.16 = (bf16[128,2048]{1,0:T(8,128)(2,1)S(1)}, bf16[128,2048]{1,0:T(8,128)(2,1)S(1)}, u32[]{:S(2)}, u32[]{:S(2)}) collective-permute-start(bf16[128,2048]{1,0:T(8,128)(2,1)S(1)} %fusion.1), channel_id=1, source_target_pairs={{0,1},{3,2},{4,5},{7,6},{8,9},{11,10},{12,13},{15,14},{16,17},{19,... | collective-permute-start | bytes 1572872 | tf_op jit(solution)/shard_map/r5/ppermute | solution.py:201
  74.8 5.0 %collective-permute-done.15 = bf16[128,2048]{1,0:T(8,128)(2,1)S(1)} collective-permute-done((bf16[128,2048]{1,0:T(8,128)(2,1)S(1)}, bf16[128,2048]{1,0:T(8,128)(2,1)S(1)}, u32[]{:S(2)}, u32[]{:S(2)}) %collective-permute-start.15) | collective-permute-done | bytes 524320 | tf_op jit(solution)/shard_map/g_mid_out/ppermute | solution.py:201
  81.2 1.2 fusion.43
  82.4 1.2 fusion.2
  83.6 1.5 %collective-permute-start.19 = (bf16[128,2048]{1,0:T(8,128)(2,1)S(1)}, bf16[128,2048]{1,0:T(8,128)(2,1)S(1)}, u32[]{:S(2)}, u32[]{:S(2)}) collective-permute-start(bf16[128,2048]{1,0:T(8,128)(2,1)S(1)} %fusion.2), channel_id=1, source_target_pairs={{0,1},{3,2},{4,5},{7,6},{8,9},{11,10},{12,13},{15,14},{16,17},{19,... | collective-permute-start | bytes 1572872 | tf_op jit(solution)/shard_map/r4/ppermute | solution.py:201
  86.2 1.0 convolution_convert_fusion.3
  87.2 1.9 %convolution_convert_fusion.1 = bf16[2048,768]{1,0:T(8,128)(2,1)S(1)} fusion(bf16[2048,512]{0,1:T(8,128)(2,1)S(1)} %pad_maximum_fusion, bf16[768,128]{1,0:T(8,128)(2,1)S(1)} %pad_maximum_fusion.7, bf16[768,128]{1,0:T(8,128)(2,1)S(1)} %pad_maximum_fusion.9, bf16[768,256]{1,0:T(8,128)(2,1)S(1)} %get-tuple-element.781), kind=kOutput, calls=%fused_computation.1 | convolution fusion | flops 1614544896 | bytes 6029312 | tf_op jit(solution)/shard_map/weight_grads/dot_general | solution.py:204
  90.1 1.9 %convolution_convert_fusion = bf16[2048,768]{1,0:T(8,128)(2,1)S(1)} fusion(bf16[2048,512]{0,1:T(8,128)(2,1)S(1)} %pad_maximum_fusion, bf16[768,128]{1,0:T(8,128)(2,1)S(1)} %pad_maximum_fusion.8, bf16[768,128]{1,0:T(8,128)(2,1)S(1)} %pad_maximum_fusion.10, bf16[768,256]{1,0:T(8,128)(2,1)S(1)} %get-tuple-element.783), kind=kOutput, calls=%fused_computation | convolution fusion | flops 1614544896 | bytes 6029312 | tf_op jit(solution)/shard_map/weight_grads/dot_general | solution.py:204
  92.0 3.8 %collective-permute-done.19 = bf16[128,2048]{1,0:T(8,128)(2,1)S(1)} collective-permute-done((bf16[128,2048]{1,0:T(8,128)(2,1)S(1)}, bf16[128,2048]{1,0:T(8,128)(2,1)S(1)}, u32[]{:S(2)}, u32[]{:S(2)}) %collective-permute-start.19) | collective-permute-done | bytes 524320 | tf_op jit(solution)/shard_map/r4/ppermute | solution.py:201
  96.6 1.3 %collective-permute-start.23 = (bf16[128,2048]{1,0:T(8,128)(2,1)S(1)}, bf16[128,2048]{1,0:T(8,128)(2,1)S(1)}, u32[]{:S(2)}, u32[]{:S(2)}) collective-permute-start(bf16[128,2048]{1,0:T(8,128)(2,1)S(1)} %slice_add_fusion.2), channel_id=1, source_target_pairs={{1,24},{2,27},{9,0},{10,3},{17,8},{18,11},{25,16},{26,19},{5,28},{... | collective-permute-start | bytes 1572872 | tf_op jit(solution)/shard_map/r1/ppermute | solution.py:201
  98.6 5.4 %collective-permute-done.21 = bf16[384,2048]{1,0:T(8,128)(2,1)S(1)} collective-permute-done((bf16[384,2048]{1,0:T(8,128)(2,1)S(1)}, bf16[384,2048]{1,0:T(8,128)(2,1)S(1)}, u32[]{:S(2)}, u32[]{:S(2)}) %collective-permute-start.21) | collective-permute-done | bytes 1572896 | tf_op jit(solution)/shard_map/got_dn/ppermute | solution.py:201
  104.0 1.7 %add.151 = bf16[384,2048]{1,0:T(8,128)(2,1)} add(bf16[384,2048]{1,0:T(8,128)(2,1)S(1)} %convolution_convert_fusion.3, bf16[384,2048]{1,0:T(8,128)(2,1)S(1)} %collective-permute-done.21) | non-fusion elementwise | flops 786432 | bytes 4718592 | tf_op jit(solution)/shard_map/add | solution.py:362
  105.7 2.0 %slice_add_fusion = (bf16[2048,384]{1,0:T(8,128)(2,1)}, bf16[2048,384]{1,0:T(8,128)(2,1)}) fusion(bf16[2048,768]{1,0:T(8,128)(2,1)S(1)} %collective-permute-done.22, bf16[2048,768]{1,0:T(8,128)(2,1)S(1)} %convolution_convert_fusion.1), kind=kLoop, calls=%fused_computation.12 | loop fusion | flops 1572864 | bytes 9437184 | tf_op jit(solution)/shard_map/add | solution.py:364
  107.7 2.5 %collective-permute-start.26 = (f32[1,128]{1,0:T(1,128)S(1)}, f32[1,128]{1,0:T(1,128)S(1)}, u32[]{:S(2)}, u32[]{:S(2)}) collective-permute-start(f32[1,128]{1,0:T(1,128)S(1)} %add_bitcast_fusion.1), channel_id=1, source_target_pairs={{0,3},{1,2},{2,1},{3,0},{4,7},{5,6},{6,5},{7,4},{8,11},{9,10},{10,... | collective-permute-start | bytes 1544 | tf_op jit(solution)/shard_map/dot/ppermute | solution.py:201
  110.2 3.6 %collective-permute-start.25 = (f32[1,128]{1,0:T(1,128)S(1)}, f32[1,128]{1,0:T(1,128)S(1)}, u32[]{:S(2)}, u32[]{:S(2)}) collective-permute-start(f32[1,128]{1,0:T(1,128)S(1)} %add_bitcast_fusion), channel_id=1, source_target_pairs={{0,2},{1,3},{2,0},{3,1},{4,6},{5,7},{6,4},{7,5},{8,10},{9,11},{10,... | collective-permute-start | bytes 1544 | tf_op jit(solution)/shard_map/dot/ppermute | solution.py:201
  113.8 1.8 %collective-permute-done.23 = bf16[128,2048]{1,0:T(8,128)(2,1)S(1)} collective-permute-done((bf16[128,2048]{1,0:T(8,128)(2,1)S(1)}, bf16[128,2048]{1,0:T(8,128)(2,1)S(1)}, u32[]{:S(2)}, u32[]{:S(2)}) %collective-permute-start.23) | collective-permute-done | bytes 524320 | tf_op jit(solution)/shard_map/r1/ppermute | solution.py:201
  115.6 1.2 fusion.19
  116.8 2.9 %collective-permute-done.25 = f32[1,128]{1,0:T(1,128)S(1)} collective-permute-done((f32[1,128]{1,0:T(1,128)S(1)}, f32[1,128]{1,0:T(1,128)S(1)}, u32[]{:S(2)}, u32[]{:S(2)}) %collective-permute-start.25) | collective-permute-done | bytes 544 | tf_op jit(solution)/shard_map/dot/ppermute | solution.py:201
  (69 shorter events, 12.9 us)
Async XLA Ops:
  0.6 19.5 %collective-permute-start.3 = (bf16[128,2048]{1,0:T(8,128)(2,1)}, bf16[128,2048]{1,0:T(8,128)(2,1)}, u32[]{:S(2)}, u32[]{:S(2)}) collective-permute-start(bf16[128,2048]{1,0:T(8,128)(2,1)} %bitcast.54), channel_id=1, source_target_pairs={{1,2},{2,1},{5,6},{6,5},{9,10},{10,9},{13,14},{14,13},{17,18},{18,... | collective-permute-start | bytes 1572872 | tf_op jit(solution)/shard_map/t_mid_in/ppermute | solution.py:201
  2.1 18.0 %collective-permute-start.4 = (bf16[128,2048]{1,0:T(8,128)(2,1)}, bf16[128,2048]{1,0:T(8,128)(2,1)}, u32[]{:S(2)}, u32[]{:S(2)}) collective-permute-start(bf16[128,2048]{1,0:T(8,128)(2,1)} %bitcast.55), channel_id=1, source_target_pairs={{0,1},{3,2},{1,0},{2,3},{4,5},{7,6},{5,4},{6,7},{8,9},{11,10},{9,8... | collective-permute-start | bytes 1572872 | tf_op jit(solution)/shard_map/t_near/ppermute | solution.py:201
  7.9 10.9 %collective-permute-start = (f32[1,128]{1,0:T(1,128)S(1)}, f32[1,128]{1,0:T(1,128)S(1)}, u32[]{:S(2)}, u32[]{:S(2)}) collective-permute-start(f32[1,128]{1,0:T(1,128)S(1)} %bitcast.81), channel_id=1, source_target_pairs={{0,2},{1,3},{2,0},{3,1},{4,6},{5,7},{6,4},{7,5},{8,10},{9,11},{10,... | collective-permute-start | bytes 1544 | tf_op jit(solution)/shard_map/p/ppermute | solution.py:201
  8.5 11.6 %collective-permute-start.1 = (f32[1,128]{1,0:T(1,128)S(1)}, f32[1,128]{1,0:T(1,128)S(1)}, u32[]{:S(2)}, u32[]{:S(2)}) collective-permute-start(f32[1,128]{1,0:T(1,128)S(1)} %bitcast.80), channel_id=1, source_target_pairs={{0,3},{1,2},{2,1},{3,0},{4,7},{5,6},{6,5},{7,4},{8,11},{9,10},{10,... | collective-permute-start | bytes 1544 | tf_op jit(solution)/shard_map/p/ppermute | solution.py:201
  10.4 9.8 %collective-permute-start.2 = (f32[1,128]{1,0:T(1,128)S(1)}, f32[1,128]{1,0:T(1,128)S(1)}, u32[]{:S(2)}, u32[]{:S(2)}) collective-permute-start(f32[1,128]{1,0:T(1,128)S(1)} %bitcast.79), channel_id=1, source_target_pairs={{0,1},{1,0},{2,3},{3,2},{4,5},{5,4},{6,7},{7,6},{8,9},{9,8},{10,11... | collective-permute-start | bytes 1544 | tf_op jit(solution)/shard_map/p/ppermute | solution.py:201
  11.5 1.4 %copy-start = (bf16[1,1,2048,384]{3,2,1,0:T(8,128)(2,1)S(1)}, bf16[1,1,2048,384]{3,2,1,0:T(8,128)(2,1)}, u32[]{:S(2)}) copy-start(bf16[1,1,2048,384]{3,2,1,0:T(8,128)(2,1)} %param.11) | copy-start | bytes 4718596
  12.9 1.4 %copy-start.1 = (bf16[1,1,2048,384]{3,2,1,0:T(8,128)(2,1)S(1)}, bf16[1,1,2048,384]{3,2,1,0:T(8,128)(2,1)}, u32[]{:S(2)}) copy-start(bf16[1,1,2048,384]{3,2,1,0:T(8,128)(2,1)} %param.12) | copy-start | bytes 4718596
  20.1 16.3 %collective-permute-start.7 = (bf16[2048,768]{1,0:T(8,128)(2,1)S(1)}, bf16[2048,768]{1,0:T(8,128)(2,1)}, u32[]{:S(2)}, u32[]{:S(2)}) collective-permute-start(bf16[2048,768]{1,0:T(8,128)(2,1)S(1)} %own_w.1), channel_id=1, source_target_pairs={{0,4},{4,0},{1,5},{5,1},{2,6},{6,2},{3,7},{7,3},{8,12},{12,8},{9,1... | collective-permute-start | bytes 9437192 | tf_op jit(solution)/shard_map/sib_w/ppermute | solution.py:201
  20.2 16.2 %collective-permute-start.6 = (bf16[384,2048]{1,0:T(8,128)(2,1)}, bf16[384,2048]{1,0:T(8,128)(2,1)}, u32[]{:S(2)}, u32[]{:S(2)}) collective-permute-start(bf16[384,2048]{1,0:T(8,128)(2,1)} %bitcast.6.refs_1_), channel_id=1, source_target_pairs={{0,4},{4,0},{1,5},{5,1},{2,6},{6,2},{3,7},{7,3},{8,12},{12,8},{9,1... | collective-permute-start | bytes 4718600 | tf_op jit(solution)/shard_map/sib_d/ppermute | solution.py:201
  20.7 15.0 %collective-permute-start.5 = (bf16[128,2048]{1,0:T(8,128)(2,1)}, bf16[128,2048]{1,0:T(8,128)(2,1)S(1)}, u32[]{:S(2)}, u32[]{:S(2)}) collective-permute-start(bf16[128,2048]{1,0:T(8,128)(2,1)} %bitcast.63), channel_id=1, source_target_pairs={{0,1},{3,2},{1,0},{2,3},{4,5},{7,6},{5,4},{6,7},{8,9},{11,10},{9,8... | collective-permute-start | bytes 1572872 | tf_op jit(solution)/shard_map/g_near/ppermute | solution.py:201
  21.5 15.0 %collective-permute-start.8 = (bf16[128,2048]{1,0:T(8,128)(2,1)}, bf16[128,2048]{1,0:T(8,128)(2,1)S(1)}, u32[]{:S(2)}, u32[]{:S(2)}) collective-permute-start(bf16[128,2048]{1,0:T(8,128)(2,1)} %collective-permute-done.4), channel_id=1, source_target_pairs={{1,2},{2,1},{5,6},{6,5},{9,10},{10,9},{13,14},{14,13},{17,18},{18,... | collective-permute-start | bytes 1572872 | tf_op jit(solution)/shard_map/t_far_in/ppermute | solution.py:201
  22.1 26.2 %collective-permute-start.11 = (bf16[128,2048]{1,0:T(8,128)(2,1)}, bf16[128,2048]{1,0:T(8,128)(2,1)S(1)}, u32[]{:S(2)}, u32[]{:S(2)}) collective-permute-start(bf16[128,2048]{1,0:T(8,128)(2,1)} %collective-permute-done.3), channel_id=1, source_target_pairs={{1,0},{2,3},{5,4},{6,7},{9,8},{10,11},{13,12},{14,15},{17,16},{18,... | collective-permute-start | bytes 1572872 | tf_op jit(solution)/shard_map/t_mid_out/ppermute | solution.py:201
  35.7 12.6 %collective-permute-start.10 = (bf16[128,2048]{1,0:T(8,128)(2,1)S(1)}, bf16[128,2048]{1,0:T(8,128)(2,1)S(1)}, u32[]{:S(2)}, u32[]{:S(2)}) collective-permute-start(bf16[128,2048]{1,0:T(8,128)(2,1)S(1)} %collective-permute-done.5), channel_id=1, source_target_pairs={{1,2},{2,1},{5,6},{6,5},{9,10},{10,9},{13,14},{14,13},{17,18},{18,... | collective-permute-start | bytes 1572872 | tf_op jit(solution)/shard_map/g_far_in/ppermute | solution.py:201
  36.4 22.7 %collective-permute-start.12 = (bf16[128,2048]{1,0:T(8,128)(2,1)S(1)}, bf16[128,2048]{1,0:T(8,128)(2,1)S(1)}, u32[]{:S(2)}, u32[]{:S(2)}) collective-permute-start(bf16[128,2048]{1,0:T(8,128)(2,1)S(1)} %collective-permute-done.8), channel_id=1, source_target_pairs={{1,0},{2,3},{5,4},{6,7},{9,8},{10,11},{13,12},{14,15},{17,16},{18,... | collective-permute-start | bytes 1572872 | tf_op jit(solution)/shard_map/t_far_out/ppermute | solution.py:201
  40.6 1.2 %copy-start.3 = (bf16[1,128,2048]{2,1,0:T(8,128)(2,1)S(1)}, bf16[1,128,2048]{2,1,0:T(8,128)(2,1)}, u32[]{:S(2)}) copy-start(bf16[1,128,2048]{2,1,0:T(8,128)(2,1)} %param.8) | copy-start | bytes 1572868
  45.6 39.5 %collective-permute-start.9 = (f32[1,128]{1,0:T(1,128)S(1)}, f32[1,128]{1,0:T(1,128)S(1)}, u32[]{:S(2)}, u32[]{:S(2)}) collective-permute-start(f32[1,128]{1,0:T(1,128)S(1)} %slice.101), channel_id=1, source_target_pairs={{0,1},{1,0},{2,3},{3,2},{4,5},{5,4},{6,7},{7,6},{8,9},{9,8},{10,11... | collective-permute-start | bytes 1544 | tf_op jit(solution)/shard_map/dot/ppermute | solution.py:201
  48.3 14.5 %collective-permute-start.13 = (bf16[128,2048]{1,0:T(8,128)(2,1)S(1)}, bf16[128,2048]{1,0:T(8,128)(2,1)S(1)}, u32[]{:S(2)}, u32[]{:S(2)}) collective-permute-start(bf16[128,2048]{1,0:T(8,128)(2,1)S(1)} %bitcast.65), channel_id=1, source_target_pairs={{1,2},{2,1},{5,6},{6,5},{9,10},{10,9},{13,14},{14,13},{17,18},{18,... | collective-permute-start | bytes 1572872 | tf_op jit(solution)/shard_map/g_mid_in/ppermute | solution.py:201
  49.0 20.4 %collective-permute-start.14 = (bf16[128,2048]{1,0:T(8,128)(2,1)S(1)}, bf16[128,2048]{1,0:T(8,128)(2,1)S(1)}, u32[]{:S(2)}, u32[]{:S(2)}) collective-permute-start(bf16[128,2048]{1,0:T(8,128)(2,1)S(1)} %collective-permute-done.10), channel_id=1, source_target_pairs={{1,0},{2,3},{5,4},{6,7},{9,8},{10,11},{13,12},{14,15},{17,16},{18,... | collective-permute-start | bytes 1572872 | tf_op jit(solution)/shard_map/g_far_out/ppermute | solution.py:201
  50.4 34.7 %collective-permute-start.17 = (bf16[128,2048]{1,0:T(8,128)(2,1)S(1)}, bf16[128,2048]{1,0:T(8,128)(2,1)S(1)}, u32[]{:S(2)}, u32[]{:S(2)}) collective-permute-start(bf16[128,2048]{1,0:T(8,128)(2,1)S(1)} %get-tuple-element.904), channel_id=1, source_target_pairs={{0,25},{3,26},{8,1},{11,2},{16,9},{19,10},{24,17},{27,18},{4,29},{... | collective-permute-start | bytes 1572872 | tf_op jit(solution)/shard_map/up/ppermute | solution.py:201
  59.1 26.0 %collective-permute-start.18 = (bf16[128,2048]{1,0:T(8,128)(2,1)S(1)}, bf16[128,2048]{1,0:T(8,128)(2,1)S(1)}, u32[]{:S(2)}, u32[]{:S(2)}) collective-permute-start(bf16[128,2048]{1,0:T(8,128)(2,1)S(1)} %get-tuple-element.903), channel_id=1, source_target_pairs={{0,24},{8,0},{16,8},{24,16},{1,25},{9,1},{17,9},{25,17},{2,26},{10... | collective-permute-start | bytes 1572872 | tf_op jit(solution)/shard_map/up/ppermute | solution.py:201
  61.8 2.5 %copy-start.2 = (bf16[1,128,2048]{2,1,0:T(8,128)(2,1)S(1)}, bf16[1,128,2048]{2,1,0:T(8,128)(2,1)}, u32[]{:S(2)}) copy-start(bf16[1,128,2048]{2,1,0:T(8,128)(2,1)} %param.7) | copy-start | bytes 1572868
  62.9 16.9 %collective-permute-start.15 = (bf16[128,2048]{1,0:T(8,128)(2,1)S(1)}, bf16[128,2048]{1,0:T(8,128)(2,1)S(1)}, u32[]{:S(2)}, u32[]{:S(2)}) collective-permute-start(bf16[128,2048]{1,0:T(8,128)(2,1)S(1)} %collective-permute-done.13), channel_id=1, source_target_pairs={{1,0},{2,3},{5,4},{6,7},{9,8},{10,11},{13,12},{14,15},{17,16},{18,... | collective-permute-start | bytes 1572872 | tf_op jit(solution)/shard_map/g_mid_out/ppermute | solution.py:201
  73.3 11.9 %collective-permute-start.16 = (bf16[128,2048]{1,0:T(8,128)(2,1)S(1)}, bf16[128,2048]{1,0:T(8,128)(2,1)S(1)}, u32[]{:S(2)}, u32[]{:S(2)}) collective-permute-start(bf16[128,2048]{1,0:T(8,128)(2,1)S(1)} %fusion.1), channel_id=1, source_target_pairs={{0,1},{3,2},{4,5},{7,6},{8,9},{11,10},{12,13},{15,14},{16,17},{19,... | collective-permute-start | bytes 1572872 | tf_op jit(solution)/shard_map/r5/ppermute | solution.py:201
  83.6 12.2 %collective-permute-start.19 = (bf16[128,2048]{1,0:T(8,128)(2,1)S(1)}, bf16[128,2048]{1,0:T(8,128)(2,1)S(1)}, u32[]{:S(2)}, u32[]{:S(2)}) collective-permute-start(bf16[128,2048]{1,0:T(8,128)(2,1)S(1)} %fusion.2), channel_id=1, source_target_pairs={{0,1},{3,2},{4,5},{7,6},{8,9},{11,10},{12,13},{15,14},{16,17},{19,... | collective-permute-start | bytes 1572872 | tf_op jit(solution)/shard_map/r4/ppermute | solution.py:201
  85.3 10.5 %collective-permute-start.20 = (bf16[128,2048]{1,0:T(8,128)(2,1)S(1)}, bf16[128,2048]{1,0:T(8,128)(2,1)S(1)}, u32[]{:S(2)}, u32[]{:S(2)}) collective-permute-start(bf16[128,2048]{1,0:T(8,128)(2,1)S(1)} %add.147), channel_id=1, source_target_pairs={{1,2},{2,1},{5,6},{6,5},{9,10},{10,9},{13,14},{14,13},{17,18},{18,... | collective-permute-start | bytes 1572872 | tf_op jit(solution)/shard_map/r3/ppermute | solution.py:201
  96.0 8.0 %collective-permute-start.22 = (bf16[2048,768]{1,0:T(8,128)(2,1)S(1)}, bf16[2048,768]{1,0:T(8,128)(2,1)S(1)}, u32[]{:S(2)}, u32[]{:S(2)}) collective-permute-start(bf16[2048,768]{1,0:T(8,128)(2,1)S(1)} %convolution_convert_fusion), channel_id=1, source_target_pairs={{0,4},{4,0},{1,5},{5,1},{2,6},{6,2},{3,7},{7,3},{8,12},{12,8},{9,1... | collective-permute-start | bytes 9437192 | tf_op jit(solution)/shard_map/got_gu/ppermute | solution.py:201
  96.1 7.9 %collective-permute-start.21 = (bf16[384,2048]{1,0:T(8,128)(2,1)S(1)}, bf16[384,2048]{1,0:T(8,128)(2,1)S(1)}, u32[]{:S(2)}, u32[]{:S(2)}) collective-permute-start(bf16[384,2048]{1,0:T(8,128)(2,1)S(1)} %convolution_convert_fusion.2), channel_id=1, source_target_pairs={{0,4},{4,0},{1,5},{5,1},{2,6},{6,2},{3,7},{7,3},{8,12},{12,8},{9,1... | collective-permute-start | bytes 4718600 | tf_op jit(solution)/shard_map/got_dn/ppermute | solution.py:201
  96.6 19.0 %collective-permute-start.23 = (bf16[128,2048]{1,0:T(8,128)(2,1)S(1)}, bf16[128,2048]{1,0:T(8,128)(2,1)S(1)}, u32[]{:S(2)}, u32[]{:S(2)}) collective-permute-start(bf16[128,2048]{1,0:T(8,128)(2,1)S(1)} %slice_add_fusion.2), channel_id=1, source_target_pairs={{1,24},{2,27},{9,0},{10,3},{17,8},{18,11},{25,16},{26,19},{5,28},{... | collective-permute-start | bytes 1572872 | tf_op jit(solution)/shard_map/r1/ppermute | solution.py:201
  97.8 17.8 %collective-permute-start.24 = (bf16[128,2048]{1,0:T(8,128)(2,1)S(1)}, bf16[128,2048]{1,0:T(8,128)(2,1)S(1)}, u32[]{:S(2)}, u32[]{:S(2)}) collective-permute-start(bf16[128,2048]{1,0:T(8,128)(2,1)S(1)} %add.149), channel_id=1, source_target_pairs={{1,26},{2,25},{9,2},{10,1},{17,10},{18,9},{25,18},{26,17},{5,30},{... | collective-permute-start | bytes 1572872 | tf_op jit(solution)/shard_map/r2/ppermute | solution.py:201
  105.7 14.0 %copy-start.4 = (s32[1,128,2]{1,2,0:T(2,128)S(1)}, s32[1,128,2]{1,2,0:T(2,128)}, u32[]{:S(2)}) copy-start(s32[1,128,2]{1,2,0:T(2,128)} %param.9) | copy-start | bytes 3076
  107.7 9.1 %collective-permute-start.26 = (f32[1,128]{1,0:T(1,128)S(1)}, f32[1,128]{1,0:T(1,128)S(1)}, u32[]{:S(2)}, u32[]{:S(2)}) collective-permute-start(f32[1,128]{1,0:T(1,128)S(1)} %add_bitcast_fusion.1), channel_id=1, source_target_pairs={{0,3},{1,2},{2,1},{3,0},{4,7},{5,6},{6,5},{7,4},{8,11},{9,10},{10,... | collective-permute-start | bytes 1544 | tf_op jit(solution)/shard_map/dot/ppermute | solution.py:201
  110.2 9.5 %collective-permute-start.25 = (f32[1,128]{1,0:T(1,128)S(1)}, f32[1,128]{1,0:T(1,128)S(1)}, u32[]{:S(2)}, u32[]{:S(2)}) collective-permute-start(f32[1,128]{1,0:T(1,128)S(1)} %add_bitcast_fusion), channel_id=1, source_target_pairs={{0,2},{1,3},{2,0},{3,1},{4,6},{5,7},{6,4},{7,5},{8,10},{9,11},{10,... | collective-permute-start | bytes 1544 | tf_op jit(solution)/shard_map/dot/ppermute | solution.py:201
